TPU v7x, 32 devices: a whole 2x2x4 slice. The times are simulated.
32 devices in a mesh: brick: 32 (over z, y, x, core).
Axes of the slice: x: 2, y: 2, z: 4, core: 2. Of those that a mesh axis runs over, the one named last changes fastest.
Arguments:
- sensitivity: float32 [32, 65536], P(None, 'brick'), may hold values from -40 to 40
- diagonal: float32 [65536], P('brick'), may hold values from 1 to 16
- displacement: bfloat16 [65536], P('brick'), may hold values from -3 to 3
- connectivity: int32 [4096, 128], P('brick'), may hold values from 0 to 2559
- normal_stiff: float32 [4096], P('brick'), may hold values from 0.5 to 2
- shear_stiff: float32 [4096], P('brick'), may hold values from 0.3 to 1.5
- friction: float32 [4096], P('brick'), may hold values from 0.3 to 0.8
- slip_state: int32 [4096], P('brick'), may hold values 0 or 1
- owner_map: int32 [32, 2, 256], P('brick'), may hold values from 0 to 255, each once within a row
- templates: bfloat16 [3, 128, 128], replicated, may hold values from -0.25 to 0.25
Outputs:
- adjoint: float32 [32, 65536], P(None, 'brick')
- joint_grads: float32 [3, 32, 4096], P(None, None, 'brick')
Inputs may be any that keep to these rules, and one draw needn't show every extreme that they name: connectivity[e, i] names a slot of the extended field of element e's brick. For each brick and side, owner_map is a permutation of 0 .. 255.
All inputs are finite; a program needn't handle non-finite values. No bound on the sum of `slip_state` on one device may be relied on, other than what follows from the above.
Results may differ from a plain program's by a relative error of at most 0.0042.
The roundings to bfloat16 on the way count: a program that leaves them out, or rounds other values in their place, can miss the bound.
Values may be sent and summed in bfloat16 or wider, within the bound.
No kernel may reach another device: no remote copies, remote signals or barrier semaphores. Data moves between devices by JAX's collectives and lax.ppermute only.
A program may use at most 64 MiB of HBM per device.

v0:
```python
import jax
import jax.numpy as jnp
from jax import lax
from jax.sharding import PartitionSpec as P

ITERS = 2


FULL_PRECISION = lax.Precision.HIGHEST


def padded_2(cells, sides, width):
    for axis, dim in sides:
        count = lax.axis_size(axis)
        ends = count - 1
        head = lax.slice_in_dim(cells, 0, width, axis=dim)
        tail = lax.slice_in_dim(cells, cells.shape[dim] - width, cells.shape[dim], axis=dim)
        cells = jnp.concatenate(
            [
                lax.ppermute(tail, axis, [(i, (i + 1) % count) for i in range(ends)]),
                cells,
                lax.ppermute(head, axis, [((i + 1) % count, i) for i in range(ends)]),
            ],
            axis=dim,
        )
    return cells


def shifted(block, axis, distance):
    devices = range(lax.axis_size(axis))
    route = [(i - distance, i) for i in devices if i - distance in devices]
    return lax.ppermute(block, axis, route)


def inner(first, second):
    return jnp.dot(first, second.T, precision=FULL_PRECISION, preferred_element_type=jnp.float32)


def lower_inverse(gram_matrix):
    factor = jnp.linalg.cholesky(gram_matrix)
    identity = jnp.eye(gram_matrix.shape[0], dtype=jnp.float32)
    return (jax.scipy.linalg.solve_triangular(factor, identity, lower=True), factor)


def element_partials(extended, connectivity, stiff_coeffs, templates):
    rows = extended.shape[0]
    width = extended.shape[1]
    elem_count = connectivity.shape[0]
    block_size = min(elem_count, 64)
    blocks = elem_count // block_size
    slot_count = templates.shape[1]
    stacked = templates.reshape(3 * slot_count, slot_count)
    connect_blocks = connectivity.reshape(blocks, block_size, slot_count)
    coeff_blocks = stiff_coeffs.reshape(3, blocks, block_size).transpose(1, 0, 2)

    def one_block(total, inputs):
        block_conn, block_coeff = inputs
        values = extended[:, block_conn]
        scaled = (values[:, :, None, :] * block_coeff.T[None, :, :, None]).astype(jnp.bfloat16)
        result = jnp.dot(
            scaled.reshape(rows * block_size, 3 * slot_count),
            stacked,
            preferred_element_type=jnp.float32,
        )
        total = total.at[:, block_conn].add(result.reshape(rows, block_size, slot_count))
        return (total, None)

    total, unused = lax.scan(
        one_block, jnp.zeros((rows, width), jnp.float32), (connect_blocks, coeff_blocks)
    )
    return total


def ghost_extend(local_rows, owner_map):
    ghost_count = owner_map.shape[2]
    padded = padded_2(local_rows, (("brick", 1),), ghost_count)
    total_width = padded.shape[1]
    lower_band = padded[:, :ghost_count]
    upper_band = padded[:, total_width - ghost_count :]
    middle = padded[:, ghost_count : total_width - ghost_count]
    return jnp.concatenate(
        [lower_band[:, owner_map[0, 0]], middle, upper_band[:, owner_map[0, 1]]], axis=1
    )


def apply_operator(extended, current, diagonal, connectivity, stiff_coeffs, owner_map, templates):
    ghost_count = owner_map.shape[2]
    dof_count = current.shape[1]
    rows = current.shape[0]
    partial_value = element_partials(extended, connectivity, stiff_coeffs, templates)
    empty = jnp.zeros((rows, ghost_count), jnp.float32)
    to_lower = empty.at[:, owner_map[0, 0]].add(partial_value[:, :ghost_count])
    to_upper = empty.at[:, owner_map[0, 1]].add(partial_value[:, ghost_count + dof_count :])
    from_upper = shifted(to_lower.astype(jnp.bfloat16), "brick", -1).astype(to_lower.dtype)
    from_lower = shifted(to_upper.astype(jnp.bfloat16), "brick", 1).astype(to_upper.dtype)
    owned = partial_value[:, ghost_count : ghost_count + dof_count]
    owned = owned.at[:, dof_count - ghost_count :].add(from_upper)
    owned = owned.at[:, :ghost_count].add(from_lower)
    return diagonal[None, :] * current + owned


def project_out(image, projections, basis):
    reduced = image
    for earlier in range(projections.shape[0]):
        reduced = reduced - jnp.dot(
            projections[earlier].T,
            basis[earlier],
            precision=FULL_PRECISION,
            preferred_element_type=jnp.float32,
        )
    return reduced


def least_squares(projections, factors):
    count = factors[0].shape[0]
    iterations = len(projections)
    hessenberg = jnp.zeros(((iterations + 1) * count, iterations * count), jnp.float32)
    for column in range(iterations):
        for block_row in range(column + 1):
            hessenberg = hessenberg.at[
                block_row * count : (block_row + 1) * count, column * count : (column + 1) * count
            ].set(projections[column][block_row])
        hessenberg = hessenberg.at[
            (column + 1) * count : (column + 2) * count, column * count : (column + 1) * count
        ].set(factors[column + 1].T)
    target = jnp.zeros(((iterations + 1) * count, count), jnp.float32).at[:count].set(factors[0].T)
    normal_matrix = jnp.dot(
        hessenberg.T, hessenberg, precision=FULL_PRECISION, preferred_element_type=jnp.float32
    )
    right_side = jnp.dot(
        hessenberg.T, target, precision=FULL_PRECISION, preferred_element_type=jnp.float32
    )
    cholesky_factor = jnp.linalg.cholesky(normal_matrix)
    return jax.scipy.linalg.cho_solve((cholesky_factor, True), right_side)


def combine(weights, fields):
    count = weights.shape[1]
    total = jnp.dot(
        weights[:count].T, fields[0], precision=FULL_PRECISION, preferred_element_type=jnp.float32
    )
    total = total + jnp.dot(
        weights[count : 2 * count].T,
        fields[1],
        precision=FULL_PRECISION,
        preferred_element_type=jnp.float32,
    )
    return total


def on_device(
    sensitivity,
    diagonal,
    displacement,
    connectivity,
    normal_stiff,
    shear_stiff,
    friction,
    slip_state,
    owner_map,
    templates,
):
    slip_real = slip_state.astype(jnp.float32)
    stiff_coeffs = jnp.stack([normal_stiff, shear_stiff, slip_real * friction * normal_stiff])
    start_matrix = lax.psum(inner(sensitivity, sensitivity), "brick")
    inverse, factor = lower_inverse(start_matrix)
    basis = [
        jnp.dot(inverse, sensitivity, precision=FULL_PRECISION, preferred_element_type=jnp.float32)
    ]
    halves = []
    extended_list = []
    projections = []
    factors = [factor]
    displace_ext = None
    for column in range(ITERS):
        current = basis[column]
        half = current.astype(jnp.bfloat16)
        halves.append(half)
        if column == 0:
            joined = ghost_extend(jnp.concatenate([displacement[None, :], half], axis=0), owner_map)
            displace_ext = joined[0]
            extended = joined[1:]
        else:
            extended = ghost_extend(half, owner_map)
        extended_list.append(extended)
        image = apply_operator(
            extended, current, diagonal, connectivity, stiff_coeffs, owner_map, templates
        )
        local_proj = jnp.stack([inner(basis[earlier], image) for earlier in range(column + 1)])
        current_proj = lax.psum(local_proj, "brick")
        reduced = project_out(image, current_proj, basis)
        gram_next = lax.psum(inner(reduced, reduced), "brick")
        inverse, factor = lower_inverse(gram_next)
        if column + 1 < ITERS:
            basis.append(
                jnp.dot(
                    inverse, reduced, precision=FULL_PRECISION, preferred_element_type=jnp.float32
                )
            )
        projections.append(current_proj)
        factors.append(factor)
    weights = least_squares(projections, factors)
    adjoint = combine(weights, basis)
    adjoint_half = combine(weights, halves).astype(jnp.bfloat16)
    adjoint_ext = ghost_extend(adjoint_half, owner_map)
    displace_elem = displace_ext[connectivity]
    pushed = jnp.einsum(
        "ej,kij->eki", displace_elem, templates, preferred_element_type=jnp.float32
    ).astype(jnp.bfloat16)
    adjoint_elem = adjoint_ext[:, connectivity]
    pairs = lax.dot_general(
        adjoint_elem, pushed, (((2,), (2,)), ((1,), (0,))), preferred_element_type=jnp.float32
    )
    pairs = pairs.transpose(2, 1, 0)
    grad_normal = -(pairs[0] + (slip_real * friction)[None, :] * pairs[2])
    grad_shear = -pairs[1]
    grad_friction = -(slip_real * normal_stiff)[None, :] * pairs[2]
    return (adjoint, jnp.stack([grad_normal, grad_shear, grad_friction]))


def solution(mesh):
    in_specs = (
        P(None, "brick"),
        P("brick"),
        P("brick"),
        P("brick", None),
        P("brick"),
        P("brick"),
        P("brick"),
        P("brick"),
        P("brick", None, None),
        P(),
    )
    out_specs = (P(None, "brick"), P(None, None, "brick"))
    return jax.shard_map(
        on_device, mesh=mesh, in_specs=in_specs, out_specs=out_specs, check_vma=False
    )
```

profile of v0, /device:TPU:0, one launch (start us, length us, event | category | flops | bytes accessed | tf_op | source)
XLA Modules:
  0.0 935.7 jit_solution(18208557851984772817)
XLA Ops:
  1.9 42.1 %psum.35 = f32[32,32]{0,1:T(8,128)S(1)} all-reduce(f32[32,32]{0,1:T(8,128)S(1)} %fusion.75), channel_id=1, replica_groups=mesh['brick'=32] {'brick'}, use_global_device_ids=true, to_apply=%region_0.0 | all-reduce | flops 1024 | bytes 8192 | tf_op jit(solution)/shard_map/psum | solution.py:165
  66.5 193.1 %while.30 = (s32[]{:T(128)}, f32[32,2560]{0,1:T(8,128)S(1)}, s32[2,64,128]{2,1,0:T(8,128)}, bf16[32,2560]{0,1:T(8,128)(2,1)S(1)}, f32[2,3,64]{1,2,0:T(8,128)}, /*index=5*/bf16[384,128]{1,0:T(8,128)(2,1)}, s32[]{:T(128)}) while((s32[]{:T(128)}, f32[32,2560]{0,1:T(8,128)S(1)}, s32[2,64,128]{2,1,0:T(8,128)}, bf16[32,2560]{0,1:T(8,128)(2,1)S(1)}, ...), condition=%wide.region_5.8_spmd, body=%wide.region_3.7_spmd.sunk | while | flops 203456512 | bytes 25305456 | solution.py:68
  67.9 29.2 %gather_fusion = bf16[8192,32]{1,0:T(8,128)(2,1)} fusion(bf16[32,2560]{0,1:T(8,128)(2,1)S(1)} %get-tuple-element.393, s32[8192]{0:T(1024)S(1)} %get-tuple-element.367), kind=kCustom, calls=%fused_computation.clone.1 | custom fusion | bytes 1081344 | tf_op jit(solution)/shard_map/while/body/eval_jaxpr/gather | solution.py:58
  106.8 6.1 mul.154
  118.2 44.8 %scatter_fusion = f32[32,2560]{0,1:T(8,128)S(1)} fusion(f32[32,2560]{0,1:T(8,128)S(1)} %get-tuple-element.384, s32[8192]{0:T(1024)} %get-tuple-element.366, f32[8192,32]{1,0:T(8,128)} %bitcast.202), kind=kCustom, calls=%fused_computation.10.clone.1 | custom fusion | flops 262144 | bytes 3178496 | tf_op jit(solution)/shard_map/while/body/eval_jaxpr/scatter-add | solution.py:65
  164.4 29.2 %gather_fusion = bf16[8192,32]{1,0:T(8,128)(2,1)} fusion(bf16[32,2560]{0,1:T(8,128)(2,1)S(1)} %get-tuple-element.393, s32[8192]{0:T(1024)S(1)} %get-tuple-element.367), kind=kCustom, calls=%fused_computation.clone.1 | custom fusion | bytes 1081344 | tf_op jit(solution)/shard_map/while/body/eval_jaxpr/gather | solution.py:58
  203.4 6.1 mul.154
  214.7 44.8 %scatter_fusion = f32[32,2560]{0,1:T(8,128)S(1)} fusion(f32[32,2560]{0,1:T(8,128)S(1)} %get-tuple-element.384, s32[8192]{0:T(1024)} %get-tuple-element.366, f32[8192,32]{1,0:T(8,128)} %bitcast.202), kind=kCustom, calls=%fused_computation.10.clone.1 | custom fusion | flops 262144 | bytes 3178496 | tf_op jit(solution)/shard_map/while/body/eval_jaxpr/scatter-add | solution.py:65
  265.5 6.2 collective-permute-start.3
  273.5 44.8 %psum.36 = f32[32,32]{1,0:T(8,128)S(1)} all-reduce(f32[32,32]{1,0:T(8,128)S(1)} %fusion.13), channel_id=1, replica_groups=mesh['brick'=32] {'brick'}, use_global_device_ids=true, to_apply=%region_9.12 | all-reduce | flops 1024 | bytes 8192 | tf_op jit(solution)/shard_map/psum | solution.py:190
  319.3 39.2 %psum.37 = f32[32,32]{0,1:T(8,128)S(1)} all-reduce(f32[32,32]{0,1:T(8,128)S(1)} %fusion.76), channel_id=1, replica_groups=mesh['brick'=32] {'brick'}, use_global_device_ids=true, to_apply=%region_10.13 | all-reduce | flops 1024 | bytes 8192 | tf_op jit(solution)/shard_map/psum | solution.py:192
  369.8 173.0 %gather_fusion.9 = bf16[16384]{0:T(1024)(128)(2,1)} fusion(bf16[2560]{0:T(1024)(128)(2,1)S(1)} %maximum_reduce_fusion, s32[16384]{0:T(1024)S(1)} %copy-done.10), kind=kCustom, calls=%fused_computation.9 | custom fusion | bytes 131072 | tf_op jit(solution)/shard_map/gather | solution.py:206
  545.4 193.0 %while.31 = (s32[]{:T(128)}, f32[32,2560]{0,1:T(8,128)S(1)}, s32[2,64,128]{2,1,0:T(8,128)}, bf16[32,2560]{0,1:T(8,128)(2,1)S(1)}, f32[2,3,64]{1,2,0:T(8,128)}, /*index=5*/bf16[384,128]{1,0:T(8,128)(2,1)}, s32[]{:T(128)}) while((s32[]{:T(128)}, f32[32,2560]{0,1:T(8,128)S(1)}, s32[2,64,128]{2,1,0:T(8,128)}, bf16[32,2560]{0,1:T(8,128)(2,1)S(1)}, ...), condition=%wide.region_14.17_spmd, body=%wide.region_12.16_spmd.sunk | while | flops 203456512 | bytes 25305456 | solution.py:68
  546.8 29.2 %gather_fusion.1 = bf16[8192,32]{1,0:T(8,128)(2,1)} fusion(bf16[32,2560]{0,1:T(8,128)(2,1)S(1)} %get-tuple-element.414, s32[8192]{0:T(1024)S(1)} %get-tuple-element.375), kind=kCustom, calls=%fused_computation.1.clone.1 | custom fusion | bytes 1081344 | tf_op jit(solution)/shard_map/while/body/eval_jaxpr/gather | solution.py:58
  585.8 6.1 mul.159
  597.1 44.8 %scatter_fusion.1 = f32[32,2560]{0,1:T(8,128)S(1)} fusion(f32[32,2560]{0,1:T(8,128)S(1)} %get-tuple-element.405, s32[8192]{0:T(1024)} %get-tuple-element.374, f32[8192,32]{1,0:T(8,128)} %bitcast.203), kind=kCustom, calls=%fused_computation.11.clone.1 | custom fusion | flops 262144 | bytes 3178496 | tf_op jit(solution)/shard_map/while/body/eval_jaxpr/scatter-add | solution.py:65
  643.3 29.2 %gather_fusion.1 = bf16[8192,32]{1,0:T(8,128)(2,1)} fusion(bf16[32,2560]{0,1:T(8,128)(2,1)S(1)} %get-tuple-element.414, s32[8192]{0:T(1024)S(1)} %get-tuple-element.375), kind=kCustom, calls=%fused_computation.1.clone.1 | custom fusion | bytes 1081344 | tf_op jit(solution)/shard_map/while/body/eval_jaxpr/gather | solution.py:58
  682.3 6.1 mul.159
  693.6 44.8 %scatter_fusion.1 = f32[32,2560]{0,1:T(8,128)S(1)} fusion(f32[32,2560]{0,1:T(8,128)S(1)} %get-tuple-element.405, s32[8192]{0:T(1024)} %get-tuple-element.374, f32[8192,32]{1,0:T(8,128)} %bitcast.203), kind=kCustom, calls=%fused_computation.11.clone.1 | custom fusion | flops 262144 | bytes 3178496 | tf_op jit(solution)/shard_map/while/body/eval_jaxpr/scatter-add | solution.py:65
  747.1 6.2 collective-permute-start.7
  755.6 44.6 %psum.38 = f32[2,32,32]{2,1,0:T(8,128)S(1)} all-reduce(f32[2,32,32]{2,1,0:T(8,128)S(1)} %pad_maximum_fusion.4), channel_id=1, replica_groups=mesh['brick'=32] {'brick'}, use_global_device_ids=true, to_apply=%region_17.20 | all-reduce | flops 2048 | bytes 16384 | tf_op jit(solution)/shard_map/psum | solution.py:190
  801.4 39.6 %psum.39 = f32[32,32]{0,1:T(8,128)S(1)} all-reduce(f32[32,32]{0,1:T(8,128)S(1)} %fusion.77), channel_id=1, replica_groups=mesh['brick'=32] {'brick'}, use_global_device_ids=true, to_apply=%region_18.21 | all-reduce | flops 1024 | bytes 8192 | tf_op jit(solution)/shard_map/psum | solution.py:192
  851.5 5.8 cholesky.41
  873.4 57.4 %gather_fusion.8 = bf16[16384,32]{1,0:T(8,128)(2,1)} fusion(bf16[32,2560]{0,1:T(8,128)(2,1)S(1)} %copy.173, s32[16384]{0:T(1024)S(1)} %copy-done.11), kind=kCustom, calls=%fused_computation.8 | custom fusion | bytes 2162688 | tf_op jit(solution)/shard_map/gather | solution.py:210
  (237 shorter events, 154.8 us)
Async XLA Ops:
  52.0 14.3 %copy-start.3 = (bf16[32,2048]{1,0:T(8,128)(2,1)}, bf16[32,2048]{1,0:T(8,128)(2,1)S(1)}, u32[]{:S(2)}) copy-start(bf16[32,2048]{1,0:T(8,128)(2,1)S(1)} %get-tuple-element.290) | copy-start | bytes 393220
  52.0 266.3 %copy-start.1 = (f32[32,2048]{1,0:T(8,128)}, f32[32,2048]{1,0:T(8,128)S(1)}, u32[]{:S(2)}) copy-start(f32[32,2048]{1,0:T(8,128)S(1)} %get-tuple-element.291) | copy-start | bytes 786436
  52.8 10.3 %collective-permute-start = (bf16[33,256]{1,0:T(8,128)(2,1)S(1)}, bf16[33,256]{1,0:T(8,128)(2,1)S(1)}, u32[]{:S(2)}, u32[]{:S(2)}) collective-permute-start(bf16[33,256]{1,0:T(8,128)(2,1)S(1)} %get-tuple-element.272), channel_id=1, source_target_pairs={{0,1},{1,2},{2,3},{3,4},{4,5},{5,6},{6,7},{7,8},{8,9},{9,10},{10,1... | collective-permute-start | bytes 50696 | tf_op jit(solution)/shard_map/ppermute | solution.py:20
  54.1 10.1 %collective-permute-start.1 = (bf16[33,256]{1,0:T(8,128)(2,1)S(1)}, bf16[33,256]{1,0:T(8,128)(2,1)S(1)}, u32[]{:S(2)}, u32[]{:S(2)}) collective-permute-start(bf16[33,256]{1,0:T(8,128)(2,1)S(1)} %get-tuple-element.273), channel_id=1, source_target_pairs={{1,0},{2,1},{3,2},{4,3},{5,4},{6,5},{7,6},{8,7},{9,8},{10,9},{11,1... | collective-permute-start | bytes 50696 | tf_op jit(solution)/shard_map/ppermute | solution.py:22
  259.5 13.7 %copy-start.12 = (f32[2048]{0:T(1024)S(1)}, f32[2048]{0:T(1024)}, u32[]{:S(2)}) copy-start(f32[2048]{0:T(1024)} %param.38) | copy-start | bytes 24580
  261.2 10.5 %collective-permute-start.2 = (bf16[32,256]{1,0:T(8,128)(2,1)S(1)}, bf16[32,256]{1,0:T(8,128)(2,1)S(1)}, u32[]{:S(2)}, u32[]{:S(2)}) collective-permute-start(bf16[32,256]{1,0:T(8,128)(2,1)S(1)} %copy.150), channel_id=1, source_target_pairs={{1,0},{2,1},{3,2},{4,3},{5,4},{6,5},{7,6},{8,7},{9,8},{10,9},{11,1... | collective-permute-start | bytes 49160 | tf_op jit(solution)/shard_map/ppermute | solution.py:32
  263.6 106.1 %copy-start.4 = (bf16[32,2048]{1,0:T(8,128)(2,1)S(1)}, bf16[32,2048]{1,0:T(8,128)(2,1)}, u32[]{:S(2)}) copy-start(bf16[32,2048]{1,0:T(8,128)(2,1)} %copy-done.3) | copy-start | bytes 393220
  263.6 106.1 %copy-start.14 = (bf16[256,33]{0,1:T(8,128)(2,1)S(1)}, bf16[256,33]{0,1:T(8,128)(2,1)}, u32[]{:S(2)}) copy-start(bf16[256,33]{0,1:T(8,128)(2,1)} %copy-done.13) | copy-start | bytes 50692
  263.7 106.1 %copy-start.16 = (bf16[256,33]{0,1:T(8,128)(2,1)S(1)}, bf16[256,33]{0,1:T(8,128)(2,1)}, u32[]{:S(2)}) copy-start(bf16[256,33]{0,1:T(8,128)(2,1)} %copy-done.15) | copy-start | bytes 50692
  263.7 106.1 %copy-start.10 = (s32[16384]{0:T(1024)S(1)}, s32[16384]{0:T(1024)}, u32[]{:S(2)}) copy-start(s32[16384]{0:T(1024)} %fusion.29) | copy-start | bytes 196612
  265.5 7.0 collective-permute-start.3
  366.5 178.5 %copy-start.8 = (bf16[32,2048]{1,0:T(8,128)(2,1)}, bf16[32,2048]{1,0:T(8,128)(2,1)S(1)}, u32[]{:S(2)}) copy-start(bf16[32,2048]{1,0:T(8,128)(2,1)S(1)} %get-tuple-element.292) | copy-start | bytes 393220
  366.5 176.3 %collective-permute-start.4 = (bf16[32,256]{1,0:T(8,128)(2,1)S(1)}, bf16[32,256]{1,0:T(8,128)(2,1)S(1)}, u32[]{:S(2)}, u32[]{:S(2)}) collective-permute-start(bf16[32,256]{1,0:T(8,128)(2,1)S(1)} %get-tuple-element.276), channel_id=1, source_target_pairs={{0,1},{1,2},{2,3},{3,4},{4,5},{5,6},{6,7},{7,8},{8,9},{9,10},{10,1... | collective-permute-start | bytes 49160 | tf_op jit(solution)/shard_map/ppermute | solution.py:20
  367.8 176.1 %collective-permute-start.5 = (bf16[32,256]{1,0:T(8,128)(2,1)S(1)}, bf16[32,256]{1,0:T(8,128)(2,1)S(1)}, u32[]{:S(2)}, u32[]{:S(2)}) collective-permute-start(bf16[32,256]{1,0:T(8,128)(2,1)S(1)} %get-tuple-element.277), channel_id=1, source_target_pairs={{1,0},{2,1},{3,2},{4,3},{5,4},{6,5},{7,6},{8,7},{9,8},{10,9},{11,1... | collective-permute-start | bytes 49160 | tf_op jit(solution)/shard_map/ppermute | solution.py:22
  369.8 173.1 %copy-start.22 = (s32[1024]{0:T(1024)S(1)}, s32[1024]{0:T(1024)}, u32[]{:S(2)}) copy-start(s32[1024]{0:T(1024)} %copy-done.21) | copy-start | bytes 12292
  369.8 174.2 %copy-start.20 = (s32[1024]{0:T(1024)S(1)}, s32[1024]{0:T(1024)}, u32[]{:S(2)}) copy-start(s32[1024]{0:T(1024)} %copy-done.19) | copy-start | bytes 12292
  738.4 16.4 %copy-start.2 = (f32[32,2048]{1,0:T(8,128)S(1)}, f32[32,2048]{1,0:T(8,128)}, u32[]{:S(2)}) copy-start(f32[32,2048]{1,0:T(8,128)} %copy-done.1) | copy-start | bytes 786436
  740.3 13.0 %collective-permute-start.6 = (bf16[32,256]{1,0:T(8,128)(2,1)S(1)}, bf16[32,256]{1,0:T(8,128)(2,1)S(1)}, u32[]{:S(2)}, u32[]{:S(2)}) collective-permute-start(bf16[32,256]{1,0:T(8,128)(2,1)S(1)} %copy.163), channel_id=1, source_target_pairs={{1,0},{2,1},{3,2},{4,3},{5,4},{6,5},{7,6},{8,7},{9,8},{10,9},{11,1... | collective-permute-start | bytes 49160 | tf_op jit(solution)/shard_map/ppermute | solution.py:32
  747.1 7.0 collective-permute-start.7
  755.2 108.4 %copy-start.18 = (f32[32,32]{0,1:T(8,128)S(1)}, f32[32,32]{0,1:T(8,128)}, u32[]{:S(2)}) copy-start(f32[32,32]{0,1:T(8,128)} %get-tuple-element.281) | copy-start | bytes 12292
  755.2 108.9 %copy-start.5 = (bf16[32,2048]{1,0:T(8,128)(2,1)S(1)}, bf16[32,2048]{1,0:T(8,128)(2,1)}, u32[]{:S(2)}) copy-start(bf16[32,2048]{1,0:T(8,128)(2,1)} %copy-done.3) | copy-start | bytes 393220
  800.2 64.5 %copy-start.9 = (bf16[32,2048]{1,0:T(8,128)(2,1)S(1)}, bf16[32,2048]{1,0:T(8,128)(2,1)}, u32[]{:S(2)}) copy-start(bf16[32,2048]{1,0:T(8,128)(2,1)} %copy-done.8) | copy-start | bytes 393220
  865.0 3.7 collective-permute-start.8
  866.3 5.6 collective-permute-start.9
  (15 other events, 71.1 us)
where the time goes:
time: 940 us; the launch traced here: 936 us
  local copies, waits for them, and re-layouts  430 us (46%)
  other arithmetic  248 us (26%)
  blocking collectives  210 us (22%)
  starting transfers between devices  22.9 us (2%)
  matrix products  18.9 us (2%)
    scatter-add x4, other arithmetic, one_block(): total.at[:, block_conn].add(result.reshape(rows, block_size, slot_count))  179 us
    gather x1, local copies, waits for them, and re-layouts, on_device(): displace_elem = displace_ext[connectivity]  173 us
    gather x4, local copies, waits for them, and re-layouts, one_block(): values = extended[:, block_conn]  117 us
    psum x2, blocking collectives, on_device(): current_proj = lax.psum(local_proj, 'brick')  89.4 us
    psum x2, blocking collectives, on_device(): gram_next = lax.psum(inner(reduced, reduced), 'brick')  78.8 us
    gather x2, local copies, waits for them, and re-layouts, on_device(): adjoint_elem = adjoint_ext[:, connectivity]  61 us
    psum x1, blocking collectives, on_device(): start_matrix = lax.psum(inner(sensitivity, sensitivity), 'brick')  42.1 us
    mul x12, local copies, waits for them, and re-layouts, one_block(): values[:, :, None, :] * block_coeff.T[None, :, :, None]  35.6 us
  transfers between devices with their start and end apart: 10, of which 3 were waited for; matrix products, arithmetic and copies ran while one was open for 21% of the time, Pallas kernels for 0%

commit v1 on v0

v1 whole, which is shorter than its diff:
```python
import functools

import jax
import jax.numpy as jnp
from jax import lax
from jax.experimental import pallas as pl
from jax.experimental.pallas import tpu as pltpu
from jax.sharding import PartitionSpec as P

LO = 256
CHUNK = 8
VMEM_LIMIT = 40 * 1024 * 1024
F32 = jnp.float32
BF16 = jnp.bfloat16
NN = (((1,), (0,)), ((), ()))
NT = (((1,), (1,)), ((), ()))
TN = (((0,), (0,)), ((), ()))


def fdot(a, b, dims=NN):
    return lax.dot_general(a, b, dims, precision=lax.Precision.HIGHEST, preferred_element_type=F32)


def bdot(a, b, dims=NN):
    return lax.dot_general(a, b, dims, preferred_element_type=F32)


def eye(n):
    return (
        lax.broadcasted_iota(jnp.int32, (n, n), 0) == lax.broadcasted_iota(jnp.int32, (n, n), 1)
    ).astype(F32)


def lower_inverse(gram):
    n = gram.shape[0]
    row_id = lax.broadcasted_iota(jnp.int32, (n, n), 0)
    col_id = lax.broadcasted_iota(jnp.int32, (n, n), 1)
    work, side = gram, eye(n)
    for k in range(n):
        pivot = work[k : k + 1, k : k + 1]
        step = jnp.where(row_id[:, :1] > k, work[:, k : k + 1] / pivot, 0.0)
        side = side - step * side[k : k + 1, :]
        work = work - step * work[k : k + 1, :]
    diag = jnp.sum(jnp.where(row_id == col_id, work, 0.0), axis=1, keepdims=True)
    scale = 1.0 / jnp.sqrt(diag)
    return side * scale, jnp.where(col_id >= row_id, work, 0.0) * scale


def one_hot(lo_rows):
    lane = lax.broadcasted_iota(jnp.int32, (LO, lo_rows.shape[1]), 0)
    return jnp.concatenate(
        [
            jnp.where(lane == lo_rows[e : e + 1, :], 1.0, 0.0).astype(BF16)
            for e in range(lo_rows.shape[0])
        ],
        axis=1,
    )


def stack_tiles(field):
    return jnp.concatenate(
        [field[:, h * LO : (h + 1) * LO] for h in range(field.shape[1] // LO)], axis=0
    )


def gathered(tiles, hot, hi_rows, rows):
    spread = bdot(tiles, hot)
    slots = hi_rows.shape[1]
    values = []
    for e in range(hi_rows.shape[0]):
        value = jnp.zeros((rows, slots), F32)
        for h in range(tiles.shape[0] // rows):
            value = jnp.where(
                hi_rows[e : e + 1, :] == h,
                spread[h * rows : (h + 1) * rows, e * slots : (e + 1) * slots],
                value,
            )
        values.append(value)
    return values


def apply_elements(half, hi_ref, lo_ref, coeff_ref, stacked_ref, tiles_ref, total_ref):
    rows, width = half.shape
    tiles = width // LO
    elems, slots = lo_ref.shape
    tiles_ref[...] = stack_tiles(half)
    total_ref[...] = jnp.zeros_like(total_ref)

    def chunk(step, carry):
        start = pl.multiple_of(step * CHUNK, CHUNK)
        hi_rows = hi_ref[pl.ds(start, CHUNK), :]
        hot = one_hot(lo_ref[pl.ds(start, CHUNK), :])
        values = gathered(tiles_ref[...], hot, hi_rows, rows)
        scaled = jnp.concatenate(
            [
                jnp.concatenate(
                    [(values[e] * coeff_ref[k, start + e]).astype(BF16) for k in range(3)], axis=1
                )
                for e in range(CHUNK)
            ],
            axis=0,
        )
        result = bdot(scaled, stacked_ref[...])
        spread = jnp.concatenate(
            [
                jnp.concatenate(
                    [
                        jnp.where(
                            hi_rows[e : e + 1, :] == h, result[e * rows : (e + 1) * rows, :], 0.0
                        ).astype(BF16)
                        for e in range(CHUNK)
                    ],
                    axis=1,
                )
                for h in range(tiles)
            ],
            axis=0,
        )
        total_ref[...] += bdot(spread, hot, NT)
        return carry

    lax.fori_loop(0, elems // CHUNK, chunk, 0)
    return jnp.concatenate([total_ref[h * rows : (h + 1) * rows, :] for h in range(tiles)], axis=1)


def write_image(basis, partial, diag_ref, image_ref, low_ref, high_ref, ghost):
    width = basis.shape[1]
    own = diag_ref[...] * basis[:, ghost : width - ghost] + partial[:, ghost : width - ghost]
    owned = own.shape[1]
    image_ref[:, :ghost] = partial[:, :ghost]
    image_ref[:, ghost : width - ghost] = own
    image_ref[:, width - ghost :] = partial[:, width - ghost :]
    low_ref[:, :ghost] = own[:, :ghost]
    low_ref[:, ghost:] = partial[:, :ghost]
    high_ref[:, :ghost] = own[:, owned - ghost :]
    high_ref[:, ghost:] = partial[:, width - ghost :]


def prepare_kernel(edge_ref, conn_ref, owner_ref, disp_ref, templ_ref, hi_ref, lo_ref, push_ref, elem_ref):
    elems, slots = conn_ref.shape
    last = disp_ref.shape[0] - 1
    first_hi = edge_ref[0]
    last_hi = edge_ref[1]
    owner = owner_ref[...].astype(F32).astype(BF16)
    disp = disp_ref[...]

    def chunk(step, carry):
        start = pl.multiple_of(step * CHUNK, CHUNK)
        conn = conn_ref[pl.ds(start, CHUNK), :]
        hi = conn // LO
        lo = conn - hi * LO
        renamed = bdot(owner, one_hot(lo))
        below = jnp.concatenate(
            [renamed[0:1, e * slots : (e + 1) * slots] for e in range(CHUNK)], axis=0
        ).astype(jnp.int32)
        above = jnp.concatenate(
            [renamed[1:2, e * slots : (e + 1) * slots] for e in range(CHUNK)], axis=0
        ).astype(jnp.int32)
        lo = jnp.where(hi == 0, below, jnp.where(hi == last, above, lo))
        hi = jnp.where((hi < first_hi) | (hi > last_hi), -1, hi)
        hi_ref[pl.ds(start, CHUNK), :] = hi
        lo_ref[pl.ds(start, CHUNK), :] = lo
        spread = bdot(disp, one_hot(lo))
        hi_id = lax.broadcasted_iota(jnp.int32, (last + 1, slots), 0)
        elem_ref[pl.ds(start, CHUNK), :] = jnp.concatenate(
            [
                jnp.sum(
                    jnp.where(
                        hi_id == hi[e : e + 1, :], spread[:, e * slots : (e + 1) * slots], 0.0
                    ),
                    axis=0,
                    keepdims=True,
                )
                for e in range(CHUNK)
            ],
            axis=0,
        )
        return carry

    lax.fori_loop(0, elems // CHUNK, chunk, 0)
    values = elem_ref[...].astype(BF16)
    for k in range(3):
        push_ref[:, k * elems : (k + 1) * elems] = bdot(templ_ref[k], values, NT).astype(BF16)


def first_kernel(
    gram_ref, sens_ref, low_in, high_in, diag_ref, hi_ref, lo_ref, coeff_ref, stacked_ref,
    basis_ref, image_ref, low_ref, high_ref, factor_ref, tiles_ref, total_ref,
):
    ghost = low_in.shape[1]
    inverse, factor = lower_inverse(gram_ref[...])
    factor_ref[...] = factor
    basis = jnp.concatenate(
        [fdot(inverse, low_in[...]), fdot(inverse, sens_ref[...]), fdot(inverse, high_in[...])], axis=1
    )
    basis_ref[...] = basis
    partial = apply_elements(
        basis.astype(BF16), hi_ref, lo_ref, coeff_ref, stacked_ref, tiles_ref, total_ref
    )
    write_image(basis, partial, diag_ref, image_ref, low_ref, high_ref, ghost)


def complete(image_ref, low_in, high_in, full_ref):
    width = image_ref.shape[1]
    ghost = low_in.shape[1] // 2
    full_ref[:, :ghost] = image_ref[:, :ghost] + low_in[:, :ghost]
    full_ref[:, ghost : 2 * ghost] = image_ref[:, ghost : 2 * ghost] + low_in[:, ghost:]
    full_ref[:, 2 * ghost : width - 2 * ghost] = image_ref[:, 2 * ghost : width - 2 * ghost]
    full_ref[:, width - 2 * ghost : width - ghost] = (
        image_ref[:, width - 2 * ghost : width - ghost] + high_in[:, ghost:]
    )
    full_ref[:, width - ghost :] = image_ref[:, width - ghost :] + high_in[:, :ghost]


def gram_kernel(*refs):
    *basis_refs, image_ref, low_in, high_in, full_ref, gram_ref = refs
    complete(image_ref, low_in, high_in, full_ref)
    ghost = low_in.shape[1] // 2
    width = full_ref.shape[1]
    own = full_ref[:, ghost : width - ghost]
    for place, ref in enumerate(basis_refs):
        gram_ref[place] = fdot(ref[:, ghost : width - ghost], own, NT)
    gram_ref[len(basis_refs)] = fdot(own, own, NT)


def second_kernel(
    gram_ref, basis0_ref, full_ref, diag_ref, hi_ref, lo_ref, coeff_ref, stacked_ref,
    basis_ref, image_ref, low_ref, high_ref, factor_ref, tiles_ref, total_ref,
):
    ghost = low_ref.shape[1] // 2
    proj = gram_ref[0]
    inverse, factor = lower_inverse(gram_ref[1] - fdot(proj, proj, TN))
    factor_ref[...] = factor
    reduced = full_ref[...] - fdot(proj, basis0_ref[...], TN)
    basis = fdot(inverse, reduced)
    basis_ref[...] = basis
    partial = apply_elements(
        basis.astype(BF16), hi_ref, lo_ref, coeff_ref, stacked_ref, tiles_ref, total_ref
    )
    write_image(basis, partial, diag_ref, image_ref, low_ref, high_ref, ghost)


def last_kernel(
    gram0_ref, gram1_ref, factor0_ref, factor1_ref, basis0_ref, basis1_ref, hi_ref, lo_ref, push_ref,
    sticks_ref, adjoint_ref, grads_ref, tiles_ref, pairs_ref,
):
    rows, width = basis0_ref.shape
    ghost = (width - adjoint_ref.shape[1]) // 2
    elems, slots = lo_ref.shape
    p00, n00 = gram0_ref[0], gram0_ref[1]
    p01, p11, n11 = gram1_ref[0], gram1_ref[1], gram1_ref[2]
    upper0, upper1 = factor0_ref[...], factor1_ref[...]
    head, unused = lower_inverse(n00)
    head_side = fdot(head, fdot(p00, upper0, TN))
    n01 = fdot(p00, p01, TN) + fdot(upper1, p11, TN)
    cross = fdot(head, n01)
    tail, unused = lower_inverse(n11 - fdot(cross, cross, TN))
    tail_side = fdot(tail, fdot(p01, upper0, TN) - fdot(cross, head_side, TN))
    w1 = fdot(tail, tail_side, TN)
    w0 = fdot(head, head_side - fdot(cross, w1), TN)
    basis0, basis1 = basis0_ref[...], basis1_ref[...]
    adjoint_ref[...] = fdot(w0, basis0[:, ghost : width - ghost], TN) + fdot(
        w1, basis1[:, ghost : width - ghost], TN
    )
    half0, half1 = basis0.astype(BF16).astype(F32), basis1.astype(BF16).astype(F32)
    tiles_ref[...] = stack_tiles((fdot(w0, half0, TN) + fdot(w1, half1, TN)).astype(BF16))
    pairs_ref[...] = jnp.zeros_like(pairs_ref)
    lane = lax.broadcasted_iota(jnp.int32, (rows, 3 * elems), 1) % elems

    def chunk(step, carry):
        start = pl.multiple_of(step * CHUNK, CHUNK)
        hot = one_hot(lo_ref[pl.ds(start, CHUNK), :])
        values = gathered(tiles_ref[...], hot, hi_ref[pl.ds(start, CHUNK), :], rows)
        every = bdot(jnp.concatenate(values, axis=0).astype(BF16), push_ref[...])
        pairs = pairs_ref[...]
        for e in range(CHUNK):
            pairs = jnp.where(lane == start + e, every[e * rows : (e + 1) * rows, :], pairs)
        pairs_ref[...] = pairs
        return carry

    lax.fori_loop(0, elems // CHUNK, chunk, 0)
    third = pairs_ref[:, 2 * elems :]
    grads_ref[0] = -(pairs_ref[:, :elems] + sticks_ref[0:1, :] * third)
    grads_ref[1] = -pairs_ref[:, elems : 2 * elems]
    grads_ref[2] = -sticks_ref[1:2, :] * third


def call(kernel, outs, scratch, args, smem=()):
    return pl.pallas_call(
        kernel,
        out_shape=[jax.ShapeDtypeStruct(shape, dtype) for shape, dtype in outs],
        in_specs=[
            pl.BlockSpec(memory_space=pltpu.SMEM if i in smem else pltpu.VMEM)
            for i in range(len(args))
        ],
        out_specs=[pl.BlockSpec(memory_space=pltpu.VMEM) for unused in outs],
        scratch_shapes=[pltpu.VMEM(shape, dtype) for shape, dtype in scratch],
        compiler_params=pltpu.CompilerParams(vmem_limit_bytes=VMEM_LIMIT),
    )(*args)


def total(value, axis):
    count = lax.axis_size(axis)
    stride = 1
    while stride < count:
        left = count // stride
        radix = 2 if stride == 1 or left % 4 else 4
        parts = [value]
        for d in range(1, radix):
            route = []
            for i in range(count):
                digit = (i // stride) % radix
                route.append((i, i + ((digit ^ d) - digit) * stride))
            parts.append(lax.ppermute(value, axis, route))
        while len(parts) > 1:
            parts = [parts[2 * i] + parts[2 * i + 1] for i in range(len(parts) // 2)]
        value = parts[0]
        stride *= radix
    return value


def on_device(
    sensitivity, diagonal, displacement, connectivity, normal_stiff, shear_stiff, friction, slip_state,
    owner_map, templates,
):
    axis = "brick"
    count = lax.axis_size(axis)
    me = lax.axis_index(axis)
    up = [(i, i + 1) for i in range(count - 1)]
    down = [(i + 1, i) for i in range(count - 1)]
    rows, owned = sensitivity.shape
    ghost = owner_map.shape[2]
    elems, slots = connectivity.shape
    width = owned + 2 * ghost
    tiles = width // LO
    wide = ((rows, width), F32)
    band = ((rows, 2 * ghost), F32)
    small = ((rows, rows), F32)
    work = [((tiles * rows, LO), BF16), ((tiles * rows, LO), F32)]

    gram = fdot(sensitivity, sensitivity, NT)
    low_sens = lax.ppermute(sensitivity[:, owned - ghost :], axis, up)
    high_sens = lax.ppermute(sensitivity[:, :ghost], axis, down)
    low_disp = lax.ppermute(displacement[owned - ghost :], axis, up)
    high_disp = lax.ppermute(displacement[:ghost], axis, down)
    gram = total(gram, axis)

    slip = slip_state.astype(F32)
    coeffs = jnp.stack([normal_stiff, shear_stiff, slip * friction * normal_stiff])
    sticks = jnp.stack([slip * friction, slip * normal_stiff])
    stacked = templates.reshape(3 * slots, slots)
    diag_row = diagonal[None, :]
    edges = jnp.stack([jnp.where(me == 0, 1, 0), jnp.where(me == count - 1, tiles - 2, tiles - 1)])
    disp_tiles = jnp.concatenate([low_disp, displacement, high_disp]).reshape(tiles, LO)
    hi, lo, pushed = call(
        prepare_kernel,
        [((elems, slots), jnp.int32), ((elems, slots), jnp.int32), ((slots, 3 * elems), BF16)],
        [((elems, slots), F32)],
        [edges.astype(jnp.int32), connectivity, owner_map[0], disp_tiles, templates],
        smem=(0,),
    )

    basis0, image, low, high, factor0 = call(
        first_kernel,
        [wide, wide, band, band, small],
        work,
        [gram, sensitivity, low_sens, high_sens, diag_row, hi, lo, coeffs, stacked],
        smem=(7,),
    )
    low, high = lax.ppermute(high, axis, up), lax.ppermute(low, axis, down)
    full, gram0 = call(
        gram_kernel, [wide, ((2, rows, rows), F32)], [], [basis0, image, low, high]
    )
    gram0 = total(gram0, axis)

    basis1, image, low, high, factor1 = call(
        second_kernel,
        [wide, wide, band, band, small],
        work,
        [gram0, basis0, full, diag_row, hi, lo, coeffs, stacked],
        smem=(6,),
    )
    low, high = lax.ppermute(high, axis, up), lax.ppermute(low, axis, down)
    unused, gram1 = call(
        gram_kernel, [wide, ((3, rows, rows), F32)], [], [basis0, basis1, image, low, high]
    )
    gram1 = total(gram1, axis)

    adjoint, grads = call(
        last_kernel,
        [((rows, owned), F32), ((3, rows, elems), F32)],
        [((tiles * rows, LO), BF16), ((rows, 3 * elems), F32)],
        [gram0, gram1, factor0, factor1, basis0, basis1, hi, lo, pushed, sticks],
    )
    return adjoint, grads


def solution(mesh):
    in_specs = (
        P(None, "brick"),
        P("brick"),
        P("brick"),
        P("brick", None),
        P("brick"),
        P("brick"),
        P("brick"),
        P("brick"),
        P("brick", None, None),
        P(),
    )
    out_specs = (P(None, "brick"), P(None, None, "brick"))
    return jax.shard_map(
        on_device, mesh=mesh, in_specs=in_specs, out_specs=out_specs, check_vma=False
    )
```

time: 940 us -> 144 us (0.15)
  local copies, waits for them, and re-layouts: 430 us -> 2.65 us
  other arithmetic: 248 us -> 0.2 us
  blocking collectives: 210 us -> 0 us
  Pallas kernels: 0 us -> 64.6 us
  starting transfers between devices: 22.9 us -> 52.6 us
  waiting for transfers between devices: 3.75 us -> 21.5 us
  matrix products: 18.9 us -> 1.38 us
    gather x19 -> x0, local copies, waits for them, and re-layouts: 356 us -> none  [the longest x1 173 us: on_device(): displace_elem = displace_ext[connectivity]]
    psum x5 -> x0, blocking collectives: 210 us -> none  [the longest x2 89.4 us: on_device(): current_proj = lax.psum(local_proj, 'brick')]
    scatter-add x12 -> x0, other arithmetic: 187 us -> none  [the longest x4 179 us: one_block(): total.at[:, block_conn].add(result.reshape(rows, block_size, slot_count))]
    pallas_call x0 -> x6, Pallas kernels: none -> 64.6 us  [call(): pl.pallas_call(kernel, out_shape=[jax.ShapeDtypeStruct(shape, dtype) for...]
    mul x12 -> x0, local copies, waits for them, and re-layouts: 35.6 us -> none  [one_block(): values[:, :, None, :] * block_coeff.T[None, :, :, None]]
    another operation x25 -> x4, other arithmetic: 35.5 us -> 0.1 us  [the longest x1 0.07 us: on_device(): jnp.stack([jnp.where(me == 0, 1, 0), jnp.where(me == count - 1, tiles - 2...]
    ppermute x10 -> x29, starting transfers between devices: 22.9 us -> 52.6 us  [the longest x21 39.8 us: total(): parts.append(lax.ppermute(value, axis, route))]
    ppermute x10 -> x29, waiting for transfers between devices: 3.75 us -> 21.5 us  [the longest x21 16.2 us: total(): parts.append(lax.ppermute(value, axis, route))]
  transfers between devices with their start and end apart: 10 -> 29, of which waited for: 3 -> 16; matrix products, arithmetic and copies ran while one was open for 21% -> 1% of each run, Pallas kernels for 0% -> 5%
where the time goes in v1:
time: 144 us
  Pallas kernels  64.6 us (45%)
  starting transfers between devices  52.6 us (37%)
  waiting for transfers between devices  21.5 us (15%)
  local copies, waits for them, and re-layouts  2.65 us (2%)
    pallas_call x6, Pallas kernels, call(): pl.pallas_call(kernel, out_shape=[jax.ShapeDtypeStruct(shape, dtype) for...  64.6 us
    ppermute x21, starting transfers between devices, total(): parts.append(lax.ppermute(value, axis, route))  39.8 us
    ppermute x21, waiting for transfers between devices, total(): parts.append(lax.ppermute(value, axis, route))  16.2 us
    ppermute x4, starting transfers between devices, on_device(): low, high = (lax.ppermute(high, axis, up), lax.ppermute(low, axis, down))  5.45 us
    ppermute x4, waiting for transfers between devices, on_device(): low, high = (lax.ppermute(high, axis, up), lax.ppermute(low, axis, down))  5.26 us
  transfers between devices with their start and end apart: 29, of which 16 were waited for; matrix products, arithmetic and copies ran while one was open for 1% of the time, Pallas kernels for 5%

profile of v1, /device:TPU:0, one launch (start us, length us, event | category | flops | bytes accessed | tf_op | source)
XLA Modules:
  0.0 143.9 jit_solution(10722644136655902511)
XLA Ops:
  1.3 2.3 %collective-permute-start.9 = (bf16[256]{0:T(256)(128)(2,1)S(1)}, bf16[256]{0:T(256)(128)(2,1)S(1)}, u32[]{:S(2)}, u32[]{:S(2)}) collective-permute-start(bf16[256]{0:T(256)(128)(2,1)S(1)} %get-tuple-element.36), channel_id=1, source_target_pairs={{0,1},{1,2},{2,3},{3,4},{4,5},{5,6},{6,7},{7,8},{8,9},{9,10},{10,1... | collective-permute-start | bytes 1544 | tf_op jit(solution)/shard_map/ppermute | solution.py:344
  6.6 3.3 %collective-permute-start = (f32[32,32]{1,0:T(8,128)S(1)}, f32[32,32]{1,0:T(8,128)S(1)}, u32[]{:S(2)}, u32[]{:S(2)}) collective-permute-start(f32[32,32]{1,0:T(8,128)S(1)} %fusion.3), channel_id=1, source_target_pairs={{0,1},{1,0},{2,3},{3,2},{4,5},{5,4},{6,7},{7,6},{8,9},{9,8},{10,11... | collective-permute-start | bytes 12296 | tf_op jit(solution)/shard_map/ppermute | solution.py:314
  10.7 3.0 %collective-permute-start.3 = (f32[32,32]{1,0:T(8,128)S(1)}, f32[32,32]{1,0:T(8,128)S(1)}, u32[]{:S(2)}, u32[]{:S(2)}) collective-permute-start(f32[32,32]{1,0:T(8,128)S(1)} %add.63), channel_id=1, source_target_pairs={{0,6},{1,7},{2,4},{3,5},{4,2},{5,3},{6,0},{7,1},{8,14},{9,15},{10,... | collective-permute-start | bytes 12296 | tf_op jit(solution)/shard_map/ppermute | solution.py:314
  17.4 2.3 %collective-permute-start.7 = (f32[32,256]{1,0:T(8,128)S(1)}, f32[32,256]{1,0:T(8,128)S(1)}, u32[]{:S(2)}, u32[]{:S(2)}) collective-permute-start(f32[32,256]{1,0:T(8,128)S(1)} %get-tuple-element.35), channel_id=1, source_target_pairs={{0,1},{1,2},{2,3},{3,4},{4,5},{5,6},{6,7},{7,8},{8,9},{9,10},{10,1... | collective-permute-start | bytes 98312 | tf_op jit(solution)/shard_map/ppermute | solution.py:342
  19.8 6.0 %collective-permute-start.6 = (f32[32,32]{1,0:T(8,128)S(1)}, f32[32,32]{1,0:T(8,128)S(1)}, u32[]{:S(2)}, u32[]{:S(2)}) collective-permute-start(f32[32,32]{1,0:T(8,128)S(1)} %add_add_fusion.5), channel_id=1, source_target_pairs={{0,24},{1,25},{2,26},{3,27},{4,28},{5,29},{6,30},{7,31},{8,16},{9,... | collective-permute-start | bytes 12296 | tf_op jit(solution)/shard_map/ppermute | solution.py:314
  27.1 7.1 %shard_map.113 = (s32[128,128]{1,0:T(8,128)S(1)}, s32[128,128]{1,0:T(8,128)S(1)}, bf16[128,384]{1,0:T(8,128)(2,1)S(1)}) custom-call(s32[2]{0:T(128)S(1)} %pad_add_fusion.edge_ref, s32[128,128]{1,0:T(8,128)S(1)} %copy-done.2, s32[2,256]{1,0:T(2,128)S(1)} %bitcast.19, bf16[10,256]{1,0:T(8,128)(2,1)S(1)} %reshape.10.disp_ref, bf16[3,128,128]{2,1,0:T(8,128)(2,1)S(1)} %copy-done.1), custom_call_target="tpu_custom_call" | custom-call | tf_op jit(solution)/shard_map/pallas_call | solution.py:289
  34.9 19.3 %shard_map.114 = (f32[32,2560]{1,0:T(8,128)S(1)}, f32[32,2560]{1,0:T(8,128)S(1)}, f32[32,512]{1,0:T(8,128)S(1)}, f32[32,512]{1,0:T(8,128)S(1)}, f32[32,32]{1,0:T(8,128)S(1)}) custom-call(f32[32,32]{1,0:T(8,128)S(1)} %add_add_fusion.4.gram_ref, f32[32,2048]{1,0:T(8,128)S(1)} %copy-done, f32[32,256]{1,0:T(8,128)S(1)} %collective-permute-done.7.low_in, ...), custom_call_target="tpu_custom_call" | custom-call | tf_op jit(solution)/shard_map/pallas_call | solution.py:289
  54.2 1.6 %collective-permute-start.11 = (f32[32,512]{1,0:T(8,128)S(1)}, f32[32,512]{1,0:T(8,128)S(1)}, u32[]{:S(2)}, u32[]{:S(2)}) collective-permute-start(f32[32,512]{1,0:T(8,128)S(1)} %get-tuple-element.22), channel_id=1, source_target_pairs={{0,1},{1,2},{2,3},{3,4},{4,5},{5,6},{6,7},{7,8},{8,9},{9,10},{10,1... | collective-permute-start | bytes 196616 | tf_op jit(solution)/shard_map/ppermute | solution.py:370
  57.1 1.9 %collective-permute-done.12.refs_3_ = f32[32,512]{1,0:T(8,128)S(1)} collective-permute-done((f32[32,512]{1,0:T(8,128)S(1)}, f32[32,512]{1,0:T(8,128)S(1)}, u32[]{:S(2)}, u32[]{:S(2)}) %collective-permute-start.12) | collective-permute-done | bytes 65568 | tf_op jit(solution)/shard_map/ppermute | solution.py:370
  59.6 2.9 %collective-permute-start.13 = (f32[2,32,32]{2,1,0:T(8,128)S(1)}, f32[2,32,32]{2,1,0:T(8,128)S(1)}, u32[]{:S(2)}, u32[]{:S(2)}) collective-permute-start(f32[2,32,32]{2,1,0:T(8,128)S(1)} %get-tuple-element.24), channel_id=1, source_target_pairs={{0,1},{1,0},{2,3},{3,2},{4,5},{5,4},{6,7},{7,6},{8,9},{9,8},{10,11... | collective-permute-start | bytes 24584 | tf_op jit(solution)/shard_map/ppermute | solution.py:314
  63.4 5.5 %collective-permute-start.16 = (f32[2,32,32]{2,1,0:T(8,128)S(1)}, f32[2,32,32]{2,1,0:T(8,128)S(1)}, u32[]{:S(2)}, u32[]{:S(2)}) collective-permute-start(f32[2,32,32]{2,1,0:T(8,128)S(1)} %add.70), channel_id=1, source_target_pairs={{0,6},{1,7},{2,4},{3,5},{4,2},{5,3},{6,0},{7,1},{8,14},{9,15},{10,... | collective-permute-start | bytes 24584 | tf_op jit(solution)/shard_map/ppermute | solution.py:314
  70.7 2.0 %collective-permute-done.15 = f32[2,32,32]{2,1,0:T(8,128)S(1)} collective-permute-done((f32[2,32,32]{2,1,0:T(8,128)S(1)}, f32[2,32,32]{2,1,0:T(8,128)S(1)}, u32[]{:S(2)}, u32[]{:S(2)}) %collective-permute-start.15) | collective-permute-done | bytes 8224 | tf_op jit(solution)/shard_map/ppermute | solution.py:314
  72.8 2.6 %collective-permute-start.19 = (f32[2,32,32]{2,1,0:T(8,128)S(1)}, f32[2,32,32]{2,1,0:T(8,128)S(1)}, u32[]{:S(2)}, u32[]{:S(2)}) collective-permute-start(f32[2,32,32]{2,1,0:T(8,128)S(1)} %add_add_fusion.3), channel_id=1, source_target_pairs={{0,24},{1,25},{2,26},{3,27},{4,28},{5,29},{6,30},{7,31},{8,16},{9,... | collective-permute-start | bytes 24584 | tf_op jit(solution)/shard_map/ppermute | solution.py:314
  78.6 1.6 %collective-permute-done.18 = f32[2,32,32]{2,1,0:T(8,128)S(1)} collective-permute-done((f32[2,32,32]{2,1,0:T(8,128)S(1)}, f32[2,32,32]{2,1,0:T(8,128)S(1)}, u32[]{:S(2)}, u32[]{:S(2)}) %collective-permute-start.18) | collective-permute-done | bytes 8224 | tf_op jit(solution)/shard_map/ppermute | solution.py:314
  80.2 19.5 %shard_map.116 = (f32[32,2560]{1,0:T(8,128)S(1)}, f32[32,2560]{1,0:T(8,128)S(1)}, f32[32,512]{1,0:T(8,128)S(1)}, f32[32,512]{1,0:T(8,128)S(1)}, f32[32,32]{1,0:T(8,128)S(1)}) custom-call(f32[2,32,32]{2,1,0:T(8,128)S(1)} %add_add_fusion.2.gram_ref.gram0_ref, f32[32,2560]{1,0:T(8,128)S(1)} %get-tuple-element.20.refs_0_.basis0_ref, ...), custom_call_target="tpu_custom_call" | custom-call | tf_op jit(solution)/shard_map/pallas_call | solution.py:289
  102.4 3.3 %collective-permute-done.21.refs_4_ = f32[32,512]{1,0:T(8,128)S(1)} collective-permute-done((f32[32,512]{1,0:T(8,128)S(1)}, f32[32,512]{1,0:T(8,128)S(1)}, u32[]{:S(2)}, u32[]{:S(2)}) %collective-permute-start.21) | collective-permute-done | bytes 65568 | tf_op jit(solution)/shard_map/ppermute | solution.py:383
  107.1 2.9 %collective-permute-start.22 = (f32[3,32,32]{2,1,0:T(8,128)S(1)}, f32[3,32,32]{2,1,0:T(8,128)S(1)}, u32[]{:S(2)}, u32[]{:S(2)}) collective-permute-start(f32[3,32,32]{2,1,0:T(8,128)S(1)} %get-tuple-element.30), channel_id=1, source_target_pairs={{0,1},{1,0},{2,3},{3,2},{4,5},{5,4},{6,7},{7,6},{8,9},{9,8},{10,11... | collective-permute-start | bytes 36872 | tf_op jit(solution)/shard_map/ppermute | solution.py:314
  110.9 3.9 %collective-permute-start.25 = (f32[3,32,32]{2,1,0:T(8,128)S(1)}, f32[3,32,32]{2,1,0:T(8,128)S(1)}, u32[]{:S(2)}, u32[]{:S(2)}) collective-permute-start(f32[3,32,32]{2,1,0:T(8,128)S(1)} %add.77), channel_id=1, source_target_pairs={{0,6},{1,7},{2,4},{3,5},{4,2},{5,3},{6,0},{7,1},{8,14},{9,15},{10,... | collective-permute-start | bytes 36872 | tf_op jit(solution)/shard_map/ppermute | solution.py:314
  115.5 1.6 %collective-permute-done.25 = f32[3,32,32]{2,1,0:T(8,128)S(1)} collective-permute-done((f32[3,32,32]{2,1,0:T(8,128)S(1)}, f32[3,32,32]{2,1,0:T(8,128)S(1)}, u32[]{:S(2)}, u32[]{:S(2)}) %collective-permute-start.25) | collective-permute-done | bytes 12320 | tf_op jit(solution)/shard_map/ppermute | solution.py:314
  117.1 1.8 %collective-permute-done.24 = f32[3,32,32]{2,1,0:T(8,128)S(1)} collective-permute-done((f32[3,32,32]{2,1,0:T(8,128)S(1)}, f32[3,32,32]{2,1,0:T(8,128)S(1)}, u32[]{:S(2)}, u32[]{:S(2)}) %collective-permute-start.24) | collective-permute-done | bytes 12320 | tf_op jit(solution)/shard_map/ppermute | solution.py:314
  119.2 2.9 %collective-permute-start.28 = (f32[3,32,32]{2,1,0:T(8,128)S(1)}, f32[3,32,32]{2,1,0:T(8,128)S(1)}, u32[]{:S(2)}, u32[]{:S(2)}) collective-permute-start(f32[3,32,32]{2,1,0:T(8,128)S(1)} %add_add_fusion.1), channel_id=1, source_target_pairs={{0,24},{1,25},{2,26},{3,27},{4,28},{5,29},{6,30},{7,31},{8,16},{9,... | collective-permute-start | bytes 36872 | tf_op jit(solution)/shard_map/ppermute | solution.py:314
  123.6 1.6 %collective-permute-done.28 = f32[3,32,32]{2,1,0:T(8,128)S(1)} collective-permute-done((f32[3,32,32]{2,1,0:T(8,128)S(1)}, f32[3,32,32]{2,1,0:T(8,128)S(1)}, u32[]{:S(2)}, u32[]{:S(2)}) %collective-permute-start.28) | collective-permute-done | bytes 12320 | tf_op jit(solution)/shard_map/ppermute | solution.py:314
  125.2 1.9 %collective-permute-done.27 = f32[3,32,32]{2,1,0:T(8,128)S(1)} collective-permute-done((f32[3,32,32]{2,1,0:T(8,128)S(1)}, f32[3,32,32]{2,1,0:T(8,128)S(1)}, u32[]{:S(2)}, u32[]{:S(2)}) %collective-permute-start.27) | collective-permute-done | bytes 12320 | tf_op jit(solution)/shard_map/ppermute | solution.py:314
  127.1 16.8 %shard_map.118 = (f32[32,2048]{1,0:T(8,128)}, f32[3,32,128]{2,1,0:T(8,128)}) custom-call(f32[2,32,32]{2,1,0:T(8,128)S(1)} %add_add_fusion.2.gram_ref.gram0_ref, f32[3,32,32]{2,1,0:T(8,128)S(1)} %add_add_fusion.gram1_ref, f32[32,32]{1,0:T(8,128)S(1)} %get-tuple-element.31.factor0_ref, f32[32,32]{1,0:T(8,128)S(1)} %get-tuple-element.32.factor1_ref, ...), custom_call_target="tpu_custom_call" | custom-call | tf_op jit(solution)/shard_map/pallas_call | solution.py:289
  (78 shorter events, 25.2 us)
Async XLA Ops:
  1.3 24.4 %collective-permute-start.9 = (bf16[256]{0:T(256)(128)(2,1)S(1)}, bf16[256]{0:T(256)(128)(2,1)S(1)}, u32[]{:S(2)}, u32[]{:S(2)}) collective-permute-start(bf16[256]{0:T(256)(128)(2,1)S(1)} %get-tuple-element.36), channel_id=1, source_target_pairs={{0,1},{1,2},{2,3},{3,4},{4,5},{5,6},{6,7},{7,8},{8,9},{9,10},{10,1... | collective-permute-start | bytes 1544 | tf_op jit(solution)/shard_map/ppermute | solution.py:344
  3.7 22.0 %collective-permute-start.10 = (bf16[256]{0:T(256)(128)(2,1)S(1)}, bf16[256]{0:T(256)(128)(2,1)S(1)}, u32[]{:S(2)}, u32[]{:S(2)}) collective-permute-start(bf16[256]{0:T(256)(128)(2,1)S(1)} %get-tuple-element.37), channel_id=1, source_target_pairs={{1,0},{2,1},{3,2},{4,3},{5,4},{6,5},{7,6},{8,7},{9,8},{10,9},{11,1... | collective-permute-start | bytes 1544 | tf_op jit(solution)/shard_map/ppermute | solution.py:345
  6.6 4.1 %collective-permute-start = (f32[32,32]{1,0:T(8,128)S(1)}, f32[32,32]{1,0:T(8,128)S(1)}, u32[]{:S(2)}, u32[]{:S(2)}) collective-permute-start(f32[32,32]{1,0:T(8,128)S(1)} %fusion.3), channel_id=1, source_target_pairs={{0,1},{1,0},{2,3},{3,2},{4,5},{5,4},{6,7},{7,6},{8,9},{9,8},{10,11... | collective-permute-start | bytes 12296 | tf_op jit(solution)/shard_map/ppermute | solution.py:314
  10.7 4.7 %collective-permute-start.3 = (f32[32,32]{1,0:T(8,128)S(1)}, f32[32,32]{1,0:T(8,128)S(1)}, u32[]{:S(2)}, u32[]{:S(2)}) collective-permute-start(f32[32,32]{1,0:T(8,128)S(1)} %add.63), channel_id=1, source_target_pairs={{0,6},{1,7},{2,4},{3,5},{4,2},{5,3},{6,0},{7,1},{8,14},{9,15},{10,... | collective-permute-start | bytes 12296 | tf_op jit(solution)/shard_map/ppermute | solution.py:314
  14.2 5.6 %collective-permute-start.1 = (f32[32,32]{1,0:T(8,128)S(1)}, f32[32,32]{1,0:T(8,128)S(1)}, u32[]{:S(2)}, u32[]{:S(2)}) collective-permute-start(f32[32,32]{1,0:T(8,128)S(1)} %add.63), channel_id=1, source_target_pairs={{0,2},{1,3},{2,0},{3,1},{4,6},{5,7},{6,4},{7,5},{8,10},{9,11},{10,... | collective-permute-start | bytes 12296 | tf_op jit(solution)/shard_map/ppermute | solution.py:314
  15.4 18.8 %collective-permute-start.8 = (f32[32,256]{1,0:T(8,128)S(1)}, f32[32,256]{1,0:T(8,128)S(1)}, u32[]{:S(2)}, u32[]{:S(2)}) collective-permute-start(f32[32,256]{1,0:T(8,128)S(1)} %get-tuple-element.34), channel_id=1, source_target_pairs={{1,0},{2,1},{3,2},{4,3},{5,4},{6,5},{7,6},{8,7},{9,8},{10,9},{11,1... | collective-permute-start | bytes 98312 | tf_op jit(solution)/shard_map/ppermute | solution.py:343
  17.4 16.8 %collective-permute-start.7 = (f32[32,256]{1,0:T(8,128)S(1)}, f32[32,256]{1,0:T(8,128)S(1)}, u32[]{:S(2)}, u32[]{:S(2)}) collective-permute-start(f32[32,256]{1,0:T(8,128)S(1)} %get-tuple-element.35), channel_id=1, source_target_pairs={{0,1},{1,2},{2,3},{3,4},{4,5},{5,6},{6,7},{7,8},{8,9},{9,10},{10,1... | collective-permute-start | bytes 98312 | tf_op jit(solution)/shard_map/ppermute | solution.py:342
  19.8 14.4 %collective-permute-start.6 = (f32[32,32]{1,0:T(8,128)S(1)}, f32[32,32]{1,0:T(8,128)S(1)}, u32[]{:S(2)}, u32[]{:S(2)}) collective-permute-start(f32[32,32]{1,0:T(8,128)S(1)} %add_add_fusion.5), channel_id=1, source_target_pairs={{0,24},{1,25},{2,26},{3,27},{4,28},{5,29},{6,30},{7,31},{8,16},{9,... | collective-permute-start | bytes 12296 | tf_op jit(solution)/shard_map/ppermute | solution.py:314
  25.7 8.4 %collective-permute-start.5 = (f32[32,32]{1,0:T(8,128)S(1)}, f32[32,32]{1,0:T(8,128)S(1)}, u32[]{:S(2)}, u32[]{:S(2)}) collective-permute-start(f32[32,32]{1,0:T(8,128)S(1)} %add_add_fusion.5), channel_id=1, source_target_pairs={{0,16},{1,17},{2,18},{3,19},{4,20},{5,21},{6,22},{7,23},{8,24},{9,... | collective-permute-start | bytes 12296 | tf_op jit(solution)/shard_map/ppermute | solution.py:314
  25.8 8.4 %collective-permute-start.4 = (f32[32,32]{1,0:T(8,128)S(1)}, f32[32,32]{1,0:T(8,128)S(1)}, u32[]{:S(2)}, u32[]{:S(2)}) collective-permute-start(f32[32,32]{1,0:T(8,128)S(1)} %add_add_fusion.5), channel_id=1, source_target_pairs={{0,8},{1,9},{2,10},{3,11},{4,12},{5,13},{6,14},{7,15},{8,0},{9,1},... | collective-permute-start | bytes 12296 | tf_op jit(solution)/shard_map/ppermute | solution.py:314
  63.4 7.4 %collective-permute-start.16 = (f32[2,32,32]{2,1,0:T(8,128)S(1)}, f32[2,32,32]{2,1,0:T(8,128)S(1)}, u32[]{:S(2)}, u32[]{:S(2)}) collective-permute-start(f32[2,32,32]{2,1,0:T(8,128)S(1)} %add.70), channel_id=1, source_target_pairs={{0,6},{1,7},{2,4},{3,5},{4,2},{5,3},{6,0},{7,1},{8,14},{9,15},{10,... | collective-permute-start | bytes 24584 | tf_op jit(solution)/shard_map/ppermute | solution.py:314
  68.8 3.9 %collective-permute-start.15 = (f32[2,32,32]{2,1,0:T(8,128)S(1)}, f32[2,32,32]{2,1,0:T(8,128)S(1)}, u32[]{:S(2)}, u32[]{:S(2)}) collective-permute-start(f32[2,32,32]{2,1,0:T(8,128)S(1)} %add.70), channel_id=1, source_target_pairs={{0,4},{1,5},{2,6},{3,7},{4,0},{5,1},{6,2},{7,3},{8,12},{9,13},{10,... | collective-permute-start | bytes 24584 | tf_op jit(solution)/shard_map/ppermute | solution.py:314
  68.8 3.9 %collective-permute-start.14 = (f32[2,32,32]{2,1,0:T(8,128)S(1)}, f32[2,32,32]{2,1,0:T(8,128)S(1)}, u32[]{:S(2)}, u32[]{:S(2)}) collective-permute-start(f32[2,32,32]{2,1,0:T(8,128)S(1)} %add.70), channel_id=1, source_target_pairs={{0,2},{1,3},{2,0},{3,1},{4,6},{5,7},{6,4},{7,5},{8,10},{9,11},{10,... | collective-permute-start | bytes 24584 | tf_op jit(solution)/shard_map/ppermute | solution.py:314
  72.8 5.9 %collective-permute-start.19 = (f32[2,32,32]{2,1,0:T(8,128)S(1)}, f32[2,32,32]{2,1,0:T(8,128)S(1)}, u32[]{:S(2)}, u32[]{:S(2)}) collective-permute-start(f32[2,32,32]{2,1,0:T(8,128)S(1)} %add_add_fusion.3), channel_id=1, source_target_pairs={{0,24},{1,25},{2,26},{3,27},{4,28},{5,29},{6,30},{7,31},{8,16},{9,... | collective-permute-start | bytes 24584 | tf_op jit(solution)/shard_map/ppermute | solution.py:314
  75.4 4.8 %collective-permute-start.18 = (f32[2,32,32]{2,1,0:T(8,128)S(1)}, f32[2,32,32]{2,1,0:T(8,128)S(1)}, u32[]{:S(2)}, u32[]{:S(2)}) collective-permute-start(f32[2,32,32]{2,1,0:T(8,128)S(1)} %add_add_fusion.3), channel_id=1, source_target_pairs={{0,16},{1,17},{2,18},{3,19},{4,20},{5,21},{6,22},{7,23},{8,24},{9,... | collective-permute-start | bytes 24584 | tf_op jit(solution)/shard_map/ppermute | solution.py:314
  75.8 4.4 %collective-permute-start.17 = (f32[2,32,32]{2,1,0:T(8,128)S(1)}, f32[2,32,32]{2,1,0:T(8,128)S(1)}, u32[]{:S(2)}, u32[]{:S(2)}) collective-permute-start(f32[2,32,32]{2,1,0:T(8,128)S(1)} %add_add_fusion.3), channel_id=1, source_target_pairs={{0,8},{1,9},{2,10},{3,11},{4,12},{5,13},{6,14},{7,15},{8,0},{9,1},... | collective-permute-start | bytes 24584 | tf_op jit(solution)/shard_map/ppermute | solution.py:314
  101.1 4.7 %collective-permute-start.21 = (f32[32,512]{1,0:T(8,128)S(1)}, f32[32,512]{1,0:T(8,128)S(1)}, u32[]{:S(2)}, u32[]{:S(2)}) collective-permute-start(f32[32,512]{1,0:T(8,128)S(1)} %get-tuple-element.29), channel_id=1, source_target_pairs={{1,0},{2,1},{3,2},{4,3},{5,4},{6,5},{7,6},{8,7},{9,8},{10,9},{11,1... | collective-permute-start | bytes 196616 | tf_op jit(solution)/shard_map/ppermute | solution.py:383
  107.1 3.8 %collective-permute-start.22 = (f32[3,32,32]{2,1,0:T(8,128)S(1)}, f32[3,32,32]{2,1,0:T(8,128)S(1)}, u32[]{:S(2)}, u32[]{:S(2)}) collective-permute-start(f32[3,32,32]{2,1,0:T(8,128)S(1)} %get-tuple-element.30), channel_id=1, source_target_pairs={{0,1},{1,0},{2,3},{3,2},{4,5},{5,4},{6,7},{7,6},{8,9},{9,8},{10,11... | collective-permute-start | bytes 36872 | tf_op jit(solution)/shard_map/ppermute | solution.py:314
  110.9 6.1 %collective-permute-start.25 = (f32[3,32,32]{2,1,0:T(8,128)S(1)}, f32[3,32,32]{2,1,0:T(8,128)S(1)}, u32[]{:S(2)}, u32[]{:S(2)}) collective-permute-start(f32[3,32,32]{2,1,0:T(8,128)S(1)} %add.77), channel_id=1, source_target_pairs={{0,6},{1,7},{2,4},{3,5},{4,2},{5,3},{6,0},{7,1},{8,14},{9,15},{10,... | collective-permute-start | bytes 36872 | tf_op jit(solution)/shard_map/ppermute | solution.py:314
  114.8 4.1 %collective-permute-start.24 = (f32[3,32,32]{2,1,0:T(8,128)S(1)}, f32[3,32,32]{2,1,0:T(8,128)S(1)}, u32[]{:S(2)}, u32[]{:S(2)}) collective-permute-start(f32[3,32,32]{2,1,0:T(8,128)S(1)} %add.77), channel_id=1, source_target_pairs={{0,4},{1,5},{2,6},{3,7},{4,0},{5,1},{6,2},{7,3},{8,12},{9,13},{10,... | collective-permute-start | bytes 36872 | tf_op jit(solution)/shard_map/ppermute | solution.py:314
  115.0 4.1 %collective-permute-start.23 = (f32[3,32,32]{2,1,0:T(8,128)S(1)}, f32[3,32,32]{2,1,0:T(8,128)S(1)}, u32[]{:S(2)}, u32[]{:S(2)}) collective-permute-start(f32[3,32,32]{2,1,0:T(8,128)S(1)} %add.77), channel_id=1, source_target_pairs={{0,2},{1,3},{2,0},{3,1},{4,6},{5,7},{6,4},{7,5},{8,10},{9,11},{10,... | collective-permute-start | bytes 36872 | tf_op jit(solution)/shard_map/ppermute | solution.py:314
  119.2 6.1 %collective-permute-start.28 = (f32[3,32,32]{2,1,0:T(8,128)S(1)}, f32[3,32,32]{2,1,0:T(8,128)S(1)}, u32[]{:S(2)}, u32[]{:S(2)}) collective-permute-start(f32[3,32,32]{2,1,0:T(8,128)S(1)} %add_add_fusion.1), channel_id=1, source_target_pairs={{0,24},{1,25},{2,26},{3,27},{4,28},{5,29},{6,30},{7,31},{8,16},{9,... | collective-permute-start | bytes 36872 | tf_op jit(solution)/shard_map/ppermute | solution.py:314
  122.1 5.0 %collective-permute-start.27 = (f32[3,32,32]{2,1,0:T(8,128)S(1)}, f32[3,32,32]{2,1,0:T(8,128)S(1)}, u32[]{:S(2)}, u32[]{:S(2)}) collective-permute-start(f32[3,32,32]{2,1,0:T(8,128)S(1)} %add_add_fusion.1), channel_id=1, source_target_pairs={{0,16},{1,17},{2,18},{3,19},{4,20},{5,21},{6,22},{7,23},{8,24},{9,... | collective-permute-start | bytes 36872 | tf_op jit(solution)/shard_map/ppermute | solution.py:314
  122.1 4.9 %collective-permute-start.26 = (f32[3,32,32]{2,1,0:T(8,128)S(1)}, f32[3,32,32]{2,1,0:T(8,128)S(1)}, u32[]{:S(2)}, u32[]{:S(2)}) collective-permute-start(f32[3,32,32]{2,1,0:T(8,128)S(1)} %add_add_fusion.1), channel_id=1, source_target_pairs={{0,8},{1,9},{2,10},{3,11},{4,12},{5,13},{6,14},{7,15},{8,0},{9,1},... | collective-permute-start | bytes 36872 | tf_op jit(solution)/shard_map/ppermute | solution.py:314
  (15 other events, 82.5 us)

commit v2 on v1

v2 whole, which is shorter than its diff:
```python
import jax
import jax.numpy as jnp
from jax import lax
from jax.experimental import pallas as pl
from jax.experimental.pallas import tpu as pltpu
from jax.sharding import PartitionSpec as P

CHUNK = 16
PIVOTS = 4
VMEM_LIMIT = 48 * 1024 * 1024
AXIS = "brick"
F32 = jnp.float32
BF16 = jnp.bfloat16
NN = (((1,), (0,)), ((), ()))
NT = (((1,), (1,)), ((), ()))
TN = (((0,), (0,)), ((), ()))


def fdot(a, b, dims=NN):
    return lax.dot_general(a, b, dims, precision=lax.Precision.HIGHEST, preferred_element_type=F32)


def bdot(a, b, dims=NN):
    return lax.dot_general(a, b, dims, preferred_element_type=F32)


def lower_inverse(gram):
    n = gram.shape[0]
    row_id = lax.broadcasted_iota(jnp.int32, (n, n), 0)
    col_id = lax.broadcasted_iota(jnp.int32, (n, n), 1)
    work, side = gram, jnp.where(row_id == col_id, 1.0, 0.0).astype(F32)
    for first in range(0, n, PIVOTS):
        places = range(first, first + PIVOTS)
        cols = [jnp.broadcast_to(work[:, k : k + 1], (n, n)) for k in places]
        rows = [work[k : k + 1, :] for k in places]
        sides = [side[k : k + 1, :] for k in places]
        for j, k in enumerate(places):
            step = jnp.where(row_id > k, cols[j] * (1.0 / cols[j][k : k + 1, :]), 0.0)
            for m in range(j + 1, PIVOTS):
                at = first + m
                cols[m] = cols[m] - step * cols[j][at : at + 1, :]
                rows[m] = rows[m] - step[at : at + 1, :] * rows[j]
                sides[m] = sides[m] - step[at : at + 1, :] * sides[j]
            work = work - step * rows[j]
            side = side - step * sides[j]
    diag = jnp.sum(jnp.where(row_id == col_id, work, 0.0), axis=1, keepdims=True)
    scale = 1.0 / jnp.sqrt(diag)
    return side * scale, jnp.where(col_id >= row_id, work, 0.0) * scale


def packed(square):
    n = square.shape[0]
    fold = 128 // n
    part = n // fold
    return jnp.concatenate([square[j * part : (j + 1) * part, :] for j in range(fold)], axis=1)


def unpacked(tile):
    n = int((tile.shape[0] * 128) ** 0.5)
    fold = 128 // n
    return jnp.concatenate([tile[:, j * n : (j + 1) * n] for j in range(fold)], axis=0)


def tall(row, count):
    return jnp.broadcast_to(row, (count, row.shape[1])).astype(BF16)


def one_hot(lo_rows, depth):
    slots = lo_rows.shape[1]
    place = lax.broadcasted_iota(jnp.int32, (depth, slots), 0).astype(F32).astype(BF16)
    one, zero = jnp.ones((), BF16), jnp.zeros((), BF16)
    return jnp.concatenate(
        [
            jnp.where(place == tall(lo_rows[e : e + 1, :], depth), one, zero)
            for e in range(lo_rows.shape[0])
        ],
        axis=1,
    )


def apply_elements(
    half, conn_ref, owner_ref, coeff_ref, stacked_ref, values_ref, tiles_ref, total_ref,
    state=None, state_ref=None,
):
    rows, width = half.shape
    depth = owner_ref.shape[1]
    count = width // depth
    elems, slots = conn_ref.shape
    owner = owner_ref[...].astype(F32)
    below, above = one_hot(owner[0:1, :], depth), one_hot(owner[1:2, :], depth)
    tiles_ref[:rows, :] = bdot(half[:, :depth], below).astype(BF16)
    for h in range(1, count - 1):
        tiles_ref[h * rows : (h + 1) * rows, :] = half[:, h * depth : (h + 1) * depth]
    tiles_ref[(count - 1) * rows : count * rows, :] = bdot(half[:, width - depth :], above).astype(BF16)
    if state is not None:
        extra = tiles_ref.shape[0] - count * rows
        pieces = [state[:, h * depth : (h + 1) * depth] for h in range(count)]
        pieces[0] = bdot(tall(pieces[0], 16), below)[0:1, :]
        pieces[-1] = bdot(tall(pieces[-1], 16), above)[0:1, :]
        pieces.append(jnp.zeros((extra - count, depth), F32))
        tiles_ref[count * rows :, :] = jnp.concatenate(pieces, axis=0).astype(BF16)
    total_ref[...] = jnp.zeros_like(total_ref)
    zero = jnp.zeros((), BF16)

    def chunk(step, carry):
        start = pl.multiple_of(step * CHUNK, CHUNK)
        conn = conn_ref[pl.ds(start, CHUNK), :]
        hi = lax.div(conn, depth)
        hot = one_hot((conn - hi * depth).astype(F32), depth)
        spread = bdot(tiles_ref[...], hot)
        hi_wide = [tall(hi[e : e + 1, :].astype(F32), rows) for e in range(CHUNK)]
        scaled = []
        for e in range(CHUNK):
            here = slice(e * slots, (e + 1) * slots)
            value = spread[:rows, here]
            for h in range(1, count):
                value = jnp.where(
                    hi[e : e + 1, :] == h, spread[h * rows : (h + 1) * rows, here], value
                )
            values_ref[pl.ds(pl.multiple_of((start + e) * rows, rows), rows), :] = value.astype(BF16)
            scaled.append(
                jnp.concatenate(
                    [(value * coeff_ref[k, start + e]).astype(BF16) for k in range(3)], axis=1
                )
            )
            if state is not None:
                picked = spread[count * rows :, here]
                match = lax.broadcasted_iota(jnp.int32, picked.shape, 0) == hi[e : e + 1, :]
                state_ref[pl.ds(start + e, 1), :] = jnp.sum(
                    jnp.where(match, picked, 0.0), axis=0, keepdims=True
                )
        result = bdot(jnp.concatenate(scaled, axis=0), stacked_ref[...]).astype(BF16)
        masked = jnp.concatenate(
            [
                jnp.concatenate(
                    [
                        jnp.where(
                            hi_wide[e] == jnp.full((), h, BF16),
                            result[e * rows : (e + 1) * rows, :],
                            zero,
                        )
                        for e in range(CHUNK)
                    ],
                    axis=1,
                )
                for h in range(count)
            ],
            axis=0,
        )
        total_ref[...] += bdot(masked, hot, NT)
        return carry

    lax.fori_loop(0, elems // CHUNK, chunk, 0, unroll=True)
    parts = [total_ref[h * rows : (h + 1) * rows, :] for h in range(count)]
    for at, match in ((0, below), (count - 1, above)):
        top = parts[at].astype(BF16)
        rest = (parts[at] - top.astype(F32)).astype(BF16)
        both = bdot(jnp.concatenate([top, rest], axis=0), match, NT)
        parts[at] = both[:rows] + both[rows:]
    return parts


def send_bands(low, high, a_ref, b_ref):
    odd = lax.axis_index(AXIS) % 2 == 1
    a_ref[...] = jnp.where(odd, low, high)
    b_ref[...] = jnp.where(odd, high, low)


def received_bands(a_ref, b_ref):
    odd = lax.axis_index(AXIS) % 2 == 1
    a, b = a_ref[...], b_ref[...]
    return jnp.where(odd, a, b), jnp.where(odd, b, a)


def write_image(basis, parts, diag_ref, image_ref, a_ref, b_ref):
    rows, width = basis.shape
    depth = parts[0].shape[1]
    me = lax.axis_index(AXIS)
    low = parts[0] * jnp.where(me == 0, 0.0, 1.0)
    high = parts[-1] * jnp.where(me == lax.axis_size(AXIS) - 1, 0.0, 1.0)
    own = [
        diag_ref[:, (h - 1) * depth : h * depth] * basis[:, h * depth : (h + 1) * depth] + parts[h]
        for h in range(1, len(parts) - 1)
    ]
    image_ref[...] = jnp.concatenate([low] + own + [high], axis=1)
    send_bands(
        jnp.concatenate([own[0], low], axis=1), jnp.concatenate([own[-1], high], axis=1), a_ref, b_ref
    )


def complete(image_ref, a_ref, b_ref):
    depth = a_ref.shape[1] // 2
    width = image_ref.shape[1]
    low, high = received_bands(a_ref, b_ref)
    return jnp.concatenate(
        [
            image_ref[:, : 2 * depth] + low,
            image_ref[:, 2 * depth : width - 2 * depth],
            image_ref[:, width - 2 * depth :] + jnp.concatenate([high[:, depth:], high[:, :depth]], axis=1),
        ],
        axis=1,
    )


def begin_kernel(
    sens_ref, disp_ref, normal_ref, shear_ref, friction_ref, slip_ref, gram_ref, a_ref, b_ref, coeff_ref
):
    sens = sens_ref[...]
    depth = a_ref.shape[1]
    owned = sens.shape[1]
    gram = packed(fdot(sens, sens, NT))
    gram_ref[...] = jnp.broadcast_to(gram[None], gram_ref.shape)
    spare = jnp.zeros((a_ref.shape[0] - sens.shape[0] - 1, depth), F32)
    disp = disp_ref[...].astype(F32)
    low = jnp.concatenate([sens[:, :depth], disp[:, :depth], spare], axis=0)
    high = jnp.concatenate([sens[:, owned - depth :], disp[:, owned - depth :], spare], axis=0)
    send_bands(low, high, a_ref, b_ref)
    coeff_ref[0:1, :] = normal_ref[...]
    coeff_ref[1:2, :] = shear_ref[...]
    coeff_ref[2:3, :] = slip_ref[...].astype(F32) * friction_ref[...] * normal_ref[...]


def first_kernel(
    gram_ref, sens_ref, disp_ref, a_in, b_in, diag_ref, conn_ref, owner_ref, coeff_ref, stacked_ref,
    basis_ref, image_ref, a_ref, b_ref, factor_ref, values_ref, push_ref,
    tiles_ref, total_ref, state_ref,
):
    rows = sens_ref.shape[0]
    slots = conn_ref.shape[1]
    elems = conn_ref.shape[0]
    inverse, factor = lower_inverse(unpacked(jnp.sum(gram_ref[...], axis=0)))
    factor_ref[...] = factor
    low, high = received_bands(a_in, b_in)
    basis = fdot(inverse, jnp.concatenate([low[:rows], sens_ref[...], high[:rows]], axis=1))
    basis_ref[...] = basis
    state = jnp.concatenate(
        [low[rows : rows + 1], disp_ref[...].astype(F32), high[rows : rows + 1]], axis=1
    )
    parts = apply_elements(
        basis.astype(BF16), conn_ref, owner_ref, coeff_ref, stacked_ref, values_ref, tiles_ref,
        total_ref, state, state_ref,
    )
    write_image(basis, parts, diag_ref, image_ref, a_ref, b_ref)
    moved = state_ref[...].astype(BF16)
    for k in range(3):
        push_ref[:, k * elems : (k + 1) * elems] = bdot(
            stacked_ref[k * slots : (k + 1) * slots, :], moved, NT
        ).astype(BF16)


def own_part(field, depth):
    return field[:, depth : field.shape[1] - depth]


def middle_kernel(basis_ref, image_ref, a_in, b_in, full_ref, gram_ref):
    depth = a_in.shape[1] // 2
    full = complete(image_ref, a_in, b_in)
    full_ref[...] = full
    own = own_part(full, depth)
    rows = own.shape[0]
    both = fdot(jnp.concatenate([own_part(basis_ref[...], depth), own], axis=0), own, NT)
    tile = jnp.concatenate([packed(both[:rows]), packed(both[rows:])], axis=0)
    gram_ref[...] = jnp.broadcast_to(tile[None], gram_ref.shape)


def second_kernel(
    gram_ref, factor0_ref, basis0_ref, full_ref, diag_ref, conn_ref, owner_ref, coeff_ref, stacked_ref,
    basis_ref, image_ref, a_ref, b_ref, small_ref, values_ref, tiles_ref, total_ref,
):
    tile = jnp.sum(gram_ref[...], axis=0)
    part = tile.shape[0] // 2
    proj, square = unpacked(tile[:part]), unpacked(tile[part:])
    inverse, factor = lower_inverse(square - fdot(proj, proj, TN))
    head, unused = lower_inverse(square)
    reduced = full_ref[...] - fdot(proj, basis0_ref[...], TN)
    basis = fdot(inverse, reduced)
    basis_ref[...] = basis
    small_ref[0] = head
    small_ref[1] = fdot(head, proj, NT)
    small_ref[2] = fdot(head, factor, NT)
    small_ref[3] = fdot(head, fdot(proj, factor0_ref[...], TN))
    parts = apply_elements(
        basis.astype(BF16), conn_ref, owner_ref, coeff_ref, stacked_ref, values_ref, tiles_ref, total_ref
    )
    write_image(basis, parts, diag_ref, image_ref, a_ref, b_ref)


def late_kernel(basis0_ref, basis1_ref, image_ref, a_in, b_in, gram_ref):
    depth = a_in.shape[1] // 2
    own = own_part(complete(image_ref, a_in, b_in), depth)
    rows = own.shape[0]
    every = fdot(
        jnp.concatenate(
            [own_part(basis0_ref[...], depth), own_part(basis1_ref[...], depth), own], axis=0
        ),
        own,
        NT,
    )
    gram_ref[...] = jnp.concatenate(
        [packed(every[j * rows : (j + 1) * rows]) for j in range(3)], axis=0
    )


def split3(value):
    first = value.astype(BF16)
    rest = value - first.astype(F32)
    second = rest.astype(BF16)
    return jnp.concatenate([first, second, (rest - second.astype(F32)).astype(BF16)], axis=0)


def last_kernel(
    gram_ref, factor0_ref, small_ref, basis0_ref, basis1_ref, values0_ref, values1_ref, push_ref,
    normal_ref, friction_ref, slip_ref, adjoint_ref, grads_ref, pairs_ref,
):
    rows, width = basis0_ref.shape
    depth = (width - adjoint_ref.shape[1]) // 2
    elems = normal_ref.shape[1]
    slots = values0_ref.shape[1]
    part = gram_ref.shape[0] // 3
    p01, p11, n11 = (unpacked(gram_ref[j * part : (j + 1) * part, :]) for j in range(3))
    upper0 = factor0_ref[...]
    head, head_side = small_ref[0], small_ref[3]
    cross = fdot(small_ref[1], p01) + fdot(small_ref[2], p11)
    tail, unused = lower_inverse(n11 - fdot(cross, cross, TN))
    tail_side = fdot(tail, fdot(p01, upper0, TN) - fdot(cross, head_side, TN))
    w1 = fdot(tail, tail_side, TN)
    turned = jnp.concatenate(
        [fdot(head_side - fdot(cross, w1), head, TN), fdot(tail_side, tail, TN)], axis=1
    )
    adjoint_ref[...] = fdot(
        turned,
        jnp.concatenate(
            [own_part(basis0_ref[...], depth), own_part(basis1_ref[...], depth)], axis=0
        ),
    )
    weights = split3(turned)
    pairs_ref[...] = jnp.zeros_like(pairs_ref)
    lane = lax.broadcasted_iota(jnp.int32, (rows, 3 * elems), 1) % elems

    def chunk(step, carry):
        start = pl.multiple_of(step * CHUNK, CHUNK)
        fields = []
        for ref in (values0_ref, values1_ref):
            block = ref[pl.ds(pl.multiple_of(start * rows, rows), CHUNK * rows), :]
            fields.append(
                jnp.concatenate([block[e * rows : (e + 1) * rows, :] for e in range(CHUNK)], axis=1)
            )
        mixed = bdot(weights, jnp.concatenate(fields, axis=0))
        mixed = (mixed[:rows] + (mixed[rows : 2 * rows] + mixed[2 * rows :])).astype(BF16)
        every = bdot(
            jnp.concatenate([mixed[:, e * slots : (e + 1) * slots] for e in range(CHUNK)], axis=0),
            push_ref[...],
        )
        pairs = pairs_ref[...]
        for e in range(CHUNK):
            pairs = jnp.where(lane == start + e, every[e * rows : (e + 1) * rows, :], pairs)
        pairs_ref[...] = pairs
        return carry

    lax.fori_loop(0, elems // CHUNK, chunk, 0, unroll=True)
    third = pairs_ref[:, 2 * elems :]
    slip = slip_ref[...].astype(F32)
    grads_ref[0] = -(pairs_ref[:, :elems] + slip * friction_ref[...] * third)
    grads_ref[1] = -pairs_ref[:, elems : 2 * elems]
    grads_ref[2] = -slip * normal_ref[...] * third


def call(kernel, outs, scratch, args, smem=()):
    return pl.pallas_call(
        kernel,
        out_shape=[jax.ShapeDtypeStruct(shape, dtype) for shape, dtype in outs],
        in_specs=[
            pl.BlockSpec(memory_space=pltpu.SMEM if i in smem else pltpu.VMEM)
            for i in range(len(args))
        ],
        out_specs=[pl.BlockSpec(memory_space=pltpu.VMEM) for unused in outs],
        scratch_shapes=[pltpu.VMEM(shape, dtype) for shape, dtype in scratch],
        compiler_params=pltpu.CompilerParams(vmem_limit_bytes=VMEM_LIMIT),
    )(*args)


def exchanged(a, b):
    count = lax.axis_size(AXIS)
    first = [(i, i ^ 1) for i in range(count) if i ^ 1 < count]
    other = [(i, i + 1 if i % 2 else i - 1) for i in range(count)]
    second = [(i, j) for i, j in other if 0 <= j < count]
    return lax.ppermute(a, AXIS, first), lax.ppermute(b, AXIS, second)


def everyones(copies):
    return lax.all_to_all(copies, AXIS, 0, 0, tiled=True)


def total(value):
    count = lax.axis_size(AXIS)
    stride = 1
    while stride < count:
        left = count // stride
        radix = 2 if stride == 1 or left % 4 else 4
        parts = [value]
        for d in range(1, radix):
            route = []
            for i in range(count):
                digit = (i // stride) % radix
                route.append((i, i + ((digit ^ d) - digit) * stride))
            parts.append(lax.ppermute(value, AXIS, route))
        while len(parts) > 1:
            parts = [parts[2 * i] + parts[2 * i + 1] for i in range(len(parts) // 2)]
        value = parts[0]
        stride *= radix
    return value


def on_device(
    sensitivity, diagonal, displacement, connectivity, normal_stiff, shear_stiff, friction, slip_state,
    owner_map, templates,
):
    devices = lax.axis_size(AXIS)
    rows, owned = sensitivity.shape
    depth = owner_map.shape[2]
    elems, slots = connectivity.shape
    width = owned + 2 * depth
    count = width // depth
    part = rows * rows // 128
    extra = -(-count // 16) * 16
    wide = ((rows, width), F32)
    band = ((rows, 2 * depth), F32)
    picked = ((elems * rows, slots), BF16)

    line = lambda array: array[None, :]
    disp, diag = line(displacement), line(diagonal)
    normal, shear, fric, slip = line(normal_stiff), line(shear_stiff), line(friction), line(slip_state)
    owner = owner_map[0]
    stacked = templates.reshape(3 * slots, slots)

    start_band = ((rows + 8, depth), F32)
    gram, a, b, coeffs = call(
        begin_kernel,
        [((devices, part, 128), F32), start_band, start_band, ((3, elems), F32)],
        [],
        [sensitivity, disp, normal, shear, fric, slip],
    )
    a, b = exchanged(a, b)
    gram = everyones(gram)
    basis0, image, a, b, factor0, values0, pushed = call(
        first_kernel,
        [wide, wide, band, band, ((rows, rows), F32), picked, ((slots, 3 * elems), BF16)],
        [((count * rows + extra, depth), BF16), ((count * rows, depth), F32), ((elems, slots), F32)],
        [gram, sensitivity, disp, a, b, diag, connectivity, owner, coeffs, stacked],
        smem=(8,),
    )
    a, b = exchanged(a, b)
    full, gram = call(
        middle_kernel, [wide, ((devices, 2 * part, 128), F32)], [], [basis0, image, a, b]
    )
    gram = everyones(gram)
    basis1, image, a, b, small, values1 = call(
        second_kernel,
        [wide, wide, band, band, ((4, rows, rows), F32), picked],
        [((count * rows, depth), BF16), ((count * rows, depth), F32)],
        [gram, factor0, basis0, full, diag, connectivity, owner, coeffs, stacked],
        smem=(7,),
    )
    a, b = exchanged(a, b)
    gram = call(late_kernel, [((3 * part, 128), F32)], [], [basis0, basis1, image, a, b])[0]
    gram = total(gram)
    adjoint, grads = call(
        last_kernel,
        [((rows, owned), F32), ((3, rows, elems), F32)],
        [((rows, 3 * elems), F32)],
        [gram, factor0, small, basis0, basis1, values0, values1, pushed, normal, fric, slip],
    )
    return adjoint, grads


def solution(mesh):
    in_specs = (
        P(None, "brick"),
        P("brick"),
        P("brick"),
        P("brick", None),
        P("brick"),
        P("brick"),
        P("brick"),
        P("brick"),
        P("brick", None, None),
        P(),
    )
    out_specs = (P(None, "brick"), P(None, None, "brick"))
    return jax.shard_map(
        on_device, mesh=mesh, in_specs=in_specs, out_specs=out_specs, check_vma=False
    )
```

time: 144 us -> 91 us (0.63)
  Pallas kernels: 64.6 us -> 29.7 us
  starting transfers between devices: 52.6 us -> 23.3 us
  blocking collectives: 0 us -> 20.5 us
  waiting for transfers between devices: 21.5 us -> 13.4 us
    ppermute x29 -> x13, starting transfers between devices: 52.6 us -> 16 us  [the longest x7 13.2 us: total(): parts.append(lax.ppermute(value, AXIS, route))]
    pallas_call x6, Pallas kernels: 64.6 us -> 29.7 us  [call(): pl.pallas_call(kernel, out_shape=[jax.ShapeDtypeStruct(shape, dtype) for...]
    all_to_all x0 -> x1, blocking collectives: none -> 20.5 us  [everyones(): return lax.all_to_all(copies, AXIS, 0, 0, tiled=True)]
    ppermute x29 -> x13, waiting for transfers between devices: 21.5 us -> 6.46 us  [the longest x7 5.42 us: total(): parts.append(lax.ppermute(value, AXIS, route))]
    all_to_all x0 -> x1, starting transfers between devices: none -> 7.3 us  [everyones(): return lax.all_to_all(copies, AXIS, 0, 0, tiled=True)]
    all_to_all x0 -> x1, waiting for transfers between devices: none -> 6.93 us  [everyones(): return lax.all_to_all(copies, AXIS, 0, 0, tiled=True)]
  transfers between devices with their start and end apart: 29 -> 14, of which waited for: 16 -> 10; matrix products, arithmetic and copies ran while one was open for 1% -> 0% of each run, Pallas kernels for 5% -> 0%
where the time goes in v2:
time: 91 us; the launch traced here: 90.6 us
  Pallas kernels  29.7 us (33%)
  starting transfers between devices  23.3 us (26%)
  blocking collectives  20.5 us (23%)
  waiting for transfers between devices  13.4 us (15%)
  local copies, waits for them, and re-layouts  3 us (3%)
    pallas_call x6, Pallas kernels, call(): pl.pallas_call(kernel, out_shape=[jax.ShapeDtypeStruct(shape, dtype) for...  29.7 us
    all_to_all x1, blocking collectives, everyones(): return lax.all_to_all(copies, AXIS, 0, 0, tiled=True)  20.5 us
    ppermute x7, starting transfers between devices, total(): parts.append(lax.ppermute(value, AXIS, route))  13.2 us
    all_to_all x1, starting transfers between devices, everyones(): return lax.all_to_all(copies, AXIS, 0, 0, tiled=True)  7.3 us
    all_to_all x1, waiting for transfers between devices, everyones(): return lax.all_to_all(copies, AXIS, 0, 0, tiled=True)  6.93 us
    ppermute x7, waiting for transfers between devices, total(): parts.append(lax.ppermute(value, AXIS, route))  5.42 us
    ppermute x6, starting transfers between devices, exchanged(): return (lax.ppermute(a, AXIS, first), lax.ppermute(b, AXIS, second))  2.86 us
    unnamed x20, local copies, waits for them, and re-layouts  2.31 us
  transfers between devices with their start and end apart: 14, of which 10 were waited for; matrix products, arithmetic and copies ran while one was open for 0% of the time, Pallas kernels for 0%

profile of v2, /device:TPU:0, one launch (start us, length us, event | category | flops | bytes accessed | tf_op | source)
XLA Modules:
  0.0 90.6 jit_solution(9698665507973885770)
XLA Ops:
  0.6 0.7 broadcast_in_dim.18.disp_ref
  2.0 0.9 %copy-done = f32[32,2048]{1,0:T(8,128)S(1)} copy-done((f32[32,2048]{1,0:T(8,128)S(1)}, f32[32,2048]{1,0:T(8,128)}, u32[]{:S(2)}) %copy-start) | copy-done | bytes 262168
  3.0 1.1 %shard_map.113 = (f32[32,8,128]{2,1,0:T(8,128)}, f32[40,256]{1,0:T(8,128)S(1)}, f32[40,256]{1,0:T(8,128)S(1)}, f32[3,128]{1,0:T(4,128)S(1)}) custom-call(f32[32,2048]{1,0:T(8,128)S(1)} %copy-done, bf16[1,2048]{1,0:T(2,128)(2,1)S(1)} %broadcast_in_dim.18.disp_ref, f32[1,128]{1,0:T(1,128)S(1)} %bitcast.13, f32[1,128]{1,0:T(1,128)S(1)} %bitcast.19, ...), custom_call_target="tpu_custom_call" | custom-call | tf_op jit(solution)/shard_map/pallas_call | solution.py:369
  4.1 7.3 %all-to-all-start = ((f32[32,8,128]{2,1,0:T(8,128)}), f32[32,8,128]{2,1,0:T(8,128)S(1)}, u32[]{:S(2)}, u32[]{:S(2)}) async-start(f32[32,8,128]{2,1,0:T(8,128)} %get-tuple-element.21), calls=%async_computation | async-start | bytes 262144 | tf_op jit(solution)/shard_map/all_to_all | solution.py:391
  11.7 0.7 collective-permute-start.1
  12.7 6.9 %all-to-all-done.gram_ref = f32[32,8,128]{2,1,0:T(8,128)S(1)} async-done(((f32[32,8,128]{2,1,0:T(8,128)}), f32[32,8,128]{2,1,0:T(8,128)S(1)}, u32[]{:S(2)}, u32[]{:S(2)}) %all-to-all-start) | async-done | bytes 131104 | tf_op jit(solution)/shard_map/all_to_all | solution.py:391
  19.6 0.7 copy-done.5
  20.3 10.2 %shard_map.114 = (f32[32,2560]{1,0:T(8,128)S(1)}, f32[32,2560]{1,0:T(8,128)S(1)}, f32[32,512]{1,0:T(8,128)S(1)}, f32[32,512]{1,0:T(8,128)S(1)}, f32[32,32]{1,0:T...) custom-call(f32[32,8,128]{2,1,0:T(8,128)S(1)} %all-to-all-done.gram_ref, ...), custom_call_target="tpu_custom_call" | custom-call | tf_op jit(solution)/shard_map/pallas_call | solution.py:369
  30.8 0.7 collective-permute-start.3
  32.5 20.5 %all_to_all.10.gram_ref = f32[32,16,128]{2,1,0:T(8,128)S(1)} all-to-all(f32[32,16,128]{2,1,0:T(8,128)S(1)} %get-tuple-element.29), channel_id=1, replica_groups=mesh['brick'=32] {'brick'}, dimensions={0} | all-to-all | bytes 524288 | tf_op jit(solution)/shard_map/all_to_all | solution.py:391
  52.9 11.1 %shard_map.116 = (f32[32,2560]{1,0:T(8,128)S(1)}, f32[32,2560]{1,0:T(8,128)S(1)}, f32[32,512]{1,0:T(8,128)S(1)}, f32[32,512]{1,0:T(8,128)S(1)}, f32[4,32,32]{2,1,0:T(8,128)S(1)}, /*index=5*/bf16[4096,128]{1,0:T(8,128)(2,1)S(1)}) custom-call(f32[32,16,128]{2,1,0:T(8,128)S(1)} %all_to_all.10.gram_ref, f32[32,32]{1,0:T(8,128)S(1)} %get-tuple-element.30.factor0_ref, ...), custom_call_target="tpu_custom_call" | custom-call | tf_op jit(solution)/shard_map/pallas_call | solution.py:369
  64.1 0.9 collective-permute-start.5
  65.4 0.8 shard_map.117
  66.2 5.2 %collective-permute-start.6 = (f32[24,128]{1,0:T(8,128)S(1)}, f32[24,128]{1,0:T(8,128)S(1)}, u32[]{:S(2)}, u32[]{:S(2)}) collective-permute-start(f32[24,128]{1,0:T(8,128)S(1)} %shard_map.117), channel_id=1, source_target_pairs={{0,1},{1,0},{2,3},{3,2},{4,5},{5,4},{6,7},{7,6},{8,9},{9,8},{10,11... | collective-permute-start | bytes 36872 | tf_op jit(solution)/shard_map/ppermute | solution.py:406
  71.4 0.8 collective-permute-done.6
  72.3 2.6 %collective-permute-start.9 = (f32[24,128]{1,0:T(8,128)S(1)}, f32[24,128]{1,0:T(8,128)S(1)}, u32[]{:S(2)}, u32[]{:S(2)}) collective-permute-start(f32[24,128]{1,0:T(8,128)S(1)} %add.21), channel_id=1, source_target_pairs={{0,6},{1,7},{2,4},{3,5},{4,2},{5,3},{6,0},{7,1},{8,14},{9,15},{10,... | collective-permute-start | bytes 36872 | tf_op jit(solution)/shard_map/ppermute | solution.py:406
  74.9 0.9 collective-permute-start.7
  75.8 1.1 %collective-permute-done.9 = f32[24,128]{1,0:T(8,128)S(1)} collective-permute-done((f32[24,128]{1,0:T(8,128)S(1)}, f32[24,128]{1,0:T(8,128)S(1)}, u32[]{:S(2)}, u32[]{:S(2)}) %collective-permute-start.9) | collective-permute-done | bytes 12320 | tf_op jit(solution)/shard_map/ppermute | solution.py:406
  76.9 1.7 %collective-permute-done.8 = f32[24,128]{1,0:T(8,128)S(1)} collective-permute-done((f32[24,128]{1,0:T(8,128)S(1)}, f32[24,128]{1,0:T(8,128)S(1)}, u32[]{:S(2)}, u32[]{:S(2)}) %collective-permute-start.8) | collective-permute-done | bytes 12320 | tf_op jit(solution)/shard_map/ppermute | solution.py:406
  78.6 1.5 %collective-permute-start.12 = (f32[24,128]{1,0:T(8,128)S(1)}, f32[24,128]{1,0:T(8,128)S(1)}, u32[]{:S(2)}, u32[]{:S(2)}) collective-permute-start(f32[24,128]{1,0:T(8,128)S(1)} %add_add_fusion.1), channel_id=1, source_target_pairs={{0,24},{1,25},{2,26},{3,27},{4,28},{5,29},{6,30},{7,31},{8,16},{9,... | collective-permute-start | bytes 36872 | tf_op jit(solution)/shard_map/ppermute | solution.py:406
  80.1 1.0 %collective-permute-start.11 = (f32[24,128]{1,0:T(8,128)S(1)}, f32[24,128]{1,0:T(8,128)S(1)}, u32[]{:S(2)}, u32[]{:S(2)}) collective-permute-start(f32[24,128]{1,0:T(8,128)S(1)} %add_add_fusion.1), channel_id=1, source_target_pairs={{0,16},{1,17},{2,18},{3,19},{4,20},{5,21},{6,22},{7,23},{8,24},{9,... | collective-permute-start | bytes 36872 | tf_op jit(solution)/shard_map/ppermute | solution.py:406
  81.1 1.9 %collective-permute-start.10 = (f32[24,128]{1,0:T(8,128)S(1)}, f32[24,128]{1,0:T(8,128)S(1)}, u32[]{:S(2)}, u32[]{:S(2)}) collective-permute-start(f32[24,128]{1,0:T(8,128)S(1)} %add_add_fusion.1), channel_id=1, source_target_pairs={{0,8},{1,9},{2,10},{3,11},{4,12},{5,13},{6,14},{7,15},{8,0},{9,1},... | collective-permute-start | bytes 36872 | tf_op jit(solution)/shard_map/ppermute | solution.py:406
  83.0 1.1 %collective-permute-done.12 = f32[24,128]{1,0:T(8,128)S(1)} collective-permute-done((f32[24,128]{1,0:T(8,128)S(1)}, f32[24,128]{1,0:T(8,128)S(1)}, u32[]{:S(2)}, u32[]{:S(2)}) %collective-permute-start.12) | collective-permute-done | bytes 12320 | tf_op jit(solution)/shard_map/ppermute | solution.py:406
  84.8 5.8 %shard_map.118 = (f32[32,2048]{1,0:T(8,128)}, f32[3,32,128]{2,1,0:T(8,128)}) custom-call(f32[24,128]{1,0:T(8,128)S(1)} %add_add_fusion.gram_ref, f32[32,32]{1,0:T(8,128)S(1)} %get-tuple-element.30.factor0_ref, f32[4,32,32]{2,1,0:T(8,128)S(1)} %get-tuple-element.36.small_ref, f32[32,2560]{1,0:T(8,128)S(1)} %get-tuple-element.25.basis_ref.basis0_ref, ...), custom_call_target="tpu_custom_call" | custom-call | tf_op jit(solution)/shard_map/pallas_call | solution.py:369
  (35 shorter events, 3.7 us)
Async XLA Ops:
  1.3 0.7 copy-start.9
  1.3 0.7 copy-start.6
  1.3 0.7 copy-start.7
  1.3 0.7 copy-start.8
  2.0 0.9 %copy-start = (f32[32,2048]{1,0:T(8,128)S(1)}, f32[32,2048]{1,0:T(8,128)}, u32[]{:S(2)}) copy-start(f32[32,2048]{1,0:T(8,128)} %sens_ref.3) | copy-start | bytes 786436
  3.0 16.6 %copy-start.1 = (f32[32,2048]{1,0:T(8,128)S(1)}, f32[32,2048]{1,0:T(8,128)}, u32[]{:S(2)}) copy-start(f32[32,2048]{1,0:T(8,128)} %sens_ref.3) | copy-start | bytes 786436
  4.1 15.5 %copy-start.2 = (bf16[3,128,128]{2,1,0:T(8,128)(2,1)S(1)}, bf16[3,128,128]{2,1,0:T(8,128)(2,1)}, u32[]{:S(2)}) copy-start(bf16[3,128,128]{2,1,0:T(8,128)(2,1)} %param.19) | copy-start | bytes 294916
  4.1 15.5 %copy-start.3 = (s32[128,128]{1,0:T(8,128)S(1)}, s32[128,128]{1,0:T(8,128)}, u32[]{:S(2)}) copy-start(s32[128,128]{1,0:T(8,128)} %conn_ref.3) | copy-start | bytes 196612
  4.1 15.5 %all-to-all-start = ((f32[32,8,128]{2,1,0:T(8,128)}), f32[32,8,128]{2,1,0:T(8,128)S(1)}, u32[]{:S(2)}, u32[]{:S(2)}) async-start(f32[32,8,128]{2,1,0:T(8,128)} %get-tuple-element.21), calls=%async_computation | async-start | bytes 262144 | tf_op jit(solution)/shard_map/all_to_all | solution.py:391
  11.4 8.2 %copy-start.4 = (f32[2048]{0:T(1024)S(1)}, f32[2048]{0:T(1024)}, u32[]{:S(2)}) copy-start(f32[2048]{0:T(1024)} %param.11) | copy-start | bytes 24580
  11.4 1.3 %collective-permute-start = (f32[40,256]{1,0:T(8,128)S(1)}, f32[40,256]{1,0:T(8,128)S(1)}, u32[]{:S(2)}, u32[]{:S(2)}) collective-permute-start(f32[40,256]{1,0:T(8,128)S(1)} %get-tuple-element.22), channel_id=1, source_target_pairs={{0,1},{1,0},{2,3},{3,2},{4,5},{5,4},{6,7},{7,6},{8,9},{9,8},{10,11... | collective-permute-start | bytes 122888 | tf_op jit(solution)/shard_map/ppermute | solution.py:387
  11.7 1.0 %collective-permute-start.1 = (f32[40,256]{1,0:T(8,128)S(1)}, f32[40,256]{1,0:T(8,128)S(1)}, u32[]{:S(2)}, u32[]{:S(2)}) collective-permute-start(f32[40,256]{1,0:T(8,128)S(1)} %get-tuple-element.23), channel_id=1, source_target_pairs={{1,2},{2,1},{3,4},{4,3},{5,6},{6,5},{7,8},{8,7},{9,10},{10,9},{11,... | collective-permute-start | bytes 122888 | tf_op jit(solution)/shard_map/ppermute | solution.py:387
  19.6 0.7 copy-start.5
  30.5 1.3 %collective-permute-start.2 = (f32[32,512]{1,0:T(8,128)S(1)}, f32[32,512]{1,0:T(8,128)S(1)}, u32[]{:S(2)}, u32[]{:S(2)}) collective-permute-start(f32[32,512]{1,0:T(8,128)S(1)} %get-tuple-element.27), channel_id=1, source_target_pairs={{0,1},{1,0},{2,3},{3,2},{4,5},{5,4},{6,7},{7,6},{8,9},{9,8},{10,11... | collective-permute-start | bytes 196616 | tf_op jit(solution)/shard_map/ppermute | solution.py:387
  30.8 1.0 %collective-permute-start.3 = (f32[32,512]{1,0:T(8,128)S(1)}, f32[32,512]{1,0:T(8,128)S(1)}, u32[]{:S(2)}, u32[]{:S(2)}) collective-permute-start(f32[32,512]{1,0:T(8,128)S(1)} %get-tuple-element.28), channel_id=1, source_target_pairs={{1,2},{2,1},{3,4},{4,3},{5,6},{6,5},{7,8},{8,7},{9,10},{10,9},{11,... | collective-permute-start | bytes 196616 | tf_op jit(solution)/shard_map/ppermute | solution.py:387
  64.0 1.3 %collective-permute-start.4 = (f32[32,512]{1,0:T(8,128)S(1)}, f32[32,512]{1,0:T(8,128)S(1)}, u32[]{:S(2)}, u32[]{:S(2)}) collective-permute-start(f32[32,512]{1,0:T(8,128)S(1)} %get-tuple-element.34), channel_id=1, source_target_pairs={{0,1},{1,0},{2,3},{3,2},{4,5},{5,4},{6,7},{7,6},{8,9},{9,8},{10,11... | collective-permute-start | bytes 196616 | tf_op jit(solution)/shard_map/ppermute | solution.py:387
  64.1 1.2 %collective-permute-start.5 = (f32[32,512]{1,0:T(8,128)S(1)}, f32[32,512]{1,0:T(8,128)S(1)}, u32[]{:S(2)}, u32[]{:S(2)}) collective-permute-start(f32[32,512]{1,0:T(8,128)S(1)} %get-tuple-element.35), channel_id=1, source_target_pairs={{1,2},{2,1},{3,4},{4,3},{5,6},{6,5},{7,8},{8,7},{9,10},{10,9},{11,... | collective-permute-start | bytes 196616 | tf_op jit(solution)/shard_map/ppermute | solution.py:387
  66.2 6.1 %collective-permute-start.6 = (f32[24,128]{1,0:T(8,128)S(1)}, f32[24,128]{1,0:T(8,128)S(1)}, u32[]{:S(2)}, u32[]{:S(2)}) collective-permute-start(f32[24,128]{1,0:T(8,128)S(1)} %shard_map.117), channel_id=1, source_target_pairs={{0,1},{1,0},{2,3},{3,2},{4,5},{5,4},{6,7},{7,6},{8,9},{9,8},{10,11... | collective-permute-start | bytes 36872 | tf_op jit(solution)/shard_map/ppermute | solution.py:406
  72.3 4.6 %collective-permute-start.9 = (f32[24,128]{1,0:T(8,128)S(1)}, f32[24,128]{1,0:T(8,128)S(1)}, u32[]{:S(2)}, u32[]{:S(2)}) collective-permute-start(f32[24,128]{1,0:T(8,128)S(1)} %add.21), channel_id=1, source_target_pairs={{0,6},{1,7},{2,4},{3,5},{4,2},{5,3},{6,0},{7,1},{8,14},{9,15},{10,... | collective-permute-start | bytes 36872 | tf_op jit(solution)/shard_map/ppermute | solution.py:406
  74.9 3.7 %collective-permute-start.8 = (f32[24,128]{1,0:T(8,128)S(1)}, f32[24,128]{1,0:T(8,128)S(1)}, u32[]{:S(2)}, u32[]{:S(2)}) collective-permute-start(f32[24,128]{1,0:T(8,128)S(1)} %add.21), channel_id=1, source_target_pairs={{0,4},{1,5},{2,6},{3,7},{4,0},{5,1},{6,2},{7,3},{8,12},{9,13},{10,... | collective-permute-start | bytes 36872 | tf_op jit(solution)/shard_map/ppermute | solution.py:406
  74.9 3.7 %collective-permute-start.7 = (f32[24,128]{1,0:T(8,128)S(1)}, f32[24,128]{1,0:T(8,128)S(1)}, u32[]{:S(2)}, u32[]{:S(2)}) collective-permute-start(f32[24,128]{1,0:T(8,128)S(1)} %add.21), channel_id=1, source_target_pairs={{0,2},{1,3},{2,0},{3,1},{4,6},{5,7},{6,4},{7,5},{8,10},{9,11},{10,... | collective-permute-start | bytes 36872 | tf_op jit(solution)/shard_map/ppermute | solution.py:406
  78.6 5.6 %collective-permute-start.12 = (f32[24,128]{1,0:T(8,128)S(1)}, f32[24,128]{1,0:T(8,128)S(1)}, u32[]{:S(2)}, u32[]{:S(2)}) collective-permute-start(f32[24,128]{1,0:T(8,128)S(1)} %add_add_fusion.1), channel_id=1, source_target_pairs={{0,24},{1,25},{2,26},{3,27},{4,28},{5,29},{6,30},{7,31},{8,16},{9,... | collective-permute-start | bytes 36872 | tf_op jit(solution)/shard_map/ppermute | solution.py:406
  80.1 4.6 %collective-permute-start.11 = (f32[24,128]{1,0:T(8,128)S(1)}, f32[24,128]{1,0:T(8,128)S(1)}, u32[]{:S(2)}, u32[]{:S(2)}) collective-permute-start(f32[24,128]{1,0:T(8,128)S(1)} %add_add_fusion.1), channel_id=1, source_target_pairs={{0,16},{1,17},{2,18},{3,19},{4,20},{5,21},{6,22},{7,23},{8,24},{9,... | collective-permute-start | bytes 36872 | tf_op jit(solution)/shard_map/ppermute | solution.py:406
  81.1 3.7 %collective-permute-start.10 = (f32[24,128]{1,0:T(8,128)S(1)}, f32[24,128]{1,0:T(8,128)S(1)}, u32[]{:S(2)}, u32[]{:S(2)}) collective-permute-start(f32[24,128]{1,0:T(8,128)S(1)} %add_add_fusion.1), channel_id=1, source_target_pairs={{0,8},{1,9},{2,10},{3,11},{4,12},{5,13},{6,14},{7,15},{8,0},{9,1},... | collective-permute-start | bytes 36872 | tf_op jit(solution)/shard_map/ppermute | solution.py:406

commit v3 on v2

--- a/solution.py
+++ b/solution.py
@@ -6,7 +6,7 @@
 from jax.sharding import PartitionSpec as P
 
 CHUNK = 16
-PIVOTS = 4
+PIVOTS = 16
 VMEM_LIMIT = 48 * 1024 * 1024
 AXIS = "brick"
 F32 = jnp.float32
@@ -78,8 +78,13 @@
     )
 
 
+def coefficients(joint_refs, element):
+    normal, shear, friction, slip = (ref[element] for ref in joint_refs)
+    return normal, shear, slip.astype(F32) * friction * normal
+
+
 def apply_elements(
-    half, conn_ref, owner_ref, coeff_ref, stacked_ref, values_ref, tiles_ref, total_ref,
+    half, conn_ref, owner_ref, joint_refs, stacked_ref, values_ref, tiles_ref, total_ref,
     state=None, state_ref=None,
 ):
     rows, width = half.shape
@@ -120,7 +125,8 @@
             values_ref[pl.ds(pl.multiple_of((start + e) * rows, rows), rows), :] = value.astype(BF16)
             scaled.append(
                 jnp.concatenate(
-                    [(value * coeff_ref[k, start + e]).astype(BF16) for k in range(3)], axis=1
+                    [(value * coeff).astype(BF16) for coeff in coefficients(joint_refs, start + e)],
+                    axis=1,
                 )
             )
             if state is not None:
@@ -172,7 +178,7 @@
     return jnp.where(odd, a, b), jnp.where(odd, b, a)
 
 
-def write_image(basis, parts, diag_ref, image_ref, a_ref, b_ref):
+def write_image(basis, parts, diag_ref, image_ref, a_ref, b_ref, state=None):
     rows, width = basis.shape
     depth = parts[0].shape[1]
     me = lax.axis_index(AXIS)
@@ -183,15 +189,20 @@
         for h in range(1, len(parts) - 1)
     ]
     image_ref[...] = jnp.concatenate([low] + own + [high], axis=1)
-    send_bands(
-        jnp.concatenate([own[0], low], axis=1), jnp.concatenate([own[-1], high], axis=1), a_ref, b_ref
-    )
-
-
-def complete(image_ref, a_ref, b_ref):
-    depth = a_ref.shape[1] // 2
-    width = image_ref.shape[1]
-    low, high = received_bands(a_ref, b_ref)
+    bands = [jnp.concatenate([own[0], low], axis=1), jnp.concatenate([own[-1], high], axis=1)]
+    if state is not None:
+        spare = jnp.zeros((a_ref.shape[0] - rows - 1, 2 * depth), F32)
+        bands = [
+            jnp.concatenate([band, row, spare], axis=0)
+            for band, row in zip(bands, (state[:, : 2 * depth], state[:, -2 * depth :]))
+        ]
+    send_bands(*bands, a_ref, b_ref)
+
+
+def complete(image_ref, low, high):
+    rows, width = image_ref.shape
+    depth = low.shape[1] // 2
+    low, high = low[:rows], high[:rows]
     return jnp.concatenate(
         [
             image_ref[:, : 2 * depth] + low,
@@ -202,59 +213,47 @@
     )
 
 
-def begin_kernel(
-    sens_ref, disp_ref, normal_ref, shear_ref, friction_ref, slip_ref, gram_ref, a_ref, b_ref, coeff_ref
-):
+def begin_kernel(sens_ref, owner_in, gram_ref, a_ref, b_ref, owner_ref, sem):
+    copy = pltpu.make_async_copy(owner_in, owner_ref, sem)
+    copy.start()
     sens = sens_ref[...]
     depth = a_ref.shape[1]
     owned = sens.shape[1]
     gram = packed(fdot(sens, sens, NT))
     gram_ref[...] = jnp.broadcast_to(gram[None], gram_ref.shape)
-    spare = jnp.zeros((a_ref.shape[0] - sens.shape[0] - 1, depth), F32)
-    disp = disp_ref[...].astype(F32)
-    low = jnp.concatenate([sens[:, :depth], disp[:, :depth], spare], axis=0)
-    high = jnp.concatenate([sens[:, owned - depth :], disp[:, owned - depth :], spare], axis=0)
-    send_bands(low, high, a_ref, b_ref)
-    coeff_ref[0:1, :] = normal_ref[...]
-    coeff_ref[1:2, :] = shear_ref[...]
-    coeff_ref[2:3, :] = slip_ref[...].astype(F32) * friction_ref[...] * normal_ref[...]
+    send_bands(sens[:, :depth], sens[:, owned - depth :], a_ref, b_ref)
+    copy.wait()
 
 
 def first_kernel(
-    gram_ref, sens_ref, disp_ref, a_in, b_in, diag_ref, conn_ref, owner_ref, coeff_ref, stacked_ref,
-    basis_ref, image_ref, a_ref, b_ref, factor_ref, values_ref, push_ref,
-    tiles_ref, total_ref, state_ref,
+    gram_ref, sens_ref, disp_ref, a_in, b_in, diag_ref, conn_ref, owner_ref, stacked_ref,
+    normal_ref, shear_ref, friction_ref, slip_ref,
+    basis_ref, image_ref, a_ref, b_ref, factor_ref, values_ref, tiles_ref, total_ref,
 ):
-    rows = sens_ref.shape[0]
-    slots = conn_ref.shape[1]
-    elems = conn_ref.shape[0]
     inverse, factor = lower_inverse(unpacked(jnp.sum(gram_ref[...], axis=0)))
     factor_ref[...] = factor
     low, high = received_bands(a_in, b_in)
-    basis = fdot(inverse, jnp.concatenate([low[:rows], sens_ref[...], high[:rows]], axis=1))
+    basis = fdot(inverse, jnp.concatenate([low, sens_ref[...], high], axis=1))
     basis_ref[...] = basis
-    state = jnp.concatenate(
-        [low[rows : rows + 1], disp_ref[...].astype(F32), high[rows : rows + 1]], axis=1
-    )
     parts = apply_elements(
-        basis.astype(BF16), conn_ref, owner_ref, coeff_ref, stacked_ref, values_ref, tiles_ref,
-        total_ref, state, state_ref,
-    )
-    write_image(basis, parts, diag_ref, image_ref, a_ref, b_ref)
-    moved = state_ref[...].astype(BF16)
-    for k in range(3):
-        push_ref[:, k * elems : (k + 1) * elems] = bdot(
-            stacked_ref[k * slots : (k + 1) * slots, :], moved, NT
-        ).astype(BF16)
+        basis.astype(BF16), conn_ref, owner_ref, (normal_ref, shear_ref, friction_ref, slip_ref),
+        stacked_ref, values_ref, tiles_ref, total_ref,
+    )
+    write_image(basis, parts, diag_ref, image_ref, a_ref, b_ref, disp_ref[...].astype(F32))
 
 
 def own_part(field, depth):
     return field[:, depth : field.shape[1] - depth]
 
 
-def middle_kernel(basis_ref, image_ref, a_in, b_in, full_ref, gram_ref):
+def middle_kernel(basis_ref, image_ref, disp_ref, a_in, b_in, full_ref, state_ref, gram_ref):
     depth = a_in.shape[1] // 2
-    full = complete(image_ref, a_in, b_in)
+    low, high = received_bands(a_in, b_in)
+    full = complete(image_ref, low, high)
+    at = full.shape[0]
+    state_ref[...] = jnp.concatenate(
+        [low[at : at + 1, depth:], disp_ref[...].astype(F32), high[at : at + 1, :depth]], axis=1
+    )
     full_ref[...] = full
     own = own_part(full, depth)
     rows = own.shape[0]
@@ -264,9 +263,12 @@
 
 
 def second_kernel(
-    gram_ref, factor0_ref, basis0_ref, full_ref, diag_ref, conn_ref, owner_ref, coeff_ref, stacked_ref,
-    basis_ref, image_ref, a_ref, b_ref, small_ref, values_ref, tiles_ref, total_ref,
+    gram_ref, factor0_ref, basis0_ref, full_ref, row_ref, diag_ref, conn_ref, owner_ref, stacked_ref,
+    normal_ref, shear_ref, friction_ref, slip_ref,
+    basis_ref, image_ref, a_ref, b_ref, small_ref, values_ref, push_ref,
+    tiles_ref, total_ref, state_ref,
 ):
+    elems, slots = conn_ref.shape
     tile = jnp.sum(gram_ref[...], axis=0)
     part = tile.shape[0] // 2
     proj, square = unpacked(tile[:part]), unpacked(tile[part:])
@@ -280,14 +282,20 @@
     small_ref[2] = fdot(head, factor, NT)
     small_ref[3] = fdot(head, fdot(proj, factor0_ref[...], TN))
     parts = apply_elements(
-        basis.astype(BF16), conn_ref, owner_ref, coeff_ref, stacked_ref, values_ref, tiles_ref, total_ref
+        basis.astype(BF16), conn_ref, owner_ref, (normal_ref, shear_ref, friction_ref, slip_ref),
+        stacked_ref, values_ref, tiles_ref, total_ref, row_ref[...], state_ref,
     )
     write_image(basis, parts, diag_ref, image_ref, a_ref, b_ref)
+    moved = state_ref[...].astype(BF16)
+    for k in range(3):
+        push_ref[:, k * elems : (k + 1) * elems] = bdot(
+            stacked_ref[k * slots : (k + 1) * slots, :], moved, NT
+        ).astype(BF16)
 
 
 def late_kernel(basis0_ref, basis1_ref, image_ref, a_in, b_in, gram_ref):
     depth = a_in.shape[1] // 2
-    own = own_part(complete(image_ref, a_in, b_in), depth)
+    own = own_part(complete(image_ref, *received_bands(a_in, b_in)), depth)
     rows = own.shape[0]
     every = fdot(
         jnp.concatenate(
@@ -365,16 +373,18 @@
     grads_ref[2] = -slip * normal_ref[...] * third
 
 
-def call(kernel, outs, scratch, args, smem=()):
+def call(kernel, outs, scratch, args, smem=(), anywhere=()):
+    spaces = {i: pltpu.SMEM for i in smem} | {i: pl.ANY for i in anywhere}
     return pl.pallas_call(
         kernel,
         out_shape=[jax.ShapeDtypeStruct(shape, dtype) for shape, dtype in outs],
         in_specs=[
-            pl.BlockSpec(memory_space=pltpu.SMEM if i in smem else pltpu.VMEM)
-            for i in range(len(args))
+            pl.BlockSpec(memory_space=spaces.get(i, pltpu.VMEM)) for i in range(len(args))
         ],
         out_specs=[pl.BlockSpec(memory_space=pltpu.VMEM) for unused in outs],
-        scratch_shapes=[pltpu.VMEM(shape, dtype) for shape, dtype in scratch],
+        scratch_shapes=[
+            pltpu.SemaphoreType.DMA if item is None else pltpu.VMEM(*item) for item in scratch
+        ],
         compiler_params=pltpu.CompilerParams(vmem_limit_bytes=VMEM_LIMIT),
     )(*args)
 
@@ -429,37 +439,43 @@
 
     line = lambda array: array[None, :]
     disp, diag = line(displacement), line(diagonal)
-    normal, shear, fric, slip = line(normal_stiff), line(shear_stiff), line(friction), line(slip_state)
+    normal, fric, slip = line(normal_stiff), line(friction), line(slip_state)
     owner = owner_map[0]
     stacked = templates.reshape(3 * slots, slots)
 
-    start_band = ((rows + 8, depth), F32)
-    gram, a, b, coeffs = call(
+    joints = [normal_stiff, shear_stiff, friction, slip_state]
+
+    gram, a, b, owner = call(
         begin_kernel,
-        [((devices, part, 128), F32), start_band, start_band, ((3, elems), F32)],
-        [],
-        [sensitivity, disp, normal, shear, fric, slip],
+        [((devices, part, 128), F32), ((rows, depth), F32), ((rows, depth), F32), (owner.shape, owner.dtype)],
+        [None],
+        [sensitivity, owner],
+        anywhere=(1,),
     )
     a, b = exchanged(a, b)
     gram = everyones(gram)
-    basis0, image, a, b, factor0, values0, pushed = call(
+    taller = ((rows + 8, 2 * depth), F32)
+    basis0, image, a, b, factor0, values0 = call(
         first_kernel,
-        [wide, wide, band, band, ((rows, rows), F32), picked, ((slots, 3 * elems), BF16)],
+        [wide, wide, taller, taller, ((rows, rows), F32), picked],
+        [((count * rows, depth), BF16), ((count * rows, depth), F32)],
+        [gram, sensitivity, disp, a, b, diag, connectivity, owner, stacked] + joints,
+        smem=(9, 10, 11, 12),
+    )
+    a, b = exchanged(a, b)
+    full, state, gram = call(
+        middle_kernel,
+        [wide, ((1, width), F32), ((devices, 2 * part, 128), F32)],
+        [],
+        [basis0, image, disp, a, b],
+    )
+    gram = everyones(gram)
+    basis1, image, a, b, small, values1, pushed = call(
+        second_kernel,
+        [wide, wide, band, band, ((4, rows, rows), F32), picked, ((slots, 3 * elems), BF16)],
         [((count * rows + extra, depth), BF16), ((count * rows, depth), F32), ((elems, slots), F32)],
-        [gram, sensitivity, disp, a, b, diag, connectivity, owner, coeffs, stacked],
-        smem=(8,),
-    )
-    a, b = exchanged(a, b)
-    full, gram = call(
-        middle_kernel, [wide, ((devices, 2 * part, 128), F32)], [], [basis0, image, a, b]
-    )
-    gram = everyones(gram)
-    basis1, image, a, b, small, values1 = call(
-        second_kernel,
-        [wide, wide, band, band, ((4, rows, rows), F32), picked],
-        [((count * rows, depth), BF16), ((count * rows, depth), F32)],
-        [gram, factor0, basis0, full, diag, connectivity, owner, coeffs, stacked],
-        smem=(7,),
+        [gram, factor0, basis0, full, state, diag, connectivity, owner, stacked] + joints,
+        smem=(9, 10, 11, 12),
     )
     a, b = exchanged(a, b)
     gram = call(late_kernel, [((3 * part, 128), F32)], [], [basis0, basis1, image, a, b])[0]

time: 91 us -> 88.1 us (0.968)
  Pallas kernels: 29.7 us -> 27.2 us
    pallas_call x6, Pallas kernels: 29.7 us -> 27.2 us  [call(): pl.pallas_call(kernel, out_shape=[jax.ShapeDtypeStruct(shape, dtype) for...]
    unnamed x20 -> x22, local copies, waits for them, and re-layouts: 2.31 us -> 2.3 us
where the time goes in v3:
time: 88.1 us; the launch traced here: 87.7 us
  Pallas kernels  27.2 us (31%)
  starting transfers between devices  23.5 us (27%)
  blocking collectives  20.7 us (23%)
  waiting for transfers between devices  13.2 us (15%)
  local copies, waits for them, and re-layouts  2.3 us (3%)
    pallas_call x6, Pallas kernels, call(): pl.pallas_call(kernel, out_shape=[jax.ShapeDtypeStruct(shape, dtype) for...  27.2 us
    all_to_all x1, blocking collectives, everyones(): return lax.all_to_all(copies, AXIS, 0, 0, tiled=True)  20.7 us
    ppermute x7, starting transfers between devices, total(): parts.append(lax.ppermute(value, AXIS, route))  13.2 us
    all_to_all x1, starting transfers between devices, everyones(): return lax.all_to_all(copies, AXIS, 0, 0, tiled=True)  7.3 us
    all_to_all x1, waiting for transfers between devices, everyones(): return lax.all_to_all(copies, AXIS, 0, 0, tiled=True)  6.95 us
    ppermute x7, waiting for transfers between devices, total(): parts.append(lax.ppermute(value, AXIS, route))  5.42 us
    ppermute x6, starting transfers between devices, exchanged(): return (lax.ppermute(a, AXIS, first), lax.ppermute(b, AXIS, second))  3 us
    unnamed x22, local copies, waits for them, and re-layouts  2.3 us
  transfers between devices with their start and end apart: 14, of which 10 were waited for; matrix products, arithmetic and copies ran while one was open for 0% of the time, Pallas kernels for 0%

profile of v3, /device:TPU:0, one launch (start us, length us, event | category | flops | bytes accessed | tf_op | source)
XLA Modules:
  0.0 87.7 jit_solution(11945035052370142723)
XLA Ops:
  0.6 0.9 %copy-done = f32[32,2048]{1,0:T(8,128)S(1)} copy-done((f32[32,2048]{1,0:T(8,128)S(1)}, f32[32,2048]{1,0:T(8,128)}, u32[]{:S(2)}) %copy-start) | copy-done | bytes 262168
  1.6 0.7 copy-done.8
  2.3 1.1 %shard_map.113 = (f32[32,8,128]{2,1,0:T(8,128)}, f32[32,256]{1,0:T(8,128)S(1)}, f32[32,256]{1,0:T(8,128)S(1)}, s32[2,256]{1,0:T(2,128)S(1)}) custom-call(f32[32,2048]{1,0:T(8,128)S(1)} %copy-done, s32[2,256]{1,0:T(2,128)S(1)} %bitcast.13), custom_call_target="tpu_custom_call" | custom-call | tf_op jit(solution)/shard_map/pallas_call | solution.py:378
  3.4 7.3 %all-to-all-start = ((f32[32,8,128]{2,1,0:T(8,128)}), f32[32,8,128]{2,1,0:T(8,128)S(1)}, u32[]{:S(2)}, u32[]{:S(2)}) async-start(f32[32,8,128]{2,1,0:T(8,128)} %get-tuple-element.22), calls=%async_computation | async-start | bytes 262144 | tf_op jit(solution)/shard_map/all_to_all | solution.py:401
  11.0 0.8 collective-permute-start.1
  12.0 7.0 %all-to-all-done.gram_ref = f32[32,8,128]{2,1,0:T(8,128)S(1)} async-done(((f32[32,8,128]{2,1,0:T(8,128)}), f32[32,8,128]{2,1,0:T(8,128)S(1)}, u32[]{:S(2)}, u32[]{:S(2)}) %all-to-all-start) | async-done | bytes 131104 | tf_op jit(solution)/shard_map/all_to_all | solution.py:401
  19.6 9.1 %shard_map.114 = (f32[32,2560]{1,0:T(8,128)S(1)}, f32[32,2560]{1,0:T(8,128)S(1)}, f32[40,512]{1,0:T(8,128)S(1)}, f32[40,512]{1,0:T(8,128)S(1)}, f32[32,32]{1,0:T(8,128)S(1)}, /*index=5*/bf16[4096,128]{1,0:T(8,128)(2,1)S(1)}) custom-call(f32[32,8,128]{2,1,0:T(8,128)S(1)} %all-to-all-done.gram_ref, f32[32,2048]{1,0:T(8,128)S(1)} %copy-done.1, ...), custom_call_target="tpu_custom_call" | custom-call | tf_op jit(solution)/shard_map/pallas_call | solution.py:378
  29.0 0.7 collective-permute-start.3
  30.1 0.7 shard_map.115
  30.7 20.7 %all_to_all.10.gram_ref = f32[32,16,128]{2,1,0:T(8,128)S(1)} all-to-all(f32[32,16,128]{2,1,0:T(8,128)S(1)} %get-tuple-element.30), channel_id=1, replica_groups=mesh['brick'=32] {'brick'}, dimensions={0} | all-to-all | bytes 524288 | tf_op jit(solution)/shard_map/all_to_all | solution.py:401
  51.4 10.3 %shard_map.116 = (f32[32,2560]{1,0:T(8,128)S(1)}, f32[32,2560]{1,0:T(8,128)S(1)}, f32[32,512]{1,0:T(8,128)S(1)}, f32[32,512]{1,0:T(8,128)S(1)}, f32[4,32,32]{2,1...) custom-call(f32[32,16,128]{2,1,0:T(8,128)S(1)} %all_to_all.10.gram_ref, ...), custom_call_target="tpu_custom_call" | custom-call | tf_op jit(solution)/shard_map/pallas_call | solution.py:378
  61.8 0.9 %collective-permute-start.5 = (f32[32,512]{1,0:T(8,128)S(1)}, f32[32,512]{1,0:T(8,128)S(1)}, u32[]{:S(2)}, u32[]{:S(2)}) collective-permute-start(f32[32,512]{1,0:T(8,128)S(1)} %get-tuple-element.37), channel_id=1, source_target_pairs={{1,2},{2,1},{3,4},{4,3},{5,6},{6,5},{7,8},{8,7},{9,10},{10,9},{11,... | collective-permute-start | bytes 196616 | tf_op jit(solution)/shard_map/ppermute | solution.py:397
  63.0 0.8 shard_map.117
  63.9 5.2 %collective-permute-start.6 = (f32[24,128]{1,0:T(8,128)S(1)}, f32[24,128]{1,0:T(8,128)S(1)}, u32[]{:S(2)}, u32[]{:S(2)}) collective-permute-start(f32[24,128]{1,0:T(8,128)S(1)} %shard_map.117), channel_id=1, source_target_pairs={{0,1},{1,0},{2,3},{3,2},{4,5},{5,4},{6,7},{7,6},{8,9},{9,8},{10,11... | collective-permute-start | bytes 36872 | tf_op jit(solution)/shard_map/ppermute | solution.py:416
  69.1 0.8 collective-permute-done.6
  69.9 2.6 %collective-permute-start.9 = (f32[24,128]{1,0:T(8,128)S(1)}, f32[24,128]{1,0:T(8,128)S(1)}, u32[]{:S(2)}, u32[]{:S(2)}) collective-permute-start(f32[24,128]{1,0:T(8,128)S(1)} %add.21), channel_id=1, source_target_pairs={{0,6},{1,7},{2,4},{3,5},{4,2},{5,3},{6,0},{7,1},{8,14},{9,15},{10,... | collective-permute-start | bytes 36872 | tf_op jit(solution)/shard_map/ppermute | solution.py:416
  72.6 0.9 collective-permute-start.7
  73.4 1.1 %collective-permute-done.9 = f32[24,128]{1,0:T(8,128)S(1)} collective-permute-done((f32[24,128]{1,0:T(8,128)S(1)}, f32[24,128]{1,0:T(8,128)S(1)}, u32[]{:S(2)}, u32[]{:S(2)}) %collective-permute-start.9) | collective-permute-done | bytes 12320 | tf_op jit(solution)/shard_map/ppermute | solution.py:416
  74.5 1.7 %collective-permute-done.8 = f32[24,128]{1,0:T(8,128)S(1)} collective-permute-done((f32[24,128]{1,0:T(8,128)S(1)}, f32[24,128]{1,0:T(8,128)S(1)}, u32[]{:S(2)}, u32[]{:S(2)}) %collective-permute-start.8) | collective-permute-done | bytes 12320 | tf_op jit(solution)/shard_map/ppermute | solution.py:416
  76.3 1.5 %collective-permute-start.12 = (f32[24,128]{1,0:T(8,128)S(1)}, f32[24,128]{1,0:T(8,128)S(1)}, u32[]{:S(2)}, u32[]{:S(2)}) collective-permute-start(f32[24,128]{1,0:T(8,128)S(1)} %add_add_fusion.1), channel_id=1, source_target_pairs={{0,24},{1,25},{2,26},{3,27},{4,28},{5,29},{6,30},{7,31},{8,16},{9,... | collective-permute-start | bytes 36872 | tf_op jit(solution)/shard_map/ppermute | solution.py:416
  77.7 1.0 %collective-permute-start.11 = (f32[24,128]{1,0:T(8,128)S(1)}, f32[24,128]{1,0:T(8,128)S(1)}, u32[]{:S(2)}, u32[]{:S(2)}) collective-permute-start(f32[24,128]{1,0:T(8,128)S(1)} %add_add_fusion.1), channel_id=1, source_target_pairs={{0,16},{1,17},{2,18},{3,19},{4,20},{5,21},{6,22},{7,23},{8,24},{9,... | collective-permute-start | bytes 36872 | tf_op jit(solution)/shard_map/ppermute | solution.py:416
  78.8 1.9 %collective-permute-start.10 = (f32[24,128]{1,0:T(8,128)S(1)}, f32[24,128]{1,0:T(8,128)S(1)}, u32[]{:S(2)}, u32[]{:S(2)}) collective-permute-start(f32[24,128]{1,0:T(8,128)S(1)} %add_add_fusion.1), channel_id=1, source_target_pairs={{0,8},{1,9},{2,10},{3,11},{4,12},{5,13},{6,14},{7,15},{8,0},{9,1},... | collective-permute-start | bytes 36872 | tf_op jit(solution)/shard_map/ppermute | solution.py:416
  80.7 1.1 %collective-permute-done.12 = f32[24,128]{1,0:T(8,128)S(1)} collective-permute-done((f32[24,128]{1,0:T(8,128)S(1)}, f32[24,128]{1,0:T(8,128)S(1)}, u32[]{:S(2)}, u32[]{:S(2)}) %collective-permute-start.12) | collective-permute-done | bytes 12320 | tf_op jit(solution)/shard_map/ppermute | solution.py:416
  82.5 5.2 %shard_map.118 = (f32[32,2048]{1,0:T(8,128)}, f32[3,32,128]{2,1,0:T(8,128)}) custom-call(f32[24,128]{1,0:T(8,128)S(1)} %add_add_fusion.gram_ref, f32[32,32]{1,0:T(8,128)S(1)} %get-tuple-element.31.factor0_ref, f32[4,32,32]{2,1,0:T(8,128)S(1)} %get-tuple-element.38.small_ref, f32[32,2560]{1,0:T(8,128)S(1)} %get-tuple-element.26.basis_ref.basis0_ref, ...), custom_call_target="tpu_custom_call" | custom-call | tf_op jit(solution)/shard_map/pallas_call | solution.py:378
  (37 shorter events, 2.9 us)
Async XLA Ops:
  0.6 1.0 %copy-start = (f32[32,2048]{1,0:T(8,128)S(1)}, f32[32,2048]{1,0:T(8,128)}, u32[]{:S(2)}) copy-start(f32[32,2048]{1,0:T(8,128)} %sens_ref.3) | copy-start | bytes 786436
  1.6 0.7 copy-start.8
  2.3 16.7 %copy-start.1 = (f32[32,2048]{1,0:T(8,128)S(1)}, f32[32,2048]{1,0:T(8,128)}, u32[]{:S(2)}) copy-start(f32[32,2048]{1,0:T(8,128)} %sens_ref.3) | copy-start | bytes 786436
  3.4 8.5 %copy-start.10 = (bf16[2048]{0:T(1024)(128)(2,1)S(1)}, bf16[2048]{0:T(1024)(128)(2,1)}, u32[]{:S(2)}) copy-start(bf16[2048]{0:T(1024)(128)(2,1)} %param.12) | copy-start | bytes 12292
  3.4 15.6 %copy-start.2 = (bf16[3,128,128]{2,1,0:T(8,128)(2,1)S(1)}, bf16[3,128,128]{2,1,0:T(8,128)(2,1)}, u32[]{:S(2)}) copy-start(bf16[3,128,128]{2,1,0:T(8,128)(2,1)} %param.19) | copy-start | bytes 294916
  3.4 15.6 %copy-start.3 = (s32[128,128]{1,0:T(8,128)S(1)}, s32[128,128]{1,0:T(8,128)}, u32[]{:S(2)}) copy-start(s32[128,128]{1,0:T(8,128)} %conn_ref.3) | copy-start | bytes 196612
  3.4 15.5 %all-to-all-start = ((f32[32,8,128]{2,1,0:T(8,128)}), f32[32,8,128]{2,1,0:T(8,128)S(1)}, u32[]{:S(2)}, u32[]{:S(2)}) async-start(f32[32,8,128]{2,1,0:T(8,128)} %get-tuple-element.22), calls=%async_computation | async-start | bytes 262144 | tf_op jit(solution)/shard_map/all_to_all | solution.py:401
  10.7 1.3 %collective-permute-start = (f32[32,256]{1,0:T(8,128)S(1)}, f32[32,256]{1,0:T(8,128)S(1)}, u32[]{:S(2)}, u32[]{:S(2)}) collective-permute-start(f32[32,256]{1,0:T(8,128)S(1)} %get-tuple-element.23), channel_id=1, source_target_pairs={{0,1},{1,0},{2,3},{3,2},{4,5},{5,4},{6,7},{7,6},{8,9},{9,8},{10,11... | collective-permute-start | bytes 98312 | tf_op jit(solution)/shard_map/ppermute | solution.py:397
  11.0 7.9 %copy-start.4 = (f32[2048]{0:T(1024)S(1)}, f32[2048]{0:T(1024)}, u32[]{:S(2)}) copy-start(f32[2048]{0:T(1024)} %param.11) | copy-start | bytes 24580
  11.0 1.0 %collective-permute-start.1 = (f32[32,256]{1,0:T(8,128)S(1)}, f32[32,256]{1,0:T(8,128)S(1)}, u32[]{:S(2)}, u32[]{:S(2)}) collective-permute-start(f32[32,256]{1,0:T(8,128)S(1)} %get-tuple-element.24), channel_id=1, source_target_pairs={{1,2},{2,1},{3,4},{4,3},{5,6},{6,5},{7,8},{8,7},{9,10},{10,9},{11,... | collective-permute-start | bytes 98312 | tf_op jit(solution)/shard_map/ppermute | solution.py:397
  11.8 7.2 %copy-start.9 = (f32[128]{0:T(128)S(1)}, f32[128]{0:T(128)}, u32[]{:S(2)}) copy-start(f32[128]{0:T(128)} %shear_ref.3) | copy-start | bytes 1540
  18.9 0.7 copy-start.6
  19.0 0.7 copy-start.7
  28.7 1.3 %collective-permute-start.2 = (f32[40,512]{1,0:T(8,128)S(1)}, f32[40,512]{1,0:T(8,128)S(1)}, u32[]{:S(2)}, u32[]{:S(2)}) collective-permute-start(f32[40,512]{1,0:T(8,128)S(1)} %get-tuple-element.28), channel_id=1, source_target_pairs={{0,1},{1,0},{2,3},{3,2},{4,5},{5,4},{6,7},{7,6},{8,9},{9,8},{10,11... | collective-permute-start | bytes 245768 | tf_op jit(solution)/shard_map/ppermute | solution.py:397
  29.0 1.1 %collective-permute-start.3 = (f32[40,512]{1,0:T(8,128)S(1)}, f32[40,512]{1,0:T(8,128)S(1)}, u32[]{:S(2)}, u32[]{:S(2)}) collective-permute-start(f32[40,512]{1,0:T(8,128)S(1)} %get-tuple-element.29), channel_id=1, source_target_pairs={{1,2},{2,1},{3,4},{4,3},{5,6},{6,5},{7,8},{8,7},{9,10},{10,9},{11,... | collective-permute-start | bytes 245768 | tf_op jit(solution)/shard_map/ppermute | solution.py:397
  61.7 1.3 %collective-permute-start.4 = (f32[32,512]{1,0:T(8,128)S(1)}, f32[32,512]{1,0:T(8,128)S(1)}, u32[]{:S(2)}, u32[]{:S(2)}) collective-permute-start(f32[32,512]{1,0:T(8,128)S(1)} %get-tuple-element.36), channel_id=1, source_target_pairs={{0,1},{1,0},{2,3},{3,2},{4,5},{5,4},{6,7},{7,6},{8,9},{9,8},{10,11... | collective-permute-start | bytes 196616 | tf_op jit(solution)/shard_map/ppermute | solution.py:397
  61.8 1.2 %collective-permute-start.5 = (f32[32,512]{1,0:T(8,128)S(1)}, f32[32,512]{1,0:T(8,128)S(1)}, u32[]{:S(2)}, u32[]{:S(2)}) collective-permute-start(f32[32,512]{1,0:T(8,128)S(1)} %get-tuple-element.37), channel_id=1, source_target_pairs={{1,2},{2,1},{3,4},{4,3},{5,6},{6,5},{7,8},{8,7},{9,10},{10,9},{11,... | collective-permute-start | bytes 196616 | tf_op jit(solution)/shard_map/ppermute | solution.py:397
  63.9 6.1 %collective-permute-start.6 = (f32[24,128]{1,0:T(8,128)S(1)}, f32[24,128]{1,0:T(8,128)S(1)}, u32[]{:S(2)}, u32[]{:S(2)}) collective-permute-start(f32[24,128]{1,0:T(8,128)S(1)} %shard_map.117), channel_id=1, source_target_pairs={{0,1},{1,0},{2,3},{3,2},{4,5},{5,4},{6,7},{7,6},{8,9},{9,8},{10,11... | collective-permute-start | bytes 36872 | tf_op jit(solution)/shard_map/ppermute | solution.py:416
  69.9 4.6 %collective-permute-start.9 = (f32[24,128]{1,0:T(8,128)S(1)}, f32[24,128]{1,0:T(8,128)S(1)}, u32[]{:S(2)}, u32[]{:S(2)}) collective-permute-start(f32[24,128]{1,0:T(8,128)S(1)} %add.21), channel_id=1, source_target_pairs={{0,6},{1,7},{2,4},{3,5},{4,2},{5,3},{6,0},{7,1},{8,14},{9,15},{10,... | collective-permute-start | bytes 36872 | tf_op jit(solution)/shard_map/ppermute | solution.py:416
  72.6 3.7 %collective-permute-start.8 = (f32[24,128]{1,0:T(8,128)S(1)}, f32[24,128]{1,0:T(8,128)S(1)}, u32[]{:S(2)}, u32[]{:S(2)}) collective-permute-start(f32[24,128]{1,0:T(8,128)S(1)} %add.21), channel_id=1, source_target_pairs={{0,4},{1,5},{2,6},{3,7},{4,0},{5,1},{6,2},{7,3},{8,12},{9,13},{10,... | collective-permute-start | bytes 36872 | tf_op jit(solution)/shard_map/ppermute | solution.py:416
  72.6 3.7 %collective-permute-start.7 = (f32[24,128]{1,0:T(8,128)S(1)}, f32[24,128]{1,0:T(8,128)S(1)}, u32[]{:S(2)}, u32[]{:S(2)}) collective-permute-start(f32[24,128]{1,0:T(8,128)S(1)} %add.21), channel_id=1, source_target_pairs={{0,2},{1,3},{2,0},{3,1},{4,6},{5,7},{6,4},{7,5},{8,10},{9,11},{10,... | collective-permute-start | bytes 36872 | tf_op jit(solution)/shard_map/ppermute | solution.py:416
  76.3 5.6 %collective-permute-start.12 = (f32[24,128]{1,0:T(8,128)S(1)}, f32[24,128]{1,0:T(8,128)S(1)}, u32[]{:S(2)}, u32[]{:S(2)}) collective-permute-start(f32[24,128]{1,0:T(8,128)S(1)} %add_add_fusion.1), channel_id=1, source_target_pairs={{0,24},{1,25},{2,26},{3,27},{4,28},{5,29},{6,30},{7,31},{8,16},{9,... | collective-permute-start | bytes 36872 | tf_op jit(solution)/shard_map/ppermute | solution.py:416
  77.7 4.6 %collective-permute-start.11 = (f32[24,128]{1,0:T(8,128)S(1)}, f32[24,128]{1,0:T(8,128)S(1)}, u32[]{:S(2)}, u32[]{:S(2)}) collective-permute-start(f32[24,128]{1,0:T(8,128)S(1)} %add_add_fusion.1), channel_id=1, source_target_pairs={{0,16},{1,17},{2,18},{3,19},{4,20},{5,21},{6,22},{7,23},{8,24},{9,... | collective-permute-start | bytes 36872 | tf_op jit(solution)/shard_map/ppermute | solution.py:416
  78.8 3.7 %collective-permute-start.10 = (f32[24,128]{1,0:T(8,128)S(1)}, f32[24,128]{1,0:T(8,128)S(1)}, u32[]{:S(2)}, u32[]{:S(2)}) collective-permute-start(f32[24,128]{1,0:T(8,128)S(1)} %add_add_fusion.1), channel_id=1, source_target_pairs={{0,8},{1,9},{2,10},{3,11},{4,12},{5,13},{6,14},{7,15},{8,0},{9,1},... | collective-permute-start | bytes 36872 | tf_op jit(solution)/shard_map/ppermute | solution.py:416
  (1 other events, 0.7 us)

commit v4 on v3

--- a/solution.py
+++ b/solution.py
@@ -78,20 +78,15 @@
     )
 
 
-def coefficients(joint_refs, element):
-    normal, shear, friction, slip = (ref[element] for ref in joint_refs)
-    return normal, shear, slip.astype(F32) * friction * normal
-
-
 def apply_elements(
-    half, conn_ref, owner_ref, joint_refs, stacked_ref, values_ref, tiles_ref, total_ref,
+    half, conn_ref, owner_ref, coeff_ref, stacked_ref, values_ref, tiles_ref, total_ref,
     state=None, state_ref=None,
 ):
     rows, width = half.shape
     depth = owner_ref.shape[1]
     count = width // depth
     elems, slots = conn_ref.shape
-    owner = owner_ref[...].astype(F32)
+    owner = owner_ref[...]
     below, above = one_hot(owner[0:1, :], depth), one_hot(owner[1:2, :], depth)
     tiles_ref[:rows, :] = bdot(half[:, :depth], below).astype(BF16)
     for h in range(1, count - 1):
@@ -125,8 +120,7 @@
             values_ref[pl.ds(pl.multiple_of((start + e) * rows, rows), rows), :] = value.astype(BF16)
             scaled.append(
                 jnp.concatenate(
-                    [(value * coeff).astype(BF16) for coeff in coefficients(joint_refs, start + e)],
-                    axis=1,
+                    [(value * coeff_ref[k, start + e]).astype(BF16) for k in range(3)], axis=1
                 )
             )
             if state is not None:
@@ -213,21 +207,18 @@
     )
 
 
-def begin_kernel(sens_ref, owner_in, gram_ref, a_ref, b_ref, owner_ref, sem):
-    copy = pltpu.make_async_copy(owner_in, owner_ref, sem)
-    copy.start()
+def begin_kernel(sens_ref, gram_ref, a_ref, b_ref):
     sens = sens_ref[...]
     depth = a_ref.shape[1]
     owned = sens.shape[1]
     gram = packed(fdot(sens, sens, NT))
     gram_ref[...] = jnp.broadcast_to(gram[None], gram_ref.shape)
     send_bands(sens[:, :depth], sens[:, owned - depth :], a_ref, b_ref)
-    copy.wait()
 
 
 def first_kernel(
-    gram_ref, sens_ref, disp_ref, a_in, b_in, diag_ref, conn_ref, owner_ref, stacked_ref,
-    normal_ref, shear_ref, friction_ref, slip_ref,
+    gram_ref, sens_ref, disp_ref, a_in, b_in, diag_ref, conn_ref, owner_ref, coeff_ref,
+    stacked_ref,
     basis_ref, image_ref, a_ref, b_ref, factor_ref, values_ref, tiles_ref, total_ref,
 ):
     inverse, factor = lower_inverse(unpacked(jnp.sum(gram_ref[...], axis=0)))
@@ -236,10 +227,10 @@
     basis = fdot(inverse, jnp.concatenate([low, sens_ref[...], high], axis=1))
     basis_ref[...] = basis
     parts = apply_elements(
-        basis.astype(BF16), conn_ref, owner_ref, (normal_ref, shear_ref, friction_ref, slip_ref),
+        basis.astype(BF16), conn_ref, owner_ref, coeff_ref,
         stacked_ref, values_ref, tiles_ref, total_ref,
     )
-    write_image(basis, parts, diag_ref, image_ref, a_ref, b_ref, disp_ref[...].astype(F32))
+    write_image(basis, parts, diag_ref, image_ref, a_ref, b_ref, disp_ref[...])
 
 
 def own_part(field, depth):
@@ -252,7 +243,7 @@
     full = complete(image_ref, low, high)
     at = full.shape[0]
     state_ref[...] = jnp.concatenate(
-        [low[at : at + 1, depth:], disp_ref[...].astype(F32), high[at : at + 1, :depth]], axis=1
+        [low[at : at + 1, depth:], disp_ref[...], high[at : at + 1, :depth]], axis=1
     )
     full_ref[...] = full
     own = own_part(full, depth)
@@ -263,8 +254,8 @@
 
 
 def second_kernel(
-    gram_ref, factor0_ref, basis0_ref, full_ref, row_ref, diag_ref, conn_ref, owner_ref, stacked_ref,
-    normal_ref, shear_ref, friction_ref, slip_ref,
+    gram_ref, factor0_ref, basis0_ref, full_ref, row_ref, diag_ref, conn_ref, owner_ref, coeff_ref,
+    stacked_ref,
     basis_ref, image_ref, a_ref, b_ref, small_ref, values_ref, push_ref,
     tiles_ref, total_ref, state_ref,
 ):
@@ -282,7 +273,7 @@
     small_ref[2] = fdot(head, factor, NT)
     small_ref[3] = fdot(head, fdot(proj, factor0_ref[...], TN))
     parts = apply_elements(
-        basis.astype(BF16), conn_ref, owner_ref, (normal_ref, shear_ref, friction_ref, slip_ref),
+        basis.astype(BF16), conn_ref, owner_ref, coeff_ref,
         stacked_ref, values_ref, tiles_ref, total_ref, row_ref[...], state_ref,
     )
     write_image(basis, parts, diag_ref, image_ref, a_ref, b_ref)
@@ -373,18 +364,16 @@
     grads_ref[2] = -slip * normal_ref[...] * third
 
 
-def call(kernel, outs, scratch, args, smem=(), anywhere=()):
-    spaces = {i: pltpu.SMEM for i in smem} | {i: pl.ANY for i in anywhere}
+def call(kernel, outs, scratch, args, smem=()):
     return pl.pallas_call(
         kernel,
         out_shape=[jax.ShapeDtypeStruct(shape, dtype) for shape, dtype in outs],
         in_specs=[
-            pl.BlockSpec(memory_space=spaces.get(i, pltpu.VMEM)) for i in range(len(args))
+            pl.BlockSpec(memory_space=pltpu.SMEM if i in smem else pltpu.VMEM)
+            for i in range(len(args))
         ],
         out_specs=[pl.BlockSpec(memory_space=pltpu.VMEM) for unused in outs],
-        scratch_shapes=[
-            pltpu.SemaphoreType.DMA if item is None else pltpu.VMEM(*item) for item in scratch
-        ],
+        scratch_shapes=[pltpu.VMEM(shape, dtype) for shape, dtype in scratch],
         compiler_params=pltpu.CompilerParams(vmem_limit_bytes=VMEM_LIMIT),
     )(*args)
 
@@ -438,19 +427,18 @@
     picked = ((elems * rows, slots), BF16)
 
     line = lambda array: array[None, :]
-    disp, diag = line(displacement), line(diagonal)
+    disp, diag = line(displacement.astype(F32)), line(diagonal)
     normal, fric, slip = line(normal_stiff), line(friction), line(slip_state)
-    owner = owner_map[0]
+    owner = owner_map[0].astype(F32)
     stacked = templates.reshape(3 * slots, slots)
 
-    joints = [normal_stiff, shear_stiff, friction, slip_state]
-
-    gram, a, b, owner = call(
+    coeffs = jnp.stack([normal_stiff, shear_stiff, slip_state.astype(F32) * friction * normal_stiff])
+
+    gram, a, b = call(
         begin_kernel,
-        [((devices, part, 128), F32), ((rows, depth), F32), ((rows, depth), F32), (owner.shape, owner.dtype)],
-        [None],
-        [sensitivity, owner],
-        anywhere=(1,),
+        [((devices, part, 128), F32), ((rows, depth), F32), ((rows, depth), F32)],
+        [],
+        [sensitivity],
     )
     a, b = exchanged(a, b)
     gram = everyones(gram)
@@ -459,8 +447,8 @@
         first_kernel,
         [wide, wide, taller, taller, ((rows, rows), F32), picked],
         [((count * rows, depth), BF16), ((count * rows, depth), F32)],
-        [gram, sensitivity, disp, a, b, diag, connectivity, owner, stacked] + joints,
-        smem=(9, 10, 11, 12),
+        [gram, sensitivity, disp, a, b, diag, connectivity, owner, coeffs, stacked],
+        smem=(8,),
     )
     a, b = exchanged(a, b)
     full, state, gram = call(
@@ -474,8 +462,8 @@
         second_kernel,
         [wide, wide, band, band, ((4, rows, rows), F32), picked, ((slots, 3 * elems), BF16)],
         [((count * rows + extra, depth), BF16), ((count * rows, depth), F32), ((elems, slots), F32)],
-        [gram, factor0, basis0, full, state, diag, connectivity, owner, stacked] + joints,
-        smem=(9, 10, 11, 12),
+        [gram, factor0, basis0, full, state, diag, connectivity, owner, coeffs, stacked],
+        smem=(8,),
     )
     a, b = exchanged(a, b)
     gram = call(late_kernel, [((3 * part, 128), F32)], [], [basis0, basis1, image, a, b])[0]

time: 88.1 us -> 86.6 us (0.983)
  transfers between devices with their start and end apart: 14 -> 14, of which waited for: 10 -> 9; matrix products, arithmetic and copies ran while one was open for 0% -> 0% of each run, Pallas kernels for 0% -> 0%
where the time goes in v4:
time: 86.6 us; the launch traced here: 86.3 us
  Pallas kernels  27.2 us (31%)
  starting transfers between devices  23.5 us (27%)
  blocking collectives  20.7 us (24%)
  waiting for transfers between devices  12.5 us (14%)
  local copies, waits for them, and re-layouts  1.65 us (2%)
    pallas_call x6, Pallas kernels, call(): pl.pallas_call(kernel, out_shape=[jax.ShapeDtypeStruct(shape, dtype) for...  27.2 us
    all_to_all x1, blocking collectives, everyones(): return lax.all_to_all(copies, AXIS, 0, 0, tiled=True)  20.7 us
    ppermute x7, starting transfers between devices, total(): parts.append(lax.ppermute(value, AXIS, route))  13.2 us
    all_to_all x1, starting transfers between devices, everyones(): return lax.all_to_all(copies, AXIS, 0, 0, tiled=True)  7.3 us
    all_to_all x1, waiting for transfers between devices, everyones(): return lax.all_to_all(copies, AXIS, 0, 0, tiled=True)  6.32 us
    ppermute x7, waiting for transfers between devices, total(): parts.append(lax.ppermute(value, AXIS, route))  5.41 us
    ppermute x6, starting transfers between devices, exchanged(): return (lax.ppermute(a, AXIS, first), lax.ppermute(b, AXIS, second))  2.99 us
  transfers between devices with their start and end apart: 14, of which 9 were waited for; matrix products, arithmetic and copies ran while one was open for 0% of the time, Pallas kernels for 0%

profile of v4, /device:TPU:0, one launch (start us, length us, event | category | flops | bytes accessed | tf_op | source)
XLA Modules:
  0.0 86.3 jit_solution(13360694294248860818)
XLA Ops:
  0.6 0.9 %copy-done = f32[32,2048]{1,0:T(8,128)S(1)} copy-done((f32[32,2048]{1,0:T(8,128)S(1)}, f32[32,2048]{1,0:T(8,128)}, u32[]{:S(2)}) %copy-start) | copy-done | bytes 262168
  1.6 1.1 %shard_map.113 = (f32[32,8,128]{2,1,0:T(8,128)}, f32[32,256]{1,0:T(8,128)S(1)}, f32[32,256]{1,0:T(8,128)S(1)}) custom-call(f32[32,2048]{1,0:T(8,128)S(1)} %copy-done), custom_call_target="tpu_custom_call" | custom-call | tf_op jit(solution)/shard_map/pallas_call | solution.py:368
  2.7 7.3 %all-to-all-start = ((f32[32,8,128]{2,1,0:T(8,128)}), f32[32,8,128]{2,1,0:T(8,128)S(1)}, u32[]{:S(2)}, u32[]{:S(2)}) async-start(f32[32,8,128]{2,1,0:T(8,128)} %get-tuple-element.21), calls=%async_computation | async-start | bytes 262144 | tf_op jit(solution)/shard_map/all_to_all | solution.py:390
  10.3 0.8 collective-permute-start.1
  11.2 0.6 copy-done.10
  11.9 6.3 %all-to-all-done.gram_ref = f32[32,8,128]{2,1,0:T(8,128)S(1)} async-done(((f32[32,8,128]{2,1,0:T(8,128)}), f32[32,8,128]{2,1,0:T(8,128)S(1)}, u32[]{:S(2)}, u32[]{:S(2)}) %all-to-all-start) | async-done | bytes 131104 | tf_op jit(solution)/shard_map/all_to_all | solution.py:390
  18.2 9.1 %shard_map.114 = (f32[32,2560]{1,0:T(8,128)S(1)}, f32[32,2560]{1,0:T(8,128)S(1)}, f32[40,512]{1,0:T(8,128)S(1)}, f32[40,512]{1,0:T(8,128)S(1)}, f32[32,32]{1,0:T(8,128)S(1)}, /*index=5*/bf16[4096,128]{1,0:T(8,128)(2,1)S(1)}) custom-call(f32[32,8,128]{2,1,0:T(8,128)S(1)} %all-to-all-done.gram_ref, f32[32,2048]{1,0:T(8,128)S(1)} %copy-done.1, ...), custom_call_target="tpu_custom_call" | custom-call | tf_op jit(solution)/shard_map/pallas_call | solution.py:368
  27.6 0.7 collective-permute-start.3
  28.7 0.7 shard_map.115
  29.3 20.7 %all_to_all.10.gram_ref = f32[32,16,128]{2,1,0:T(8,128)S(1)} all-to-all(f32[32,16,128]{2,1,0:T(8,128)S(1)} %get-tuple-element.28), channel_id=1, replica_groups=mesh['brick'=32] {'brick'}, dimensions={0} | all-to-all | bytes 524288 | tf_op jit(solution)/shard_map/all_to_all | solution.py:390
  50.0 10.3 %shard_map.116 = (f32[32,2560]{1,0:T(8,128)S(1)}, f32[32,2560]{1,0:T(8,128)S(1)}, f32[32,512]{1,0:T(8,128)S(1)}, f32[32,512]{1,0:T(8,128)S(1)}, f32[4,32,32]{2,1...) custom-call(f32[32,16,128]{2,1,0:T(8,128)S(1)} %all_to_all.10.gram_ref, ...), custom_call_target="tpu_custom_call" | custom-call | tf_op jit(solution)/shard_map/pallas_call | solution.py:368
  60.4 0.9 %collective-permute-start.5 = (f32[32,512]{1,0:T(8,128)S(1)}, f32[32,512]{1,0:T(8,128)S(1)}, u32[]{:S(2)}, u32[]{:S(2)}) collective-permute-start(f32[32,512]{1,0:T(8,128)S(1)} %get-tuple-element.35), channel_id=1, source_target_pairs={{1,2},{2,1},{3,4},{4,3},{5,6},{6,5},{7,8},{8,7},{9,10},{10,9},{11,... | collective-permute-start | bytes 196616 | tf_op jit(solution)/shard_map/ppermute | solution.py:386
  61.6 0.8 shard_map.117
  62.5 5.2 %collective-permute-start.6 = (f32[24,128]{1,0:T(8,128)S(1)}, f32[24,128]{1,0:T(8,128)S(1)}, u32[]{:S(2)}, u32[]{:S(2)}) collective-permute-start(f32[24,128]{1,0:T(8,128)S(1)} %shard_map.117), channel_id=1, source_target_pairs={{0,1},{1,0},{2,3},{3,2},{4,5},{5,4},{6,7},{7,6},{8,9},{9,8},{10,11... | collective-permute-start | bytes 36872 | tf_op jit(solution)/shard_map/ppermute | solution.py:405
  67.7 0.8 collective-permute-done.6
  68.5 2.6 %collective-permute-start.9 = (f32[24,128]{1,0:T(8,128)S(1)}, f32[24,128]{1,0:T(8,128)S(1)}, u32[]{:S(2)}, u32[]{:S(2)}) collective-permute-start(f32[24,128]{1,0:T(8,128)S(1)} %add.21), channel_id=1, source_target_pairs={{0,6},{1,7},{2,4},{3,5},{4,2},{5,3},{6,0},{7,1},{8,14},{9,15},{10,... | collective-permute-start | bytes 36872 | tf_op jit(solution)/shard_map/ppermute | solution.py:405
  71.2 0.9 %collective-permute-start.7 = (f32[24,128]{1,0:T(8,128)S(1)}, f32[24,128]{1,0:T(8,128)S(1)}, u32[]{:S(2)}, u32[]{:S(2)}) collective-permute-start(f32[24,128]{1,0:T(8,128)S(1)} %add.21), channel_id=1, source_target_pairs={{0,2},{1,3},{2,0},{3,1},{4,6},{5,7},{6,4},{7,5},{8,10},{9,11},{10,... | collective-permute-start | bytes 36872 | tf_op jit(solution)/shard_map/ppermute | solution.py:405
  72.0 1.1 %collective-permute-done.9 = f32[24,128]{1,0:T(8,128)S(1)} collective-permute-done((f32[24,128]{1,0:T(8,128)S(1)}, f32[24,128]{1,0:T(8,128)S(1)}, u32[]{:S(2)}, u32[]{:S(2)}) %collective-permute-start.9) | collective-permute-done | bytes 12320 | tf_op jit(solution)/shard_map/ppermute | solution.py:405
  73.1 1.7 %collective-permute-done.8 = f32[24,128]{1,0:T(8,128)S(1)} collective-permute-done((f32[24,128]{1,0:T(8,128)S(1)}, f32[24,128]{1,0:T(8,128)S(1)}, u32[]{:S(2)}, u32[]{:S(2)}) %collective-permute-start.8) | collective-permute-done | bytes 12320 | tf_op jit(solution)/shard_map/ppermute | solution.py:405
  74.9 1.5 %collective-permute-start.12 = (f32[24,128]{1,0:T(8,128)S(1)}, f32[24,128]{1,0:T(8,128)S(1)}, u32[]{:S(2)}, u32[]{:S(2)}) collective-permute-start(f32[24,128]{1,0:T(8,128)S(1)} %add_add_fusion.1), channel_id=1, source_target_pairs={{0,24},{1,25},{2,26},{3,27},{4,28},{5,29},{6,30},{7,31},{8,16},{9,... | collective-permute-start | bytes 36872 | tf_op jit(solution)/shard_map/ppermute | solution.py:405
  76.3 1.0 %collective-permute-start.11 = (f32[24,128]{1,0:T(8,128)S(1)}, f32[24,128]{1,0:T(8,128)S(1)}, u32[]{:S(2)}, u32[]{:S(2)}) collective-permute-start(f32[24,128]{1,0:T(8,128)S(1)} %add_add_fusion.1), channel_id=1, source_target_pairs={{0,16},{1,17},{2,18},{3,19},{4,20},{5,21},{6,22},{7,23},{8,24},{9,... | collective-permute-start | bytes 36872 | tf_op jit(solution)/shard_map/ppermute | solution.py:405
  77.4 1.9 %collective-permute-start.10 = (f32[24,128]{1,0:T(8,128)S(1)}, f32[24,128]{1,0:T(8,128)S(1)}, u32[]{:S(2)}, u32[]{:S(2)}) collective-permute-start(f32[24,128]{1,0:T(8,128)S(1)} %add_add_fusion.1), channel_id=1, source_target_pairs={{0,8},{1,9},{2,10},{3,11},{4,12},{5,13},{6,14},{7,15},{8,0},{9,1},... | collective-permute-start | bytes 36872 | tf_op jit(solution)/shard_map/ppermute | solution.py:405
  79.3 1.1 %collective-permute-done.12 = f32[24,128]{1,0:T(8,128)S(1)} collective-permute-done((f32[24,128]{1,0:T(8,128)S(1)}, f32[24,128]{1,0:T(8,128)S(1)}, u32[]{:S(2)}, u32[]{:S(2)}) %collective-permute-start.12) | collective-permute-done | bytes 12320 | tf_op jit(solution)/shard_map/ppermute | solution.py:405
  81.1 5.2 %shard_map.118 = (f32[32,2048]{1,0:T(8,128)}, f32[3,32,128]{2,1,0:T(8,128)}) custom-call(f32[24,128]{1,0:T(8,128)S(1)} %add_add_fusion.gram_ref, f32[32,32]{1,0:T(8,128)S(1)} %get-tuple-element.29.factor0_ref, f32[4,32,32]{2,1,0:T(8,128)S(1)} %get-tuple-element.36.small_ref, f32[32,2560]{1,0:T(8,128)S(1)} %get-tuple-element.24.basis_ref.basis0_ref, ...), custom_call_target="tpu_custom_call" | custom-call | tf_op jit(solution)/shard_map/pallas_call | solution.py:368
  (40 shorter events, 2.3 us)
Async XLA Ops:
  0.6 1.0 %copy-start = (f32[32,2048]{1,0:T(8,128)S(1)}, f32[32,2048]{1,0:T(8,128)}, u32[]{:S(2)}) copy-start(f32[32,2048]{1,0:T(8,128)} %sens_ref.3) | copy-start | bytes 786436
  1.6 16.6 %copy-start.1 = (f32[32,2048]{1,0:T(8,128)S(1)}, f32[32,2048]{1,0:T(8,128)}, u32[]{:S(2)}) copy-start(f32[32,2048]{1,0:T(8,128)} %sens_ref.3) | copy-start | bytes 786436
  2.7 15.5 %copy-start.2 = (bf16[3,128,128]{2,1,0:T(8,128)(2,1)S(1)}, bf16[3,128,128]{2,1,0:T(8,128)(2,1)}, u32[]{:S(2)}) copy-start(bf16[3,128,128]{2,1,0:T(8,128)(2,1)} %param.19) | copy-start | bytes 294916
  2.7 15.5 %copy-start.3 = (s32[128,128]{1,0:T(8,128)S(1)}, s32[128,128]{1,0:T(8,128)}, u32[]{:S(2)}) copy-start(s32[128,128]{1,0:T(8,128)} %conn_ref.3) | copy-start | bytes 196612
  2.7 15.5 %all-to-all-start = ((f32[32,8,128]{2,1,0:T(8,128)}), f32[32,8,128]{2,1,0:T(8,128)S(1)}, u32[]{:S(2)}, u32[]{:S(2)}) async-start(f32[32,8,128]{2,1,0:T(8,128)} %get-tuple-element.21), calls=%async_computation | async-start | bytes 262144 | tf_op jit(solution)/shard_map/all_to_all | solution.py:390
  10.0 1.1 %copy-start.9 = (s32[1,2,256]{2,1,0:T(2,128)S(1)}, s32[1,2,256]{2,1,0:T(2,128)}, u32[]{:S(2)}) copy-start(s32[1,2,256]{2,1,0:T(2,128)} %param.18) | copy-start | bytes 6148
  10.0 1.9 %collective-permute-start = (f32[32,256]{1,0:T(8,128)S(1)}, f32[32,256]{1,0:T(8,128)S(1)}, u32[]{:S(2)}, u32[]{:S(2)}) collective-permute-start(f32[32,256]{1,0:T(8,128)S(1)} %get-tuple-element.22), channel_id=1, source_target_pairs={{0,1},{1,0},{2,3},{3,2},{4,5},{5,4},{6,7},{7,6},{8,9},{9,8},{10,11... | collective-permute-start | bytes 98312 | tf_op jit(solution)/shard_map/ppermute | solution.py:386
  10.3 0.8 copy-start.5
  10.3 0.8 copy-start.6
  10.3 0.8 copy-start.7
  10.3 1.6 %collective-permute-start.1 = (f32[32,256]{1,0:T(8,128)S(1)}, f32[32,256]{1,0:T(8,128)S(1)}, u32[]{:S(2)}, u32[]{:S(2)}) collective-permute-start(f32[32,256]{1,0:T(8,128)S(1)} %get-tuple-element.23), channel_id=1, source_target_pairs={{1,2},{2,1},{3,4},{4,3},{5,6},{6,5},{7,8},{8,7},{9,10},{10,9},{11,... | collective-permute-start | bytes 98312 | tf_op jit(solution)/shard_map/ppermute | solution.py:386
  11.2 0.7 copy-start.8
  11.9 6.3 %copy-start.4 = (f32[2048]{0:T(1024)S(1)}, f32[2048]{0:T(1024)}, u32[]{:S(2)}) copy-start(f32[2048]{0:T(1024)} %param.11) | copy-start | bytes 24580
  27.3 1.3 %collective-permute-start.2 = (f32[40,512]{1,0:T(8,128)S(1)}, f32[40,512]{1,0:T(8,128)S(1)}, u32[]{:S(2)}, u32[]{:S(2)}) collective-permute-start(f32[40,512]{1,0:T(8,128)S(1)} %get-tuple-element.26), channel_id=1, source_target_pairs={{0,1},{1,0},{2,3},{3,2},{4,5},{5,4},{6,7},{7,6},{8,9},{9,8},{10,11... | collective-permute-start | bytes 245768 | tf_op jit(solution)/shard_map/ppermute | solution.py:386
  27.6 1.1 %collective-permute-start.3 = (f32[40,512]{1,0:T(8,128)S(1)}, f32[40,512]{1,0:T(8,128)S(1)}, u32[]{:S(2)}, u32[]{:S(2)}) collective-permute-start(f32[40,512]{1,0:T(8,128)S(1)} %get-tuple-element.27), channel_id=1, source_target_pairs={{1,2},{2,1},{3,4},{4,3},{5,6},{6,5},{7,8},{8,7},{9,10},{10,9},{11,... | collective-permute-start | bytes 245768 | tf_op jit(solution)/shard_map/ppermute | solution.py:386
  60.3 1.3 %collective-permute-start.4 = (f32[32,512]{1,0:T(8,128)S(1)}, f32[32,512]{1,0:T(8,128)S(1)}, u32[]{:S(2)}, u32[]{:S(2)}) collective-permute-start(f32[32,512]{1,0:T(8,128)S(1)} %get-tuple-element.34), channel_id=1, source_target_pairs={{0,1},{1,0},{2,3},{3,2},{4,5},{5,4},{6,7},{7,6},{8,9},{9,8},{10,11... | collective-permute-start | bytes 196616 | tf_op jit(solution)/shard_map/ppermute | solution.py:386
  60.4 1.2 %collective-permute-start.5 = (f32[32,512]{1,0:T(8,128)S(1)}, f32[32,512]{1,0:T(8,128)S(1)}, u32[]{:S(2)}, u32[]{:S(2)}) collective-permute-start(f32[32,512]{1,0:T(8,128)S(1)} %get-tuple-element.35), channel_id=1, source_target_pairs={{1,2},{2,1},{3,4},{4,3},{5,6},{6,5},{7,8},{8,7},{9,10},{10,9},{11,... | collective-permute-start | bytes 196616 | tf_op jit(solution)/shard_map/ppermute | solution.py:386
  62.5 6.1 %collective-permute-start.6 = (f32[24,128]{1,0:T(8,128)S(1)}, f32[24,128]{1,0:T(8,128)S(1)}, u32[]{:S(2)}, u32[]{:S(2)}) collective-permute-start(f32[24,128]{1,0:T(8,128)S(1)} %shard_map.117), channel_id=1, source_target_pairs={{0,1},{1,0},{2,3},{3,2},{4,5},{5,4},{6,7},{7,6},{8,9},{9,8},{10,11... | collective-permute-start | bytes 36872 | tf_op jit(solution)/shard_map/ppermute | solution.py:405
  68.5 4.6 %collective-permute-start.9 = (f32[24,128]{1,0:T(8,128)S(1)}, f32[24,128]{1,0:T(8,128)S(1)}, u32[]{:S(2)}, u32[]{:S(2)}) collective-permute-start(f32[24,128]{1,0:T(8,128)S(1)} %add.21), channel_id=1, source_target_pairs={{0,6},{1,7},{2,4},{3,5},{4,2},{5,3},{6,0},{7,1},{8,14},{9,15},{10,... | collective-permute-start | bytes 36872 | tf_op jit(solution)/shard_map/ppermute | solution.py:405
  71.2 3.7 %collective-permute-start.8 = (f32[24,128]{1,0:T(8,128)S(1)}, f32[24,128]{1,0:T(8,128)S(1)}, u32[]{:S(2)}, u32[]{:S(2)}) collective-permute-start(f32[24,128]{1,0:T(8,128)S(1)} %add.21), channel_id=1, source_target_pairs={{0,4},{1,5},{2,6},{3,7},{4,0},{5,1},{6,2},{7,3},{8,12},{9,13},{10,... | collective-permute-start | bytes 36872 | tf_op jit(solution)/shard_map/ppermute | solution.py:405
  71.2 3.7 %collective-permute-start.7 = (f32[24,128]{1,0:T(8,128)S(1)}, f32[24,128]{1,0:T(8,128)S(1)}, u32[]{:S(2)}, u32[]{:S(2)}) collective-permute-start(f32[24,128]{1,0:T(8,128)S(1)} %add.21), channel_id=1, source_target_pairs={{0,2},{1,3},{2,0},{3,1},{4,6},{5,7},{6,4},{7,5},{8,10},{9,11},{10,... | collective-permute-start | bytes 36872 | tf_op jit(solution)/shard_map/ppermute | solution.py:405
  74.9 5.6 %collective-permute-start.12 = (f32[24,128]{1,0:T(8,128)S(1)}, f32[24,128]{1,0:T(8,128)S(1)}, u32[]{:S(2)}, u32[]{:S(2)}) collective-permute-start(f32[24,128]{1,0:T(8,128)S(1)} %add_add_fusion.1), channel_id=1, source_target_pairs={{0,24},{1,25},{2,26},{3,27},{4,28},{5,29},{6,30},{7,31},{8,16},{9,... | collective-permute-start | bytes 36872 | tf_op jit(solution)/shard_map/ppermute | solution.py:405
  76.3 4.6 %collective-permute-start.11 = (f32[24,128]{1,0:T(8,128)S(1)}, f32[24,128]{1,0:T(8,128)S(1)}, u32[]{:S(2)}, u32[]{:S(2)}) collective-permute-start(f32[24,128]{1,0:T(8,128)S(1)} %add_add_fusion.1), channel_id=1, source_target_pairs={{0,16},{1,17},{2,18},{3,19},{4,20},{5,21},{6,22},{7,23},{8,24},{9,... | collective-permute-start | bytes 36872 | tf_op jit(solution)/shard_map/ppermute | solution.py:405
  77.4 3.7 %collective-permute-start.10 = (f32[24,128]{1,0:T(8,128)S(1)}, f32[24,128]{1,0:T(8,128)S(1)}, u32[]{:S(2)}, u32[]{:S(2)}) collective-permute-start(f32[24,128]{1,0:T(8,128)S(1)} %add_add_fusion.1), channel_id=1, source_target_pairs={{0,8},{1,9},{2,10},{3,11},{4,12},{5,13},{6,14},{7,15},{8,0},{9,1},... | collective-permute-start | bytes 36872 | tf_op jit(solution)/shard_map/ppermute | solution.py:405
  (1 other events, 0.7 us)

commit v5 on v4

--- a/solution.py
+++ b/solution.py
@@ -5,6 +5,7 @@
 from jax.experimental.pallas import tpu as pltpu
 from jax.sharding import PartitionSpec as P
 
+PARTS = 2
 CHUNK = 16
 PIVOTS = 16
 VMEM_LIMIT = 48 * 1024 * 1024
@@ -59,6 +60,47 @@
     n = int((tile.shape[0] * 128) ** 0.5)
     fold = 128 // n
     return jnp.concatenate([tile[:, j * n : (j + 1) * n] for j in range(fold)], axis=0)
+
+
+def packed_symmetric(square):
+    n = square.shape[0]
+    half = n // 2
+    first, second, cross = square[:half, :half], square[half:, half:], square[half:, :half]
+    row_id = lax.broadcasted_iota(jnp.int32, (half, half), 0)
+    col_id = lax.broadcasted_iota(jnp.int32, (half, half), 1)
+    both = jnp.concatenate([jnp.where(row_id >= col_id, first, second), cross], axis=1)
+    fold = 128 // n
+    part = half // fold
+    diag = jnp.sum(jnp.where(row_id == col_id, second, 0.0), axis=0, keepdims=True)
+    return jnp.concatenate(
+        [
+            jnp.concatenate([both[j * part : (j + 1) * part, :] for j in range(fold)], axis=1),
+            jnp.concatenate([diag, jnp.zeros((1, 128 - half), F32)], axis=1),
+        ],
+        axis=0,
+    )
+
+
+def unpacked_symmetric(tile, n):
+    half = n // 2
+    fold = 128 // n
+    part = half // fold
+    both = jnp.concatenate([tile[:part, j * n : (j + 1) * n] for j in range(fold)], axis=0)
+    same = lax.broadcasted_iota(jnp.int32, (n, n), 0) == lax.broadcasted_iota(jnp.int32, (n, n), 1)
+    flipped = fdot(jnp.where(same, 1.0, 0.0).astype(F32), both, NT)
+    mixed, cross = both[:, :half], both[:, half:]
+    row_id = lax.broadcasted_iota(jnp.int32, (half, half), 0)
+    col_id = lax.broadcasted_iota(jnp.int32, (half, half), 1)
+    first = jnp.where(row_id >= col_id, mixed, flipped[:half])
+    second = jnp.where(row_id < col_id, mixed, flipped[:half])
+    second = jnp.where(row_id == col_id, jnp.broadcast_to(tile[part : part + 1, :half], (half, half)), second)
+    return jnp.concatenate(
+        [
+            jnp.concatenate([first, flipped[half:]], axis=1),
+            jnp.concatenate([cross, second], axis=1),
+        ],
+        axis=0,
+    )
 
 
 def tall(row, count):
@@ -249,8 +291,10 @@
     own = own_part(full, depth)
     rows = own.shape[0]
     both = fdot(jnp.concatenate([own_part(basis_ref[...], depth), own], axis=0), own, NT)
-    tile = jnp.concatenate([packed(both[:rows]), packed(both[rows:])], axis=0)
-    gram_ref[...] = jnp.broadcast_to(tile[None], gram_ref.shape)
+    tile = jnp.concatenate([packed(both[:rows]), packed_symmetric(both[rows:])], axis=0)
+    copies = gram_ref.shape[0]
+    for r in range(tile.shape[0]):
+        gram_ref[:, r] = jnp.broadcast_to(tile[r : r + 1, :][None], (copies, 1, 128))
 
 
 def second_kernel(
@@ -260,9 +304,11 @@
     tiles_ref, total_ref, state_ref,
 ):
     elems, slots = conn_ref.shape
-    tile = jnp.sum(gram_ref[...], axis=0)
-    part = tile.shape[0] // 2
-    proj, square = unpacked(tile[:part]), unpacked(tile[part:])
+    summed = jnp.sum(gram_ref[...], axis=0)
+    tile = jnp.concatenate([summed[r] for r in range(summed.shape[0])], axis=0)
+    n = basis0_ref.shape[0]
+    part = n * n // 128
+    proj, square = unpacked(tile[:part]), unpacked_symmetric(tile[part:], n)
     inverse, factor = lower_inverse(square - fdot(proj, proj, TN))
     head, unused = lower_inverse(square)
     reduced = full_ref[...] - fdot(proj, basis0_ref[...], TN)
@@ -279,9 +325,10 @@
     write_image(basis, parts, diag_ref, image_ref, a_ref, b_ref)
     moved = state_ref[...].astype(BF16)
     for k in range(3):
-        push_ref[:, k * elems : (k + 1) * elems] = bdot(
-            stacked_ref[k * slots : (k + 1) * slots, :], moved, NT
-        ).astype(BF16)
+        pushed = bdot(stacked_ref[k * slots : (k + 1) * slots, :], moved, NT).astype(BF16)
+        for part in range(PARTS):
+            group = elems // PARTS
+            push_ref[part, :, k * group : (k + 1) * group] = pushed[:, part * group : (part + 1) * group]
 
 
 def late_kernel(basis0_ref, basis1_ref, image_ref, a_in, b_in, gram_ref):
@@ -309,7 +356,7 @@
 
 def last_kernel(
     gram_ref, factor0_ref, small_ref, basis0_ref, basis1_ref, values0_ref, values1_ref, push_ref,
-    normal_ref, friction_ref, slip_ref, adjoint_ref, grads_ref, pairs_ref,
+    normal_ref, friction_ref, slip_ref, adjoint_ref, grads_ref,
 ):
     rows, width = basis0_ref.shape
     depth = (width - adjoint_ref.shape[1]) // 2
@@ -322,10 +369,9 @@
     cross = fdot(small_ref[1], p01) + fdot(small_ref[2], p11)
     tail, unused = lower_inverse(n11 - fdot(cross, cross, TN))
     tail_side = fdot(tail, fdot(p01, upper0, TN) - fdot(cross, head_side, TN))
-    w1 = fdot(tail, tail_side, TN)
-    turned = jnp.concatenate(
-        [fdot(head_side - fdot(cross, w1), head, TN), fdot(tail_side, tail, TN)], axis=1
-    )
+    w1_turned = fdot(tail_side, tail, TN)
+    w0_turned = fdot(head_side, head, TN) - fdot(w1_turned, fdot(head, cross, TN), NT)
+    turned = jnp.concatenate([w0_turned, w1_turned], axis=1)
     adjoint_ref[...] = fdot(
         turned,
         jnp.concatenate(
@@ -333,35 +379,36 @@
         ),
     )
     weights = split3(turned)
-    pairs_ref[...] = jnp.zeros_like(pairs_ref)
-    lane = lax.broadcasted_iota(jnp.int32, (rows, 3 * elems), 1) % elems
-
-    def chunk(step, carry):
-        start = pl.multiple_of(step * CHUNK, CHUNK)
-        fields = []
-        for ref in (values0_ref, values1_ref):
-            block = ref[pl.ds(pl.multiple_of(start * rows, rows), CHUNK * rows), :]
-            fields.append(
-                jnp.concatenate([block[e * rows : (e + 1) * rows, :] for e in range(CHUNK)], axis=1)
+    group = elems // PARTS
+    lane = lax.broadcasted_iota(jnp.int32, (rows, 3 * group), 1) % group
+    found = []
+    for part in range(PARTS):
+        pairs = jnp.zeros((rows, 3 * group), F32)
+        for start in range(part * group, (part + 1) * group, CHUNK):
+            fields = []
+            for ref in (values0_ref, values1_ref):
+                block = ref[start * rows : (start + CHUNK) * rows, :]
+                fields.append(
+                    jnp.concatenate([block[e * rows : (e + 1) * rows, :] for e in range(CHUNK)], axis=1)
+                )
+            mixed = bdot(weights, jnp.concatenate(fields, axis=0))
+            mixed = (mixed[:rows] + (mixed[rows : 2 * rows] + mixed[2 * rows :])).astype(BF16)
+            every = bdot(
+                jnp.concatenate([mixed[:, e * slots : (e + 1) * slots] for e in range(CHUNK)], axis=0),
+                push_ref[part],
             )
-        mixed = bdot(weights, jnp.concatenate(fields, axis=0))
-        mixed = (mixed[:rows] + (mixed[rows : 2 * rows] + mixed[2 * rows :])).astype(BF16)
-        every = bdot(
-            jnp.concatenate([mixed[:, e * slots : (e + 1) * slots] for e in range(CHUNK)], axis=0),
-            push_ref[...],
-        )
-        pairs = pairs_ref[...]
-        for e in range(CHUNK):
-            pairs = jnp.where(lane == start + e, every[e * rows : (e + 1) * rows, :], pairs)
-        pairs_ref[...] = pairs
-        return carry
-
-    lax.fori_loop(0, elems // CHUNK, chunk, 0, unroll=True)
-    third = pairs_ref[:, 2 * elems :]
+            for e in range(CHUNK):
+                at = start - part * group + e
+                pairs = jnp.where(lane == at, every[e * rows : (e + 1) * rows, :], pairs)
+        found.append(pairs)
+    pairs = [
+        jnp.concatenate([part[:, k * group : (k + 1) * group] for part in found], axis=1)
+        for k in range(3)
+    ]
     slip = slip_ref[...].astype(F32)
-    grads_ref[0] = -(pairs_ref[:, :elems] + slip * friction_ref[...] * third)
-    grads_ref[1] = -pairs_ref[:, elems : 2 * elems]
-    grads_ref[2] = -slip * normal_ref[...] * third
+    grads_ref[0] = -(pairs[0] + slip * friction_ref[...] * pairs[2])
+    grads_ref[1] = -pairs[1]
+    grads_ref[2] = -slip * normal_ref[...] * pairs[2]
 
 
 def call(kernel, outs, scratch, args, smem=()):
@@ -453,14 +500,14 @@
     a, b = exchanged(a, b)
     full, state, gram = call(
         middle_kernel,
-        [wide, ((1, width), F32), ((devices, 2 * part, 128), F32)],
+        [wide, ((1, width), F32), ((devices, part + part // 2 + 1, 1, 128), F32)],
         [],
         [basis0, image, disp, a, b],
     )
     gram = everyones(gram)
     basis1, image, a, b, small, values1, pushed = call(
         second_kernel,
-        [wide, wide, band, band, ((4, rows, rows), F32), picked, ((slots, 3 * elems), BF16)],
+        [wide, wide, band, band, ((4, rows, rows), F32), picked, ((PARTS, slots, 3 * elems // PARTS), BF16)],
         [((count * rows + extra, depth), BF16), ((count * rows, depth), F32), ((elems, slots), F32)],
         [gram, factor0, basis0, full, state, diag, connectivity, owner, coeffs, stacked],
         smem=(8,),
@@ -471,7 +518,7 @@
     adjoint, grads = call(
         last_kernel,
         [((rows, owned), F32), ((3, rows, elems), F32)],
-        [((rows, 3 * elems), F32)],
+        [],
         [gram, factor0, small, basis0, basis1, values0, values1, pushed, normal, fric, slip],
     )
     return adjoint, grads

time: 86.6 us -> 85.5 us (0.987)
  blocking collectives: 20.7 us -> 19.5 us
    all_to_all x1, blocking collectives: 20.7 us -> 19.5 us  [everyones(): return lax.all_to_all(copies, AXIS, 0, 0, tiled=True)]
  transfers between devices with their start and end apart: 14 -> 14, of which waited for: 9 -> 7; matrix products, arithmetic and copies ran while one was open for 0% -> 0% of each run, Pallas kernels for 0% -> 0%
where the time goes in v5:
time: 85.5 us; the launch traced here: 85.2 us
  Pallas kernels  27.1 us (32%)
  starting transfers between devices  23.8 us (28%)
  blocking collectives  19.5 us (23%)
  waiting for transfers between devices  12.4 us (15%)
  local copies, waits for them, and re-layouts  1.65 us (2%)
    pallas_call x6, Pallas kernels, call(): pl.pallas_call(kernel, out_shape=[jax.ShapeDtypeStruct(shape, dtype) for...  27.1 us
    all_to_all x1, blocking collectives, everyones(): return lax.all_to_all(copies, AXIS, 0, 0, tiled=True)  19.5 us
    ppermute x7, starting transfers between devices, total(): parts.append(lax.ppermute(value, AXIS, route))  13.2 us
    all_to_all x1, starting transfers between devices, everyones(): return lax.all_to_all(copies, AXIS, 0, 0, tiled=True)  7.3 us
    all_to_all x1, waiting for transfers between devices, everyones(): return lax.all_to_all(copies, AXIS, 0, 0, tiled=True)  6.32 us
    ppermute x7, waiting for transfers between devices, total(): parts.append(lax.ppermute(value, AXIS, route))  5.62 us
    ppermute x6, starting transfers between devices, exchanged(): return (lax.ppermute(a, AXIS, first), lax.ppermute(b, AXIS, second))  3.33 us
  transfers between devices with their start and end apart: 14, of which 7 were waited for; matrix products, arithmetic and copies ran while one was open for 0% of the time, Pallas kernels for 0%

profile of v5, /device:TPU:0, one launch (start us, length us, event | category | flops | bytes accessed | tf_op | source)
XLA Modules:
  0.0 85.2 jit_solution(3180999792398543578)
XLA Ops:
  0.6 0.9 %copy-done = f32[32,2048]{1,0:T(8,128)S(1)} copy-done((f32[32,2048]{1,0:T(8,128)S(1)}, f32[32,2048]{1,0:T(8,128)}, u32[]{:S(2)}) %copy-start) | copy-done | bytes 262168
  1.6 1.1 %shard_map.113 = (f32[32,8,128]{2,1,0:T(8,128)}, f32[32,256]{1,0:T(8,128)S(1)}, f32[32,256]{1,0:T(8,128)S(1)}) custom-call(f32[32,2048]{1,0:T(8,128)S(1)} %copy-done), custom_call_target="tpu_custom_call" | custom-call | tf_op jit(solution)/shard_map/pallas_call | solution.py:415
  2.7 7.3 %all-to-all-start = ((f32[32,8,128]{2,1,0:T(8,128)}), f32[32,8,128]{2,1,0:T(8,128)S(1)}, u32[]{:S(2)}, u32[]{:S(2)}) async-start(f32[32,8,128]{2,1,0:T(8,128)} %get-tuple-element.21), calls=%async_computation | async-start | bytes 262144 | tf_op jit(solution)/shard_map/all_to_all | solution.py:437
  10.3 0.8 collective-permute-start.1
  11.9 6.3 %all-to-all-done.gram_ref = f32[32,8,128]{2,1,0:T(8,128)S(1)} async-done(((f32[32,8,128]{2,1,0:T(8,128)}), f32[32,8,128]{2,1,0:T(8,128)S(1)}, u32[]{:S(2)}, u32[]{:S(2)}) %all-to-all-start) | async-done | bytes 131104 | tf_op jit(solution)/shard_map/all_to_all | solution.py:437
  18.2 9.1 %shard_map.114 = (f32[32,2560]{1,0:T(8,128)S(1)}, f32[32,2560]{1,0:T(8,128)S(1)}, f32[40,512]{1,0:T(8,128)S(1)}, f32[40,512]{1,0:T(8,128)S(1)}, f32[32,32]{1,0:T(8,128)S(1)}, /*index=5*/bf16[4096,128]{1,0:T(8,128)(2,1)S(1)}) custom-call(f32[32,8,128]{2,1,0:T(8,128)S(1)} %all-to-all-done.gram_ref, f32[32,2048]{1,0:T(8,128)S(1)} %copy-done.1, ...), custom_call_target="tpu_custom_call" | custom-call | tf_op jit(solution)/shard_map/pallas_call | solution.py:415
  27.6 0.7 collective-permute-start.3
  28.7 0.7 shard_map.115
  29.4 19.5 %all_to_all.10.gram_ref = f32[32,13,1,128]{3,2,1,0:T(1,128)S(1)} all-to-all(f32[32,13,1,128]{3,2,1,0:T(1,128)S(1)} %get-tuple-element.28), channel_id=1, replica_groups=mesh['brick'=32] {'brick'}, dimensions={0} | all-to-all | bytes 425984 | tf_op jit(solution)/shard_map/all_to_all | solution.py:437
  48.9 10.7 %shard_map.116 = (f32[32,2560]{1,0:T(8,128)S(1)}, f32[32,2560]{1,0:T(8,128)S(1)}, f32[32,512]{1,0:T(8,128)S(1)}, f32[32,512]{1,0:T(8,128)S(1)}, f32[4,32,32]{2,1...) custom-call(f32[32,13,1,128]{3,2,1,0:T(1,128)S(1)} %all_to_all.10.gram_ref, ...), custom_call_target="tpu_custom_call" | custom-call | tf_op jit(solution)/shard_map/pallas_call | solution.py:415
  60.0 0.9 %collective-permute-start.5 = (f32[32,512]{1,0:T(8,128)S(1)}, f32[32,512]{1,0:T(8,128)S(1)}, u32[]{:S(2)}, u32[]{:S(2)}) collective-permute-start(f32[32,512]{1,0:T(8,128)S(1)} %get-tuple-element.35), channel_id=1, source_target_pairs={{1,2},{2,1},{3,4},{4,3},{5,6},{6,5},{7,8},{8,7},{9,10},{10,9},{11,... | collective-permute-start | bytes 196616 | tf_op jit(solution)/shard_map/ppermute | solution.py:433
  60.9 0.8 shard_map.117
  61.7 5.2 %collective-permute-start.6 = (f32[24,128]{1,0:T(8,128)S(1)}, f32[24,128]{1,0:T(8,128)S(1)}, u32[]{:S(2)}, u32[]{:S(2)}) collective-permute-start(f32[24,128]{1,0:T(8,128)S(1)} %shard_map.117), channel_id=1, source_target_pairs={{0,1},{1,0},{2,3},{3,2},{4,5},{5,4},{6,7},{7,6},{8,9},{9,8},{10,11... | collective-permute-start | bytes 36872 | tf_op jit(solution)/shard_map/ppermute | solution.py:452
  67.0 0.8 collective-permute-done.6
  67.8 2.8 %collective-permute-start.9 = (f32[24,128]{1,0:T(8,128)S(1)}, f32[24,128]{1,0:T(8,128)S(1)}, u32[]{:S(2)}, u32[]{:S(2)}) collective-permute-start(f32[24,128]{1,0:T(8,128)S(1)} %add.21), channel_id=1, source_target_pairs={{0,6},{1,7},{2,4},{3,5},{4,2},{5,3},{6,0},{7,1},{8,14},{9,15},{10,... | collective-permute-start | bytes 36872 | tf_op jit(solution)/shard_map/ppermute | solution.py:452
  70.6 0.7 collective-permute-start.7
  71.3 1.1 %collective-permute-done.9 = f32[24,128]{1,0:T(8,128)S(1)} collective-permute-done((f32[24,128]{1,0:T(8,128)S(1)}, f32[24,128]{1,0:T(8,128)S(1)}, u32[]{:S(2)}, u32[]{:S(2)}) %collective-permute-start.9) | collective-permute-done | bytes 12320 | tf_op jit(solution)/shard_map/ppermute | solution.py:452
  72.4 1.9 %collective-permute-done.8 = f32[24,128]{1,0:T(8,128)S(1)} collective-permute-done((f32[24,128]{1,0:T(8,128)S(1)}, f32[24,128]{1,0:T(8,128)S(1)}, u32[]{:S(2)}, u32[]{:S(2)}) %collective-permute-start.8) | collective-permute-done | bytes 12320 | tf_op jit(solution)/shard_map/ppermute | solution.py:452
  74.3 1.6 %collective-permute-start.12 = (f32[24,128]{1,0:T(8,128)S(1)}, f32[24,128]{1,0:T(8,128)S(1)}, u32[]{:S(2)}, u32[]{:S(2)}) collective-permute-start(f32[24,128]{1,0:T(8,128)S(1)} %add_add_fusion.1), channel_id=1, source_target_pairs={{0,24},{1,25},{2,26},{3,27},{4,28},{5,29},{6,30},{7,31},{8,16},{9,... | collective-permute-start | bytes 36872 | tf_op jit(solution)/shard_map/ppermute | solution.py:452
  75.9 0.8 collective-permute-start.11
  76.7 2.0 %collective-permute-start.10 = (f32[24,128]{1,0:T(8,128)S(1)}, f32[24,128]{1,0:T(8,128)S(1)}, u32[]{:S(2)}, u32[]{:S(2)}) collective-permute-start(f32[24,128]{1,0:T(8,128)S(1)} %add_add_fusion.1), channel_id=1, source_target_pairs={{0,8},{1,9},{2,10},{3,11},{4,12},{5,13},{6,14},{7,15},{8,0},{9,1},... | collective-permute-start | bytes 36872 | tf_op jit(solution)/shard_map/ppermute | solution.py:452
  78.7 1.1 %collective-permute-done.12 = f32[24,128]{1,0:T(8,128)S(1)} collective-permute-done((f32[24,128]{1,0:T(8,128)S(1)}, f32[24,128]{1,0:T(8,128)S(1)}, u32[]{:S(2)}, u32[]{:S(2)}) %collective-permute-start.12) | collective-permute-done | bytes 12320 | tf_op jit(solution)/shard_map/ppermute | solution.py:452
  79.8 0.7 collective-permute-done.11
  80.5 4.7 %shard_map.118 = (f32[32,2048]{1,0:T(8,128)}, f32[3,32,128]{2,1,0:T(8,128)}) custom-call(f32[24,128]{1,0:T(8,128)S(1)} %add_add_fusion.gram_ref, f32[32,32]{1,0:T(8,128)S(1)} %get-tuple-element.29.factor0_ref, f32[4,32,32]{2,1,0:T(8,128)S(1)} %get-tuple-element.36.small_ref, f32[32,2560]{1,0:T(8,128)S(1)} %get-tuple-element.24.basis_ref.basis0_ref, ...), custom_call_target="tpu_custom_call" | custom-call | tf_op jit(solution)/shard_map/pallas_call | solution.py:415
  (40 shorter events, 2.2 us)
Async XLA Ops:
  0.6 1.0 %copy-start = (f32[32,2048]{1,0:T(8,128)S(1)}, f32[32,2048]{1,0:T(8,128)}, u32[]{:S(2)}) copy-start(f32[32,2048]{1,0:T(8,128)} %sens_ref.3) | copy-start | bytes 786436
  1.6 16.6 %copy-start.1 = (f32[32,2048]{1,0:T(8,128)S(1)}, f32[32,2048]{1,0:T(8,128)}, u32[]{:S(2)}) copy-start(f32[32,2048]{1,0:T(8,128)} %sens_ref.3) | copy-start | bytes 786436
  2.7 15.5 %copy-start.2 = (bf16[3,128,128]{2,1,0:T(8,128)(2,1)S(1)}, bf16[3,128,128]{2,1,0:T(8,128)(2,1)}, u32[]{:S(2)}) copy-start(bf16[3,128,128]{2,1,0:T(8,128)(2,1)} %param.19) | copy-start | bytes 294916
  2.7 15.5 %copy-start.3 = (s32[128,128]{1,0:T(8,128)S(1)}, s32[128,128]{1,0:T(8,128)}, u32[]{:S(2)}) copy-start(s32[128,128]{1,0:T(8,128)} %conn_ref.3) | copy-start | bytes 196612
  2.7 15.5 %all-to-all-start = ((f32[32,8,128]{2,1,0:T(8,128)}), f32[32,8,128]{2,1,0:T(8,128)S(1)}, u32[]{:S(2)}, u32[]{:S(2)}) async-start(f32[32,8,128]{2,1,0:T(8,128)} %get-tuple-element.21), calls=%async_computation | async-start | bytes 262144 | tf_op jit(solution)/shard_map/all_to_all | solution.py:437
  10.0 1.1 %copy-start.9 = (s32[1,2,256]{2,1,0:T(2,128)S(1)}, s32[1,2,256]{2,1,0:T(2,128)}, u32[]{:S(2)}) copy-start(s32[1,2,256]{2,1,0:T(2,128)} %param.18) | copy-start | bytes 6148
  10.0 1.9 %collective-permute-start = (f32[32,256]{1,0:T(8,128)S(1)}, f32[32,256]{1,0:T(8,128)S(1)}, u32[]{:S(2)}, u32[]{:S(2)}) collective-permute-start(f32[32,256]{1,0:T(8,128)S(1)} %get-tuple-element.22), channel_id=1, source_target_pairs={{0,1},{1,0},{2,3},{3,2},{4,5},{5,4},{6,7},{7,6},{8,9},{9,8},{10,11... | collective-permute-start | bytes 98312 | tf_op jit(solution)/shard_map/ppermute | solution.py:433
  10.3 0.8 copy-start.5
  10.3 0.8 copy-start.6
  10.3 0.8 copy-start.7
  10.3 1.6 %collective-permute-start.1 = (f32[32,256]{1,0:T(8,128)S(1)}, f32[32,256]{1,0:T(8,128)S(1)}, u32[]{:S(2)}, u32[]{:S(2)}) collective-permute-start(f32[32,256]{1,0:T(8,128)S(1)} %get-tuple-element.23), channel_id=1, source_target_pairs={{1,2},{2,1},{3,4},{4,3},{5,6},{6,5},{7,8},{8,7},{9,10},{10,9},{11,... | collective-permute-start | bytes 98312 | tf_op jit(solution)/shard_map/ppermute | solution.py:433
  11.2 0.7 copy-start.8
  11.9 6.3 %copy-start.4 = (f32[2048]{0:T(1024)S(1)}, f32[2048]{0:T(1024)}, u32[]{:S(2)}) copy-start(f32[2048]{0:T(1024)} %param.11) | copy-start | bytes 24580
  27.3 1.3 %collective-permute-start.2 = (f32[40,512]{1,0:T(8,128)S(1)}, f32[40,512]{1,0:T(8,128)S(1)}, u32[]{:S(2)}, u32[]{:S(2)}) collective-permute-start(f32[40,512]{1,0:T(8,128)S(1)} %get-tuple-element.26), channel_id=1, source_target_pairs={{0,1},{1,0},{2,3},{3,2},{4,5},{5,4},{6,7},{7,6},{8,9},{9,8},{10,11... | collective-permute-start | bytes 245768 | tf_op jit(solution)/shard_map/ppermute | solution.py:433
  27.6 1.1 %collective-permute-start.3 = (f32[40,512]{1,0:T(8,128)S(1)}, f32[40,512]{1,0:T(8,128)S(1)}, u32[]{:S(2)}, u32[]{:S(2)}) collective-permute-start(f32[40,512]{1,0:T(8,128)S(1)} %get-tuple-element.27), channel_id=1, source_target_pairs={{1,2},{2,1},{3,4},{4,3},{5,6},{6,5},{7,8},{8,7},{9,10},{10,9},{11,... | collective-permute-start | bytes 245768 | tf_op jit(solution)/shard_map/ppermute | solution.py:433
  59.6 1.3 %collective-permute-start.4 = (f32[32,512]{1,0:T(8,128)S(1)}, f32[32,512]{1,0:T(8,128)S(1)}, u32[]{:S(2)}, u32[]{:S(2)}) collective-permute-start(f32[32,512]{1,0:T(8,128)S(1)} %get-tuple-element.34), channel_id=1, source_target_pairs={{0,1},{1,0},{2,3},{3,2},{4,5},{5,4},{6,7},{7,6},{8,9},{9,8},{10,11... | collective-permute-start | bytes 196616 | tf_op jit(solution)/shard_map/ppermute | solution.py:433
  60.0 0.9 %collective-permute-start.5 = (f32[32,512]{1,0:T(8,128)S(1)}, f32[32,512]{1,0:T(8,128)S(1)}, u32[]{:S(2)}, u32[]{:S(2)}) collective-permute-start(f32[32,512]{1,0:T(8,128)S(1)} %get-tuple-element.35), channel_id=1, source_target_pairs={{1,2},{2,1},{3,4},{4,3},{5,6},{6,5},{7,8},{8,7},{9,10},{10,9},{11,... | collective-permute-start | bytes 196616 | tf_op jit(solution)/shard_map/ppermute | solution.py:433
  61.7 6.1 %collective-permute-start.6 = (f32[24,128]{1,0:T(8,128)S(1)}, f32[24,128]{1,0:T(8,128)S(1)}, u32[]{:S(2)}, u32[]{:S(2)}) collective-permute-start(f32[24,128]{1,0:T(8,128)S(1)} %shard_map.117), channel_id=1, source_target_pairs={{0,1},{1,0},{2,3},{3,2},{4,5},{5,4},{6,7},{7,6},{8,9},{9,8},{10,11... | collective-permute-start | bytes 36872 | tf_op jit(solution)/shard_map/ppermute | solution.py:452
  67.8 4.6 %collective-permute-start.9 = (f32[24,128]{1,0:T(8,128)S(1)}, f32[24,128]{1,0:T(8,128)S(1)}, u32[]{:S(2)}, u32[]{:S(2)}) collective-permute-start(f32[24,128]{1,0:T(8,128)S(1)} %add.21), channel_id=1, source_target_pairs={{0,6},{1,7},{2,4},{3,5},{4,2},{5,3},{6,0},{7,1},{8,14},{9,15},{10,... | collective-permute-start | bytes 36872 | tf_op jit(solution)/shard_map/ppermute | solution.py:452
  70.6 3.7 %collective-permute-start.8 = (f32[24,128]{1,0:T(8,128)S(1)}, f32[24,128]{1,0:T(8,128)S(1)}, u32[]{:S(2)}, u32[]{:S(2)}) collective-permute-start(f32[24,128]{1,0:T(8,128)S(1)} %add.21), channel_id=1, source_target_pairs={{0,4},{1,5},{2,6},{3,7},{4,0},{5,1},{6,2},{7,3},{8,12},{9,13},{10,... | collective-permute-start | bytes 36872 | tf_op jit(solution)/shard_map/ppermute | solution.py:452
  70.6 3.7 %collective-permute-start.7 = (f32[24,128]{1,0:T(8,128)S(1)}, f32[24,128]{1,0:T(8,128)S(1)}, u32[]{:S(2)}, u32[]{:S(2)}) collective-permute-start(f32[24,128]{1,0:T(8,128)S(1)} %add.21), channel_id=1, source_target_pairs={{0,2},{1,3},{2,0},{3,1},{4,6},{5,7},{6,4},{7,5},{8,10},{9,11},{10,... | collective-permute-start | bytes 36872 | tf_op jit(solution)/shard_map/ppermute | solution.py:452
  74.3 5.6 %collective-permute-start.12 = (f32[24,128]{1,0:T(8,128)S(1)}, f32[24,128]{1,0:T(8,128)S(1)}, u32[]{:S(2)}, u32[]{:S(2)}) collective-permute-start(f32[24,128]{1,0:T(8,128)S(1)} %add_add_fusion.1), channel_id=1, source_target_pairs={{0,24},{1,25},{2,26},{3,27},{4,28},{5,29},{6,30},{7,31},{8,16},{9,... | collective-permute-start | bytes 36872 | tf_op jit(solution)/shard_map/ppermute | solution.py:452
  75.9 4.6 %collective-permute-start.11 = (f32[24,128]{1,0:T(8,128)S(1)}, f32[24,128]{1,0:T(8,128)S(1)}, u32[]{:S(2)}, u32[]{:S(2)}) collective-permute-start(f32[24,128]{1,0:T(8,128)S(1)} %add_add_fusion.1), channel_id=1, source_target_pairs={{0,16},{1,17},{2,18},{3,19},{4,20},{5,21},{6,22},{7,23},{8,24},{9,... | collective-permute-start | bytes 36872 | tf_op jit(solution)/shard_map/ppermute | solution.py:452
  76.7 3.8 %collective-permute-start.10 = (f32[24,128]{1,0:T(8,128)S(1)}, f32[24,128]{1,0:T(8,128)S(1)}, u32[]{:S(2)}, u32[]{:S(2)}) collective-permute-start(f32[24,128]{1,0:T(8,128)S(1)} %add_add_fusion.1), channel_id=1, source_target_pairs={{0,8},{1,9},{2,10},{3,11},{4,12},{5,13},{6,14},{7,15},{8,0},{9,1},... | collective-permute-start | bytes 36872 | tf_op jit(solution)/shard_map/ppermute | solution.py:452
  (1 other events, 0.7 us)

commit v6 on v5

--- a/solution.py
+++ b/solution.py
@@ -298,32 +298,40 @@
 
 
 def second_kernel(
-    gram_ref, factor0_ref, basis0_ref, full_ref, row_ref, diag_ref, conn_ref, owner_ref, coeff_ref,
+    gram_ref, basis0_ref, full_ref, row_ref, diag_ref, conn_ref, owner_ref, coeff_ref,
     stacked_ref,
-    basis_ref, image_ref, a_ref, b_ref, small_ref, values_ref, push_ref,
+    basis_ref, image_ref, a_ref, b_ref, small_ref, values_ref, moved_ref,
     tiles_ref, total_ref, state_ref,
 ):
-    elems, slots = conn_ref.shape
     summed = jnp.sum(gram_ref[...], axis=0)
     tile = jnp.concatenate([summed[r] for r in range(summed.shape[0])], axis=0)
     n = basis0_ref.shape[0]
     part = n * n // 128
     proj, square = unpacked(tile[:part]), unpacked_symmetric(tile[part:], n)
     inverse, factor = lower_inverse(square - fdot(proj, proj, TN))
-    head, unused = lower_inverse(square)
     reduced = full_ref[...] - fdot(proj, basis0_ref[...], TN)
     basis = fdot(inverse, reduced)
     basis_ref[...] = basis
+    small_ref[0] = proj
+    small_ref[1] = square
+    small_ref[2] = factor
+    parts = apply_elements(
+        basis.astype(BF16), conn_ref, owner_ref, coeff_ref,
+        stacked_ref, values_ref, tiles_ref, total_ref, row_ref[...], state_ref,
+    )
+    write_image(basis, parts, diag_ref, image_ref, a_ref, b_ref)
+    moved_ref[...] = state_ref[...].astype(BF16)
+
+
+def side_kernel(small_in, factor0_ref, moved_ref, stacked_ref, small_ref, push_ref):
+    elems, slots = moved_ref.shape
+    proj, square, factor = small_in[0], small_in[1], small_in[2]
+    head, unused = lower_inverse(square)
     small_ref[0] = head
     small_ref[1] = fdot(head, proj, NT)
     small_ref[2] = fdot(head, factor, NT)
     small_ref[3] = fdot(head, fdot(proj, factor0_ref[...], TN))
-    parts = apply_elements(
-        basis.astype(BF16), conn_ref, owner_ref, coeff_ref,
-        stacked_ref, values_ref, tiles_ref, total_ref, row_ref[...], state_ref,
-    )
-    write_image(basis, parts, diag_ref, image_ref, a_ref, b_ref)
-    moved = state_ref[...].astype(BF16)
+    moved = moved_ref[...]
     for k in range(3):
         pushed = bdot(stacked_ref[k * slots : (k + 1) * slots, :], moved, NT).astype(BF16)
         for part in range(PARTS):
@@ -505,14 +513,21 @@
         [basis0, image, disp, a, b],
     )
     gram = everyones(gram)
-    basis1, image, a, b, small, values1, pushed = call(
+    basis1, image, a, b, small, values1, moved = call(
         second_kernel,
-        [wide, wide, band, band, ((4, rows, rows), F32), picked, ((PARTS, slots, 3 * elems // PARTS), BF16)],
+        [wide, wide, band, band, ((3, rows, rows), F32), picked, ((elems, slots), BF16)],
         [((count * rows + extra, depth), BF16), ((count * rows, depth), F32), ((elems, slots), F32)],
-        [gram, factor0, basis0, full, state, diag, connectivity, owner, coeffs, stacked],
-        smem=(8,),
+        [gram, basis0, full, state, diag, connectivity, owner, coeffs, stacked],
+        smem=(7,),
     )
     a, b = exchanged(a, b)
+    small, pushed = call(
+        side_kernel,
+        [((4, rows, rows), F32), ((PARTS, slots, 3 * elems // PARTS), BF16)],
+        [],
+        [small, factor0, moved, stacked],
+    )
+    image, small, pushed = lax.optimization_barrier((image, small, pushed))
     gram = call(late_kernel, [((3 * part, 128), F32)], [], [basis0, basis1, image, a, b])[0]
     gram = total(gram)
     adjoint, grads = call(

time: 85.5 us -> 84.9 us (level)
  starting transfers between devices: 23.8 us -> 22.6 us
    ppermute x7, starting transfers between devices: 13.2 us -> 12 us  [total(): parts.append(lax.ppermute(value, AXIS, route))]
    pallas_call x6 -> x7, Pallas kernels: 27.1 us -> 27.6 us  [call(): pl.pallas_call(kernel, out_shape=[jax.ShapeDtypeStruct(shape, dtype) for...]
  transfers between devices with their start and end apart: 14 -> 14, of which waited for: 7 -> 7; matrix products, arithmetic and copies ran while one was open for 0% -> 0% of each run, Pallas kernels for 0% -> 1%
where the time goes in v6:
time: 84.9 us; the launch traced here: 84.6 us
  Pallas kernels  27.6 us (33%)
  starting transfers between devices  22.6 us (27%)
  blocking collectives  19.5 us (23%)
  waiting for transfers between devices  12.4 us (15%)
  local copies, waits for them, and re-layouts  1.65 us (2%)
    pallas_call x7, Pallas kernels, call(): pl.pallas_call(kernel, out_shape=[jax.ShapeDtypeStruct(shape, dtype) for...  27.6 us
    all_to_all x1, blocking collectives, everyones(): return lax.all_to_all(copies, AXIS, 0, 0, tiled=True)  19.5 us
    ppermute x7, starting transfers between devices, total(): parts.append(lax.ppermute(value, AXIS, route))  12 us
    all_to_all x1, starting transfers between devices, everyones(): return lax.all_to_all(copies, AXIS, 0, 0, tiled=True)  7.3 us
    all_to_all x1, waiting for transfers between devices, everyones(): return lax.all_to_all(copies, AXIS, 0, 0, tiled=True)  6.32 us
    ppermute x7, waiting for transfers between devices, total(): parts.append(lax.ppermute(value, AXIS, route))  5.64 us
    ppermute x6, starting transfers between devices, exchanged(): return (lax.ppermute(a, AXIS, first), lax.ppermute(b, AXIS, second))  3.32 us
  transfers between devices with their start and end apart: 14, of which 7 were waited for; matrix products, arithmetic and copies ran while one was open for 0% of the time, Pallas kernels for 1%

profile of v6, /device:TPU:0, one launch (start us, length us, event | category | flops | bytes accessed | tf_op | source)
XLA Modules:
  0.0 84.6 jit_solution(6560675708201089373)
XLA Ops:
  0.6 0.9 %copy-done = f32[32,2048]{1,0:T(8,128)S(1)} copy-done((f32[32,2048]{1,0:T(8,128)S(1)}, f32[32,2048]{1,0:T(8,128)}, u32[]{:S(2)}) %copy-start) | copy-done | bytes 262168
  1.6 1.1 %shard_map.113 = (f32[32,8,128]{2,1,0:T(8,128)}, f32[32,256]{1,0:T(8,128)S(1)}, f32[32,256]{1,0:T(8,128)S(1)}) custom-call(f32[32,2048]{1,0:T(8,128)S(1)} %copy-done), custom_call_target="tpu_custom_call" | custom-call | tf_op jit(solution)/shard_map/pallas_call | solution.py:423
  2.7 7.3 %all-to-all-start = ((f32[32,8,128]{2,1,0:T(8,128)}), f32[32,8,128]{2,1,0:T(8,128)S(1)}, u32[]{:S(2)}, u32[]{:S(2)}) async-start(f32[32,8,128]{2,1,0:T(8,128)} %get-tuple-element.26), calls=%async_computation | async-start | bytes 262144 | tf_op jit(solution)/shard_map/all_to_all | solution.py:445
  10.3 0.8 collective-permute-start.1
  11.9 6.3 %all-to-all-done.gram_ref = f32[32,8,128]{2,1,0:T(8,128)S(1)} async-done(((f32[32,8,128]{2,1,0:T(8,128)}), f32[32,8,128]{2,1,0:T(8,128)S(1)}, u32[]{:S(2)}, u32[]{:S(2)}) %all-to-all-start) | async-done | bytes 131104 | tf_op jit(solution)/shard_map/all_to_all | solution.py:445
  18.2 9.1 %shard_map.114 = (f32[32,2560]{1,0:T(8,128)S(1)}, f32[32,2560]{1,0:T(8,128)S(1)}, f32[40,512]{1,0:T(8,128)S(1)}, f32[40,512]{1,0:T(8,128)S(1)}, f32[32,32]{1,0:T(8,128)S(1)}, /*index=5*/bf16[4096,128]{1,0:T(8,128)(2,1)S(1)}) custom-call(f32[32,8,128]{2,1,0:T(8,128)S(1)} %all-to-all-done.gram_ref, f32[32,2048]{1,0:T(8,128)S(1)} %copy-done.1, ...), custom_call_target="tpu_custom_call" | custom-call | tf_op jit(solution)/shard_map/pallas_call | solution.py:423
  28.7 0.7 shard_map.115
  29.4 19.5 %all_to_all.10.gram_ref = f32[32,13,1,128]{3,2,1,0:T(1,128)S(1)} all-to-all(f32[32,13,1,128]{3,2,1,0:T(1,128)S(1)} %get-tuple-element.33), channel_id=1, replica_groups=mesh['brick'=32] {'brick'}, dimensions={0} | all-to-all | bytes 425984 | tf_op jit(solution)/shard_map/all_to_all | solution.py:445
  48.8 10.1 %shard_map.116 = (f32[32,2560]{1,0:T(8,128)S(1)}, f32[32,2560]{1,0:T(8,128)S(1)}, f32[32,512]{1,0:T(8,128)S(1)}, f32[32,512]{1,0:T(8,128)S(1)}, f32[3,32,32]{2,1...) custom-call(f32[32,13,1,128]{3,2,1,0:T(1,128)S(1)} %all_to_all.10.gram_ref, ...), custom_call_target="tpu_custom_call" | custom-call | tf_op jit(solution)/shard_map/pallas_call | solution.py:423
  59.3 0.9 %collective-permute-start.5 = (f32[32,512]{1,0:T(8,128)S(1)}, f32[32,512]{1,0:T(8,128)S(1)}, u32[]{:S(2)}, u32[]{:S(2)}) collective-permute-start(f32[32,512]{1,0:T(8,128)S(1)} %get-tuple-element.45), channel_id=1, source_target_pairs={{1,2},{2,1},{3,4},{4,3},{5,6},{6,5},{7,8},{8,7},{9,10},{10,9},{11,... | collective-permute-start | bytes 196616 | tf_op jit(solution)/shard_map/ppermute | solution.py:441
  60.2 1.2 %shard_map.117 = (f32[4,32,32]{2,1,0:T(8,128)S(1)}, bf16[2,128,192]{2,1,0:T(8,128)(2,1)S(1)}) custom-call(f32[3,32,32]{2,1,0:T(8,128)S(1)} %get-tuple-element.38.small_in, f32[32,32]{1,0:T(8,128)S(1)} %get-tuple-element.39.factor0_ref, bf16[128,128]{1,0:T(8,128)(2,1)S(1)} %get-tuple-element.40.moved_ref, bf16[384,128]{1,0:T(8,128)(2,1)S(1)} %bitcast.13), custom_call_target="tpu_custom_call" | custom-call | tf_op jit(solution)/shard_map/pallas_call | solution.py:423
  61.4 0.8 shard_map.118
  62.2 4.1 %collective-permute-start.6 = (f32[24,128]{1,0:T(8,128)S(1)}, f32[24,128]{1,0:T(8,128)S(1)}, u32[]{:S(2)}, u32[]{:S(2)}) collective-permute-start(f32[24,128]{1,0:T(8,128)S(1)} %shard_map.118), channel_id=1, source_target_pairs={{0,1},{1,0},{2,3},{3,2},{4,5},{5,4},{6,7},{7,6},{8,9},{9,8},{10,11... | collective-permute-start | bytes 36872 | tf_op jit(solution)/shard_map/ppermute | solution.py:460
  66.3 0.8 collective-permute-done.6
  67.1 2.8 %collective-permute-start.9 = (f32[24,128]{1,0:T(8,128)S(1)}, f32[24,128]{1,0:T(8,128)S(1)}, u32[]{:S(2)}, u32[]{:S(2)}) collective-permute-start(f32[24,128]{1,0:T(8,128)S(1)} %add.21), channel_id=1, source_target_pairs={{0,6},{1,7},{2,4},{3,5},{4,2},{5,3},{6,0},{7,1},{8,14},{9,15},{10,... | collective-permute-start | bytes 36872 | tf_op jit(solution)/shard_map/ppermute | solution.py:460
  69.9 0.7 collective-permute-start.7
  70.6 1.1 %collective-permute-done.9 = f32[24,128]{1,0:T(8,128)S(1)} collective-permute-done((f32[24,128]{1,0:T(8,128)S(1)}, f32[24,128]{1,0:T(8,128)S(1)}, u32[]{:S(2)}, u32[]{:S(2)}) %collective-permute-start.9) | collective-permute-done | bytes 12320 | tf_op jit(solution)/shard_map/ppermute | solution.py:460
  71.7 1.9 %collective-permute-done.8 = f32[24,128]{1,0:T(8,128)S(1)} collective-permute-done((f32[24,128]{1,0:T(8,128)S(1)}, f32[24,128]{1,0:T(8,128)S(1)}, u32[]{:S(2)}, u32[]{:S(2)}) %collective-permute-start.8) | collective-permute-done | bytes 12320 | tf_op jit(solution)/shard_map/ppermute | solution.py:460
  73.6 1.6 %collective-permute-start.12 = (f32[24,128]{1,0:T(8,128)S(1)}, f32[24,128]{1,0:T(8,128)S(1)}, u32[]{:S(2)}, u32[]{:S(2)}) collective-permute-start(f32[24,128]{1,0:T(8,128)S(1)} %add_add_fusion.1), channel_id=1, source_target_pairs={{0,24},{1,25},{2,26},{3,27},{4,28},{5,29},{6,30},{7,31},{8,16},{9,... | collective-permute-start | bytes 36872 | tf_op jit(solution)/shard_map/ppermute | solution.py:460
  75.2 0.8 collective-permute-start.11
  76.0 2.0 %collective-permute-start.10 = (f32[24,128]{1,0:T(8,128)S(1)}, f32[24,128]{1,0:T(8,128)S(1)}, u32[]{:S(2)}, u32[]{:S(2)}) collective-permute-start(f32[24,128]{1,0:T(8,128)S(1)} %add_add_fusion.1), channel_id=1, source_target_pairs={{0,8},{1,9},{2,10},{3,11},{4,12},{5,13},{6,14},{7,15},{8,0},{9,1},... | collective-permute-start | bytes 36872 | tf_op jit(solution)/shard_map/ppermute | solution.py:460
  78.1 1.1 %collective-permute-done.12 = f32[24,128]{1,0:T(8,128)S(1)} collective-permute-done((f32[24,128]{1,0:T(8,128)S(1)}, f32[24,128]{1,0:T(8,128)S(1)}, u32[]{:S(2)}, u32[]{:S(2)}) %collective-permute-start.12) | collective-permute-done | bytes 12320 | tf_op jit(solution)/shard_map/ppermute | solution.py:460
  79.2 0.7 collective-permute-done.11
  79.9 4.7 %shard_map.119 = (f32[32,2048]{1,0:T(8,128)}, f32[3,32,128]{2,1,0:T(8,128)}) custom-call(f32[24,128]{1,0:T(8,128)S(1)} %add_add_fusion.gram_ref, f32[32,32]{1,0:T(8,128)S(1)} %get-tuple-element.39.factor0_ref, f32[4,32,32]{2,1,0:T(8,128)S(1)} %get-tuple-element.46.small_ref, f32[32,2560]{1,0:T(8,128)S(1)} %get-tuple-element.29.basis_ref.basis0_ref, ...), custom_call_target="tpu_custom_call" | custom-call | tf_op jit(solution)/shard_map/pallas_call | solution.py:423
  (41 shorter events, 2.8 us)
Async XLA Ops:
  0.6 1.0 %copy-start = (f32[32,2048]{1,0:T(8,128)S(1)}, f32[32,2048]{1,0:T(8,128)}, u32[]{:S(2)}) copy-start(f32[32,2048]{1,0:T(8,128)} %sens_ref.3) | copy-start | bytes 786436
  1.6 16.6 %copy-start.1 = (f32[32,2048]{1,0:T(8,128)S(1)}, f32[32,2048]{1,0:T(8,128)}, u32[]{:S(2)}) copy-start(f32[32,2048]{1,0:T(8,128)} %sens_ref.3) | copy-start | bytes 786436
  2.7 15.5 %copy-start.2 = (bf16[3,128,128]{2,1,0:T(8,128)(2,1)S(1)}, bf16[3,128,128]{2,1,0:T(8,128)(2,1)}, u32[]{:S(2)}) copy-start(bf16[3,128,128]{2,1,0:T(8,128)(2,1)} %param.19) | copy-start | bytes 294916
  2.7 15.5 %copy-start.3 = (s32[128,128]{1,0:T(8,128)S(1)}, s32[128,128]{1,0:T(8,128)}, u32[]{:S(2)}) copy-start(s32[128,128]{1,0:T(8,128)} %conn_ref.3) | copy-start | bytes 196612
  2.7 15.5 %all-to-all-start = ((f32[32,8,128]{2,1,0:T(8,128)}), f32[32,8,128]{2,1,0:T(8,128)S(1)}, u32[]{:S(2)}, u32[]{:S(2)}) async-start(f32[32,8,128]{2,1,0:T(8,128)} %get-tuple-element.26), calls=%async_computation | async-start | bytes 262144 | tf_op jit(solution)/shard_map/all_to_all | solution.py:445
  10.0 1.1 %copy-start.9 = (s32[1,2,256]{2,1,0:T(2,128)S(1)}, s32[1,2,256]{2,1,0:T(2,128)}, u32[]{:S(2)}) copy-start(s32[1,2,256]{2,1,0:T(2,128)} %param.18) | copy-start | bytes 6148
  10.0 1.9 %collective-permute-start = (f32[32,256]{1,0:T(8,128)S(1)}, f32[32,256]{1,0:T(8,128)S(1)}, u32[]{:S(2)}, u32[]{:S(2)}) collective-permute-start(f32[32,256]{1,0:T(8,128)S(1)} %get-tuple-element.27), channel_id=1, source_target_pairs={{0,1},{1,0},{2,3},{3,2},{4,5},{5,4},{6,7},{7,6},{8,9},{9,8},{10,11... | collective-permute-start | bytes 98312 | tf_op jit(solution)/shard_map/ppermute | solution.py:441
  10.3 0.8 copy-start.5
  10.3 0.8 copy-start.6
  10.3 0.8 %copy-start.7 = (s32[128]{0:T(128)S(1)}, s32[128]{0:T(128)}, u32[]{:S(2)}) copy-start(s32[128]{0:T(128)} %param.17) | copy-start | bytes 1540
  10.3 1.6 %collective-permute-start.1 = (f32[32,256]{1,0:T(8,128)S(1)}, f32[32,256]{1,0:T(8,128)S(1)}, u32[]{:S(2)}, u32[]{:S(2)}) collective-permute-start(f32[32,256]{1,0:T(8,128)S(1)} %get-tuple-element.28), channel_id=1, source_target_pairs={{1,2},{2,1},{3,4},{4,3},{5,6},{6,5},{7,8},{8,7},{9,10},{10,9},{11,... | collective-permute-start | bytes 98312 | tf_op jit(solution)/shard_map/ppermute | solution.py:441
  11.2 0.7 copy-start.8
  11.9 6.3 %copy-start.4 = (f32[2048]{0:T(1024)S(1)}, f32[2048]{0:T(1024)}, u32[]{:S(2)}) copy-start(f32[2048]{0:T(1024)} %param.11) | copy-start | bytes 24580
  27.3 1.3 %collective-permute-start.2 = (f32[40,512]{1,0:T(8,128)S(1)}, f32[40,512]{1,0:T(8,128)S(1)}, u32[]{:S(2)}, u32[]{:S(2)}) collective-permute-start(f32[40,512]{1,0:T(8,128)S(1)} %get-tuple-element.31), channel_id=1, source_target_pairs={{0,1},{1,0},{2,3},{3,2},{4,5},{5,4},{6,7},{7,6},{8,9},{9,8},{10,11... | collective-permute-start | bytes 245768 | tf_op jit(solution)/shard_map/ppermute | solution.py:441
  27.6 1.1 %collective-permute-start.3 = (f32[40,512]{1,0:T(8,128)S(1)}, f32[40,512]{1,0:T(8,128)S(1)}, u32[]{:S(2)}, u32[]{:S(2)}) collective-permute-start(f32[40,512]{1,0:T(8,128)S(1)} %get-tuple-element.32), channel_id=1, source_target_pairs={{1,2},{2,1},{3,4},{4,3},{5,6},{6,5},{7,8},{8,7},{9,10},{10,9},{11,... | collective-permute-start | bytes 245768 | tf_op jit(solution)/shard_map/ppermute | solution.py:441
  58.9 2.5 %collective-permute-start.4 = (f32[32,512]{1,0:T(8,128)S(1)}, f32[32,512]{1,0:T(8,128)S(1)}, u32[]{:S(2)}, u32[]{:S(2)}) collective-permute-start(f32[32,512]{1,0:T(8,128)S(1)} %get-tuple-element.44), channel_id=1, source_target_pairs={{0,1},{1,0},{2,3},{3,2},{4,5},{5,4},{6,7},{7,6},{8,9},{9,8},{10,11... | collective-permute-start | bytes 196616 | tf_op jit(solution)/shard_map/ppermute | solution.py:441
  59.3 2.1 %collective-permute-start.5 = (f32[32,512]{1,0:T(8,128)S(1)}, f32[32,512]{1,0:T(8,128)S(1)}, u32[]{:S(2)}, u32[]{:S(2)}) collective-permute-start(f32[32,512]{1,0:T(8,128)S(1)} %get-tuple-element.45), channel_id=1, source_target_pairs={{1,2},{2,1},{3,4},{4,3},{5,6},{6,5},{7,8},{8,7},{9,10},{10,9},{11,... | collective-permute-start | bytes 196616 | tf_op jit(solution)/shard_map/ppermute | solution.py:441
  62.2 4.9 %collective-permute-start.6 = (f32[24,128]{1,0:T(8,128)S(1)}, f32[24,128]{1,0:T(8,128)S(1)}, u32[]{:S(2)}, u32[]{:S(2)}) collective-permute-start(f32[24,128]{1,0:T(8,128)S(1)} %shard_map.118), channel_id=1, source_target_pairs={{0,1},{1,0},{2,3},{3,2},{4,5},{5,4},{6,7},{7,6},{8,9},{9,8},{10,11... | collective-permute-start | bytes 36872 | tf_op jit(solution)/shard_map/ppermute | solution.py:460
  67.1 4.6 %collective-permute-start.9 = (f32[24,128]{1,0:T(8,128)S(1)}, f32[24,128]{1,0:T(8,128)S(1)}, u32[]{:S(2)}, u32[]{:S(2)}) collective-permute-start(f32[24,128]{1,0:T(8,128)S(1)} %add.21), channel_id=1, source_target_pairs={{0,6},{1,7},{2,4},{3,5},{4,2},{5,3},{6,0},{7,1},{8,14},{9,15},{10,... | collective-permute-start | bytes 36872 | tf_op jit(solution)/shard_map/ppermute | solution.py:460
  69.9 3.7 %collective-permute-start.8 = (f32[24,128]{1,0:T(8,128)S(1)}, f32[24,128]{1,0:T(8,128)S(1)}, u32[]{:S(2)}, u32[]{:S(2)}) collective-permute-start(f32[24,128]{1,0:T(8,128)S(1)} %add.21), channel_id=1, source_target_pairs={{0,4},{1,5},{2,6},{3,7},{4,0},{5,1},{6,2},{7,3},{8,12},{9,13},{10,... | collective-permute-start | bytes 36872 | tf_op jit(solution)/shard_map/ppermute | solution.py:460
  69.9 3.7 %collective-permute-start.7 = (f32[24,128]{1,0:T(8,128)S(1)}, f32[24,128]{1,0:T(8,128)S(1)}, u32[]{:S(2)}, u32[]{:S(2)}) collective-permute-start(f32[24,128]{1,0:T(8,128)S(1)} %add.21), channel_id=1, source_target_pairs={{0,2},{1,3},{2,0},{3,1},{4,6},{5,7},{6,4},{7,5},{8,10},{9,11},{10,... | collective-permute-start | bytes 36872 | tf_op jit(solution)/shard_map/ppermute | solution.py:460
  73.6 5.6 %collective-permute-start.12 = (f32[24,128]{1,0:T(8,128)S(1)}, f32[24,128]{1,0:T(8,128)S(1)}, u32[]{:S(2)}, u32[]{:S(2)}) collective-permute-start(f32[24,128]{1,0:T(8,128)S(1)} %add_add_fusion.1), channel_id=1, source_target_pairs={{0,24},{1,25},{2,26},{3,27},{4,28},{5,29},{6,30},{7,31},{8,16},{9,... | collective-permute-start | bytes 36872 | tf_op jit(solution)/shard_map/ppermute | solution.py:460
  75.2 4.7 %collective-permute-start.11 = (f32[24,128]{1,0:T(8,128)S(1)}, f32[24,128]{1,0:T(8,128)S(1)}, u32[]{:S(2)}, u32[]{:S(2)}) collective-permute-start(f32[24,128]{1,0:T(8,128)S(1)} %add_add_fusion.1), channel_id=1, source_target_pairs={{0,16},{1,17},{2,18},{3,19},{4,20},{5,21},{6,22},{7,23},{8,24},{9,... | collective-permute-start | bytes 36872 | tf_op jit(solution)/shard_map/ppermute | solution.py:460
  76.0 3.8 %collective-permute-start.10 = (f32[24,128]{1,0:T(8,128)S(1)}, f32[24,128]{1,0:T(8,128)S(1)}, u32[]{:S(2)}, u32[]{:S(2)}) collective-permute-start(f32[24,128]{1,0:T(8,128)S(1)} %add_add_fusion.1), channel_id=1, source_target_pairs={{0,8},{1,9},{2,10},{3,11},{4,12},{5,13},{6,14},{7,15},{8,0},{9,1},... | collective-permute-start | bytes 36872 | tf_op jit(solution)/shard_map/ppermute | solution.py:460
  (1 other events, 0.7 us)

commit v7 on v6

--- a/solution.py
+++ b/solution.py
@@ -279,7 +279,19 @@
     return field[:, depth : field.shape[1] - depth]
 
 
-def middle_kernel(basis_ref, image_ref, disp_ref, a_in, b_in, full_ref, state_ref, gram_ref):
+def edge_part(field, depth):
+    width = field.shape[1]
+    return jnp.concatenate([field[:, depth : 2 * depth], field[:, width - 2 * depth : width - depth]], axis=1)
+
+
+def inner_kernel(owner_ref, *refs):
+    *field_refs, out_ref = refs
+    depth = owner_ref.shape[1]
+    fields = [own_part(ref[...], 2 * depth) for ref in field_refs]
+    out_ref[...] = fdot(jnp.concatenate(fields, axis=0), fields[-1], NT)
+
+
+def middle_kernel(basis_ref, image_ref, inner_ref, disp_ref, a_in, b_in, full_ref, state_ref, gram_ref):
     depth = a_in.shape[1] // 2
     low, high = received_bands(a_in, b_in)
     full = complete(image_ref, low, high)
@@ -288,9 +300,11 @@
         [low[at : at + 1, depth:], disp_ref[...], high[at : at + 1, :depth]], axis=1
     )
     full_ref[...] = full
-    own = own_part(full, depth)
-    rows = own.shape[0]
-    both = fdot(jnp.concatenate([own_part(basis_ref[...], depth), own], axis=0), own, NT)
+    edge = edge_part(full, depth)
+    rows = edge.shape[0]
+    both = inner_ref[...] + fdot(
+        jnp.concatenate([edge_part(basis_ref[...], depth), edge], axis=0), edge, NT
+    )
     tile = jnp.concatenate([packed(both[:rows]), packed_symmetric(both[rows:])], axis=0)
     copies = gram_ref.shape[0]
     for r in range(tile.shape[0]):
@@ -339,15 +353,15 @@
             push_ref[part, :, k * group : (k + 1) * group] = pushed[:, part * group : (part + 1) * group]
 
 
-def late_kernel(basis0_ref, basis1_ref, image_ref, a_in, b_in, gram_ref):
+def late_kernel(basis0_ref, basis1_ref, image_ref, inner_ref, a_in, b_in, gram_ref):
     depth = a_in.shape[1] // 2
-    own = own_part(complete(image_ref, *received_bands(a_in, b_in)), depth)
-    rows = own.shape[0]
-    every = fdot(
+    edge = edge_part(complete(image_ref, *received_bands(a_in, b_in)), depth)
+    rows = edge.shape[0]
+    every = inner_ref[...] + fdot(
         jnp.concatenate(
-            [own_part(basis0_ref[...], depth), own_part(basis1_ref[...], depth), own], axis=0
+            [edge_part(basis0_ref[...], depth), edge_part(basis1_ref[...], depth), edge], axis=0
         ),
-        own,
+        edge,
         NT,
     )
     gram_ref[...] = jnp.concatenate(
@@ -506,11 +520,12 @@
         smem=(8,),
     )
     a, b = exchanged(a, b)
+    inner = call(inner_kernel, [((2 * rows, rows), F32)], [], [owner, basis0, image])[0]
     full, state, gram = call(
         middle_kernel,
         [wide, ((1, width), F32), ((devices, part + part // 2 + 1, 1, 128), F32)],
         [],
-        [basis0, image, disp, a, b],
+        [basis0, image, inner, disp, a, b],
     )
     gram = everyones(gram)
     basis1, image, a, b, small, values1, moved = call(
@@ -527,8 +542,9 @@
         [],
         [small, factor0, moved, stacked],
     )
+    inner = call(inner_kernel, [((3 * rows, rows), F32)], [], [owner, basis0, basis1, image])[0]
     image, small, pushed = lax.optimization_barrier((image, small, pushed))
-    gram = call(late_kernel, [((3 * part, 128), F32)], [], [basis0, basis1, image, a, b])[0]
+    gram = call(late_kernel, [((3 * part, 128), F32)], [], [basis0, basis1, image, inner, a, b])[0]
     gram = total(gram)
     adjoint, grads = call(
         last_kernel,

time: 84.9 us -> 84.2 us (level)
    pallas_call x7 -> x9, Pallas kernels: 27.6 us -> 28 us  [call(): pl.pallas_call(kernel, out_shape=[jax.ShapeDtypeStruct(shape, dtype) for...]
  transfers between devices with their start and end apart: 14 -> 14, of which waited for: 7 -> 6; matrix products, arithmetic and copies ran while one was open for 0% -> 0% of each run, Pallas kernels for 1% -> 3%
where the time goes in v7:
time: 84.2 us; the launch traced here: 83.9 us
  Pallas kernels  28 us (33%)
  starting transfers between devices  22 us (26%)
  blocking collectives  19.4 us (23%)
  waiting for transfers between devices  12 us (14%)
  local copies, waits for them, and re-layouts  1.65 us (2%)
  between operations  0.85 us (1%)
    pallas_call x9, Pallas kernels, call(): pl.pallas_call(kernel, out_shape=[jax.ShapeDtypeStruct(shape, dtype) for...  28 us
    all_to_all x1, blocking collectives, everyones(): return lax.all_to_all(copies, AXIS, 0, 0, tiled=True)  19.4 us
    ppermute x7, starting transfers between devices, total(): parts.append(lax.ppermute(value, AXIS, route))  11.4 us
    all_to_all x1, starting transfers between devices, everyones(): return lax.all_to_all(copies, AXIS, 0, 0, tiled=True)  7.3 us
    all_to_all x1, waiting for transfers between devices, everyones(): return lax.all_to_all(copies, AXIS, 0, 0, tiled=True)  6.32 us
    ppermute x7, waiting for transfers between devices, total(): parts.append(lax.ppermute(value, AXIS, route))  5.63 us
    ppermute x6, starting transfers between devices, exchanged(): return (lax.ppermute(a, AXIS, first), lax.ppermute(b, AXIS, second))  3.32 us
  transfers between devices with their start and end apart: 14, of which 6 were waited for; matrix products, arithmetic and copies ran while one was open for 0% of the time, Pallas kernels for 3%

profile of v7, /device:TPU:0, one launch (start us, length us, event | category | flops | bytes accessed | tf_op | source)
XLA Modules:
  0.0 83.9 jit_solution(9147556668217725967)
XLA Ops:
  0.6 0.9 %copy-done = f32[32,2048]{1,0:T(8,128)S(1)} copy-done((f32[32,2048]{1,0:T(8,128)S(1)}, f32[32,2048]{1,0:T(8,128)}, u32[]{:S(2)}) %copy-start) | copy-done | bytes 262168
  1.6 1.1 %shard_map.113 = (f32[32,8,128]{2,1,0:T(8,128)}, f32[32,256]{1,0:T(8,128)S(1)}, f32[32,256]{1,0:T(8,128)S(1)}) custom-call(f32[32,2048]{1,0:T(8,128)S(1)} %copy-done), custom_call_target="tpu_custom_call" | custom-call | tf_op jit(solution)/shard_map/pallas_call | solution.py:437
  2.7 7.3 %all-to-all-start = ((f32[32,8,128]{2,1,0:T(8,128)}), f32[32,8,128]{2,1,0:T(8,128)S(1)}, u32[]{:S(2)}, u32[]{:S(2)}) async-start(f32[32,8,128]{2,1,0:T(8,128)} %get-tuple-element.26), calls=%async_computation | async-start | bytes 262144 | tf_op jit(solution)/shard_map/all_to_all | solution.py:459
  10.3 0.8 collective-permute-start.1
  11.9 6.3 %all-to-all-done.gram_ref = f32[32,8,128]{2,1,0:T(8,128)S(1)} async-done(((f32[32,8,128]{2,1,0:T(8,128)}), f32[32,8,128]{2,1,0:T(8,128)S(1)}, u32[]{:S(2)}, u32[]{:S(2)}) %all-to-all-start) | async-done | bytes 131104 | tf_op jit(solution)/shard_map/all_to_all | solution.py:459
  18.2 9.1 %shard_map.114 = (f32[32,2560]{1,0:T(8,128)S(1)}, f32[32,2560]{1,0:T(8,128)S(1)}, f32[40,512]{1,0:T(8,128)S(1)}, f32[40,512]{1,0:T(8,128)S(1)}, f32[32,32]{1,0:T(8,128)S(1)}, /*index=5*/bf16[4096,128]{1,0:T(8,128)(2,1)S(1)}) custom-call(f32[32,8,128]{2,1,0:T(8,128)S(1)} %all-to-all-done.gram_ref, f32[32,2048]{1,0:T(8,128)S(1)} %copy-done.1, ...), custom_call_target="tpu_custom_call" | custom-call | tf_op jit(solution)/shard_map/pallas_call | solution.py:437
  27.6 0.7 collective-permute-start.3
  29.2 19.4 %all_to_all.10.gram_ref = f32[32,13,1,128]{3,2,1,0:T(1,128)S(1)} all-to-all(f32[32,13,1,128]{3,2,1,0:T(1,128)S(1)} %get-tuple-element.33), channel_id=1, replica_groups=mesh['brick'=32] {'brick'}, dimensions={0} | all-to-all | bytes 425984 | tf_op jit(solution)/shard_map/all_to_all | solution.py:459
  48.6 10.1 %shard_map.117 = (f32[32,2560]{1,0:T(8,128)S(1)}, f32[32,2560]{1,0:T(8,128)S(1)}, f32[32,512]{1,0:T(8,128)S(1)}, f32[32,512]{1,0:T(8,128)S(1)}, f32[3,32,32]{2,1...) custom-call(f32[32,13,1,128]{3,2,1,0:T(1,128)S(1)} %all_to_all.10.gram_ref, ...), custom_call_target="tpu_custom_call" | custom-call | tf_op jit(solution)/shard_map/pallas_call | solution.py:437
  59.1 0.9 %collective-permute-start.5 = (f32[32,512]{1,0:T(8,128)S(1)}, f32[32,512]{1,0:T(8,128)S(1)}, u32[]{:S(2)}, u32[]{:S(2)}) collective-permute-start(f32[32,512]{1,0:T(8,128)S(1)} %get-tuple-element.45), channel_id=1, source_target_pairs={{1,2},{2,1},{3,4},{4,3},{5,6},{6,5},{7,8},{8,7},{9,10},{10,9},{11,... | collective-permute-start | bytes 196616 | tf_op jit(solution)/shard_map/ppermute | solution.py:455
  59.9 0.6 shard_map.119.inner_ref
  60.6 1.2 %shard_map.118 = (f32[4,32,32]{2,1,0:T(8,128)S(1)}, bf16[2,128,192]{2,1,0:T(8,128)(2,1)S(1)}) custom-call(f32[3,32,32]{2,1,0:T(8,128)S(1)} %get-tuple-element.38.small_in, f32[32,32]{1,0:T(8,128)S(1)} %get-tuple-element.39.factor0_ref, bf16[128,128]{1,0:T(8,128)(2,1)S(1)} %get-tuple-element.40.moved_ref, bf16[384,128]{1,0:T(8,128)(2,1)S(1)} %bitcast.13), custom_call_target="tpu_custom_call" | custom-call | tf_op jit(solution)/shard_map/pallas_call | solution.py:437
  62.1 3.4 %collective-permute-start.6 = (f32[24,128]{1,0:T(8,128)S(1)}, f32[24,128]{1,0:T(8,128)S(1)}, u32[]{:S(2)}, u32[]{:S(2)}) collective-permute-start(f32[24,128]{1,0:T(8,128)S(1)} %shard_map.120), channel_id=1, source_target_pairs={{0,1},{1,0},{2,3},{3,2},{4,5},{5,4},{6,7},{7,6},{8,9},{9,8},{10,11... | collective-permute-start | bytes 36872 | tf_op jit(solution)/shard_map/ppermute | solution.py:474
  65.6 0.8 collective-permute-done.6
  66.4 2.8 %collective-permute-start.9 = (f32[24,128]{1,0:T(8,128)S(1)}, f32[24,128]{1,0:T(8,128)S(1)}, u32[]{:S(2)}, u32[]{:S(2)}) collective-permute-start(f32[24,128]{1,0:T(8,128)S(1)} %add.21), channel_id=1, source_target_pairs={{0,6},{1,7},{2,4},{3,5},{4,2},{5,3},{6,0},{7,1},{8,14},{9,15},{10,... | collective-permute-start | bytes 36872 | tf_op jit(solution)/shard_map/ppermute | solution.py:474
  69.2 0.7 collective-permute-start.7
  69.9 1.1 %collective-permute-done.9 = f32[24,128]{1,0:T(8,128)S(1)} collective-permute-done((f32[24,128]{1,0:T(8,128)S(1)}, f32[24,128]{1,0:T(8,128)S(1)}, u32[]{:S(2)}, u32[]{:S(2)}) %collective-permute-start.9) | collective-permute-done | bytes 12320 | tf_op jit(solution)/shard_map/ppermute | solution.py:474
  71.0 1.9 %collective-permute-done.8 = f32[24,128]{1,0:T(8,128)S(1)} collective-permute-done((f32[24,128]{1,0:T(8,128)S(1)}, f32[24,128]{1,0:T(8,128)S(1)}, u32[]{:S(2)}, u32[]{:S(2)}) %collective-permute-start.8) | collective-permute-done | bytes 12320 | tf_op jit(solution)/shard_map/ppermute | solution.py:474
  72.9 1.6 %collective-permute-start.12 = (f32[24,128]{1,0:T(8,128)S(1)}, f32[24,128]{1,0:T(8,128)S(1)}, u32[]{:S(2)}, u32[]{:S(2)}) collective-permute-start(f32[24,128]{1,0:T(8,128)S(1)} %add_add_fusion.1), channel_id=1, source_target_pairs={{0,24},{1,25},{2,26},{3,27},{4,28},{5,29},{6,30},{7,31},{8,16},{9,... | collective-permute-start | bytes 36872 | tf_op jit(solution)/shard_map/ppermute | solution.py:474
  74.5 0.8 collective-permute-start.11
  75.3 2.0 %collective-permute-start.10 = (f32[24,128]{1,0:T(8,128)S(1)}, f32[24,128]{1,0:T(8,128)S(1)}, u32[]{:S(2)}, u32[]{:S(2)}) collective-permute-start(f32[24,128]{1,0:T(8,128)S(1)} %add_add_fusion.1), channel_id=1, source_target_pairs={{0,8},{1,9},{2,10},{3,11},{4,12},{5,13},{6,14},{7,15},{8,0},{9,1},... | collective-permute-start | bytes 36872 | tf_op jit(solution)/shard_map/ppermute | solution.py:474
  77.4 1.1 %collective-permute-done.12 = f32[24,128]{1,0:T(8,128)S(1)} collective-permute-done((f32[24,128]{1,0:T(8,128)S(1)}, f32[24,128]{1,0:T(8,128)S(1)}, u32[]{:S(2)}, u32[]{:S(2)}) %collective-permute-start.12) | collective-permute-done | bytes 12320 | tf_op jit(solution)/shard_map/ppermute | solution.py:474
  78.5 0.7 collective-permute-done.11
  79.2 4.7 %shard_map.121 = (f32[32,2048]{1,0:T(8,128)}, f32[3,32,128]{2,1,0:T(8,128)}) custom-call(f32[24,128]{1,0:T(8,128)S(1)} %add_add_fusion.gram_ref, f32[32,32]{1,0:T(8,128)S(1)} %get-tuple-element.39.factor0_ref, f32[4,32,32]{2,1,0:T(8,128)S(1)} %get-tuple-element.46.small_ref, f32[32,2560]{1,0:T(8,128)S(1)} %get-tuple-element.29.refs_0_.basis_ref.basis0_ref, ...), custom_call_target="tpu_custom_call" | custom-call | tf_op jit(solution)/shard_map/pallas_call | solution.py:437
  (43 shorter events, 3.1 us)
Async XLA Ops:
  0.6 1.0 %copy-start = (f32[32,2048]{1,0:T(8,128)S(1)}, f32[32,2048]{1,0:T(8,128)}, u32[]{:S(2)}) copy-start(f32[32,2048]{1,0:T(8,128)} %sens_ref.3) | copy-start | bytes 786436
  1.6 16.6 %copy-start.1 = (f32[32,2048]{1,0:T(8,128)S(1)}, f32[32,2048]{1,0:T(8,128)}, u32[]{:S(2)}) copy-start(f32[32,2048]{1,0:T(8,128)} %sens_ref.3) | copy-start | bytes 786436
  2.7 15.5 %copy-start.2 = (bf16[3,128,128]{2,1,0:T(8,128)(2,1)S(1)}, bf16[3,128,128]{2,1,0:T(8,128)(2,1)}, u32[]{:S(2)}) copy-start(bf16[3,128,128]{2,1,0:T(8,128)(2,1)} %param.19) | copy-start | bytes 294916
  2.7 15.5 %copy-start.3 = (s32[128,128]{1,0:T(8,128)S(1)}, s32[128,128]{1,0:T(8,128)}, u32[]{:S(2)}) copy-start(s32[128,128]{1,0:T(8,128)} %conn_ref.3) | copy-start | bytes 196612
  2.7 15.5 %all-to-all-start = ((f32[32,8,128]{2,1,0:T(8,128)}), f32[32,8,128]{2,1,0:T(8,128)S(1)}, u32[]{:S(2)}, u32[]{:S(2)}) async-start(f32[32,8,128]{2,1,0:T(8,128)} %get-tuple-element.26), calls=%async_computation | async-start | bytes 262144 | tf_op jit(solution)/shard_map/all_to_all | solution.py:459
  10.0 1.1 %copy-start.9 = (s32[1,2,256]{2,1,0:T(2,128)S(1)}, s32[1,2,256]{2,1,0:T(2,128)}, u32[]{:S(2)}) copy-start(s32[1,2,256]{2,1,0:T(2,128)} %param.18) | copy-start | bytes 6148
  10.0 1.9 %collective-permute-start = (f32[32,256]{1,0:T(8,128)S(1)}, f32[32,256]{1,0:T(8,128)S(1)}, u32[]{:S(2)}, u32[]{:S(2)}) collective-permute-start(f32[32,256]{1,0:T(8,128)S(1)} %get-tuple-element.27), channel_id=1, source_target_pairs={{0,1},{1,0},{2,3},{3,2},{4,5},{5,4},{6,7},{7,6},{8,9},{9,8},{10,11... | collective-permute-start | bytes 98312 | tf_op jit(solution)/shard_map/ppermute | solution.py:455
  10.3 0.8 copy-start.5
  10.3 0.8 %copy-start.6 = (f32[128]{0:T(128)S(1)}, f32[128]{0:T(128)}, u32[]{:S(2)}) copy-start(f32[128]{0:T(128)} %param.16) | copy-start | bytes 1540
  10.3 0.8 %copy-start.7 = (s32[128]{0:T(128)S(1)}, s32[128]{0:T(128)}, u32[]{:S(2)}) copy-start(s32[128]{0:T(128)} %param.17) | copy-start | bytes 1540
  10.3 1.6 %collective-permute-start.1 = (f32[32,256]{1,0:T(8,128)S(1)}, f32[32,256]{1,0:T(8,128)S(1)}, u32[]{:S(2)}, u32[]{:S(2)}) collective-permute-start(f32[32,256]{1,0:T(8,128)S(1)} %get-tuple-element.28), channel_id=1, source_target_pairs={{1,2},{2,1},{3,4},{4,3},{5,6},{6,5},{7,8},{8,7},{9,10},{10,9},{11,... | collective-permute-start | bytes 98312 | tf_op jit(solution)/shard_map/ppermute | solution.py:455
  11.2 0.7 copy-start.8
  11.9 6.3 %copy-start.4 = (f32[2048]{0:T(1024)S(1)}, f32[2048]{0:T(1024)}, u32[]{:S(2)}) copy-start(f32[2048]{0:T(1024)} %param.11) | copy-start | bytes 24580
  27.3 1.4 %collective-permute-start.2 = (f32[40,512]{1,0:T(8,128)S(1)}, f32[40,512]{1,0:T(8,128)S(1)}, u32[]{:S(2)}, u32[]{:S(2)}) collective-permute-start(f32[40,512]{1,0:T(8,128)S(1)} %get-tuple-element.31), channel_id=1, source_target_pairs={{0,1},{1,0},{2,3},{3,2},{4,5},{5,4},{6,7},{7,6},{8,9},{9,8},{10,11... | collective-permute-start | bytes 245768 | tf_op jit(solution)/shard_map/ppermute | solution.py:455
  27.6 1.1 %collective-permute-start.3 = (f32[40,512]{1,0:T(8,128)S(1)}, f32[40,512]{1,0:T(8,128)S(1)}, u32[]{:S(2)}, u32[]{:S(2)}) collective-permute-start(f32[40,512]{1,0:T(8,128)S(1)} %get-tuple-element.32), channel_id=1, source_target_pairs={{1,2},{2,1},{3,4},{4,3},{5,6},{6,5},{7,8},{8,7},{9,10},{10,9},{11,... | collective-permute-start | bytes 245768 | tf_op jit(solution)/shard_map/ppermute | solution.py:455
  58.6 3.1 %collective-permute-start.4 = (f32[32,512]{1,0:T(8,128)S(1)}, f32[32,512]{1,0:T(8,128)S(1)}, u32[]{:S(2)}, u32[]{:S(2)}) collective-permute-start(f32[32,512]{1,0:T(8,128)S(1)} %get-tuple-element.44), channel_id=1, source_target_pairs={{0,1},{1,0},{2,3},{3,2},{4,5},{5,4},{6,7},{7,6},{8,9},{9,8},{10,11... | collective-permute-start | bytes 196616 | tf_op jit(solution)/shard_map/ppermute | solution.py:455
  59.1 2.7 %collective-permute-start.5 = (f32[32,512]{1,0:T(8,128)S(1)}, f32[32,512]{1,0:T(8,128)S(1)}, u32[]{:S(2)}, u32[]{:S(2)}) collective-permute-start(f32[32,512]{1,0:T(8,128)S(1)} %get-tuple-element.45), channel_id=1, source_target_pairs={{1,2},{2,1},{3,4},{4,3},{5,6},{6,5},{7,8},{8,7},{9,10},{10,9},{11,... | collective-permute-start | bytes 196616 | tf_op jit(solution)/shard_map/ppermute | solution.py:455
  62.1 4.3 %collective-permute-start.6 = (f32[24,128]{1,0:T(8,128)S(1)}, f32[24,128]{1,0:T(8,128)S(1)}, u32[]{:S(2)}, u32[]{:S(2)}) collective-permute-start(f32[24,128]{1,0:T(8,128)S(1)} %shard_map.120), channel_id=1, source_target_pairs={{0,1},{1,0},{2,3},{3,2},{4,5},{5,4},{6,7},{7,6},{8,9},{9,8},{10,11... | collective-permute-start | bytes 36872 | tf_op jit(solution)/shard_map/ppermute | solution.py:474
  66.4 4.6 %collective-permute-start.9 = (f32[24,128]{1,0:T(8,128)S(1)}, f32[24,128]{1,0:T(8,128)S(1)}, u32[]{:S(2)}, u32[]{:S(2)}) collective-permute-start(f32[24,128]{1,0:T(8,128)S(1)} %add.21), channel_id=1, source_target_pairs={{0,6},{1,7},{2,4},{3,5},{4,2},{5,3},{6,0},{7,1},{8,14},{9,15},{10,... | collective-permute-start | bytes 36872 | tf_op jit(solution)/shard_map/ppermute | solution.py:474
  69.2 3.7 %collective-permute-start.8 = (f32[24,128]{1,0:T(8,128)S(1)}, f32[24,128]{1,0:T(8,128)S(1)}, u32[]{:S(2)}, u32[]{:S(2)}) collective-permute-start(f32[24,128]{1,0:T(8,128)S(1)} %add.21), channel_id=1, source_target_pairs={{0,4},{1,5},{2,6},{3,7},{4,0},{5,1},{6,2},{7,3},{8,12},{9,13},{10,... | collective-permute-start | bytes 36872 | tf_op jit(solution)/shard_map/ppermute | solution.py:474
  69.2 3.7 %collective-permute-start.7 = (f32[24,128]{1,0:T(8,128)S(1)}, f32[24,128]{1,0:T(8,128)S(1)}, u32[]{:S(2)}, u32[]{:S(2)}) collective-permute-start(f32[24,128]{1,0:T(8,128)S(1)} %add.21), channel_id=1, source_target_pairs={{0,2},{1,3},{2,0},{3,1},{4,6},{5,7},{6,4},{7,5},{8,10},{9,11},{10,... | collective-permute-start | bytes 36872 | tf_op jit(solution)/shard_map/ppermute | solution.py:474
  72.9 5.6 %collective-permute-start.12 = (f32[24,128]{1,0:T(8,128)S(1)}, f32[24,128]{1,0:T(8,128)S(1)}, u32[]{:S(2)}, u32[]{:S(2)}) collective-permute-start(f32[24,128]{1,0:T(8,128)S(1)} %add_add_fusion.1), channel_id=1, source_target_pairs={{0,24},{1,25},{2,26},{3,27},{4,28},{5,29},{6,30},{7,31},{8,16},{9,... | collective-permute-start | bytes 36872 | tf_op jit(solution)/shard_map/ppermute | solution.py:474
  74.5 4.7 %collective-permute-start.11 = (f32[24,128]{1,0:T(8,128)S(1)}, f32[24,128]{1,0:T(8,128)S(1)}, u32[]{:S(2)}, u32[]{:S(2)}) collective-permute-start(f32[24,128]{1,0:T(8,128)S(1)} %add_add_fusion.1), channel_id=1, source_target_pairs={{0,16},{1,17},{2,18},{3,19},{4,20},{5,21},{6,22},{7,23},{8,24},{9,... | collective-permute-start | bytes 36872 | tf_op jit(solution)/shard_map/ppermute | solution.py:474
  75.3 3.8 %collective-permute-start.10 = (f32[24,128]{1,0:T(8,128)S(1)}, f32[24,128]{1,0:T(8,128)S(1)}, u32[]{:S(2)}, u32[]{:S(2)}) collective-permute-start(f32[24,128]{1,0:T(8,128)S(1)} %add_add_fusion.1), channel_id=1, source_target_pairs={{0,8},{1,9},{2,10},{3,11},{4,12},{5,13},{6,14},{7,15},{8,0},{9,1},... | collective-permute-start | bytes 36872 | tf_op jit(solution)/shard_map/ppermute | solution.py:474
  (1 other events, 0.7 us)
